TPU v7x, 32 devices: a whole 2x2x4 slice. The times are simulated.
32 devices in a mesh: dp: 4 (over y, x), gx: 2 (over core), gy: 4 (over z).
Axes of the slice: x: 2, y: 2, z: 4, core: 2. Of those that a mesh axis runs over, the one named last changes fastest.
Arguments:
- magnetic: bfloat16 [4, 3, 8, 64, 512], P('dp', None, None, 'gx', 'gy'), may hold values from -6 to 6
- kernel_one: bfloat16 [3, 3, 3, 3, 32], replicated, may hold values from -0.625 to 0.625
- kernel_two: bfloat16 [3, 3, 3, 32, 64], replicated, may hold values from -0.21875 to 0.21875
- cotangent: bfloat16 [4, 2, 16, 8192], P('dp', None, 'gx', 'gy'), may hold values from -6 to 6
Outputs:
- features: bfloat16 [4, 2, 16, 8192], P('dp', None, 'gx', 'gy')
- level_grad: bfloat16 [4, 4, 32, 8192], P('dp', None, 'gx', 'gy')
- grad_one: float32 [3, 3, 3, 3, 32], P(None, None, None, None, 'dp')
- grad_two: float32 [3, 3, 3, 32, 64], P(None, None, None, None, 'dp')
All inputs are finite; a program needn't handle non-finite values.
Results may differ from a plain program's by a relative error of at most 0.012.
Values may be sent and summed in bfloat16 or wider, within the bound.
No kernel may reach another device: no remote copies, remote signals or barrier semaphores. Data moves between devices by JAX's collectives and lax.ppermute only.
A program may use at most 64 MiB of HBM per device.

v0:
```python
import math

import jax
import jax.numpy as jnp
from jax import lax
from jax.sharding import PartitionSpec as P


def shifted(value, axis, steps):
    count = lax.axis_size(axis)
    initial, last = (max(0, -steps), min(count, count - steps))
    return lax.ppermute(value, axis, [(source, source + steps) for source in range(initial, last)])


def extend(volume, toward, xdim):
    ydim = xdim + 1
    if toward == 1:
        plane_x = lax.slice_in_dim(volume, volume.shape[xdim] - 1, volume.shape[xdim], 1, xdim)
    else:
        plane_x = lax.slice_in_dim(volume, 0, 1, 1, xdim)
    got_x = shifted(plane_x, "gx", toward)
    if toward == 1:
        volume = jnp.concatenate([got_x, volume], axis=xdim)
        plane_y = lax.slice_in_dim(volume, volume.shape[ydim] - 1, volume.shape[ydim], 1, ydim)
    else:
        volume = jnp.concatenate([volume, got_x], axis=xdim)
        plane_y = lax.slice_in_dim(volume, 0, 1, 1, ydim)
    got_y = shifted(plane_y, "gy", toward)
    if toward == 1:
        return jnp.concatenate([got_y, volume], axis=ydim)
    return jnp.concatenate([volume, got_y], axis=ydim)


def conv_down(inputs_ext, kernel, layout):
    return lax.conv_general_dilated(
        inputs_ext,
        kernel,
        (2, 2, 2),
        ((1, 0), (0, 0), (0, 0)),
        dimension_numbers=(layout, "DHWIO", "NDHWC"),
        preferred_element_type=jnp.float32,
    )


def weight_grad(inputs_ext, delta, layout):
    result = lax.conv_general_dilated(
        inputs_ext,
        delta,
        (1, 1, 1),
        ((1, 0), (0, 0), (0, 0)),
        rhs_dilation=(2, 2, 2),
        dimension_numbers=(layout, "IDHWO", "NCDHW"),
        preferred_element_type=jnp.float32,
    )
    return jnp.transpose(result, (2, 3, 4, 0, 1))


def input_grad(delta_ext, kernel):
    flipped = jnp.flip(kernel, (0, 1, 2))
    return lax.conv_general_dilated(
        delta_ext,
        flipped,
        (1, 1, 1),
        ((1, 2), (1, 0), (1, 0)),
        lhs_dilation=(2, 2, 2),
        dimension_numbers=("NDHWC", "DHWOI", "NDHWC"),
        preferred_element_type=jnp.float32,
    )


def silu_slope(pre):
    sig = jax.nn.sigmoid(pre)
    return sig * (1.0 + pre * (1.0 - sig))


def body(magnetic, kernel_one, kernel_two, cotangent):
    chan_one = kernel_one.shape[4]
    chan_two = kernel_two.shape[4]
    source = extend(magnetic, 1, 3)
    pre_one = conv_down(source, kernel_one, "NCDHW")
    hidden = jax.nn.silu(pre_one).astype(jnp.bfloat16)
    hidden_ext = extend(hidden, 1, 2)
    pre_two = conv_down(hidden_ext, kernel_two, "NDHWC")
    shape_two = pre_two.shape
    features = (
        jax.nn.silu(pre_two)
        .astype(jnp.bfloat16)
        .reshape(shape_two[0], shape_two[1], shape_two[2], shape_two[3] * chan_two)
    )
    upstream = cotangent.reshape(shape_two)
    delta_two = (upstream.astype(jnp.float32) * silu_slope(pre_two)).astype(jnp.bfloat16)
    delta_ext = extend(delta_two, -1, 2)
    level_cells = input_grad(delta_ext, kernel_two).astype(jnp.bfloat16)
    delta_one = (level_cells.astype(jnp.float32) * silu_slope(pre_one)).astype(jnp.bfloat16)
    shape_one = level_cells.shape
    level_grad = level_cells.reshape(
        shape_one[0], shape_one[1], shape_one[2], shape_one[3] * chan_one
    )
    samples_all = magnetic.shape[0] * lax.axis_size("dp")
    cells_x = magnetic.shape[3] * lax.axis_size("gx")
    cells_y = magnetic.shape[4] * lax.axis_size("gy")
    depth = magnetic.shape[2]
    scale_one = 1.0 / math.sqrt(samples_all * (depth // 2) * (cells_x // 2) * (cells_y // 2))
    scale_two = 1.0 / math.sqrt(samples_all * (depth // 4) * (cells_x // 4) * (cells_y // 4))
    local_one = weight_grad(source, delta_one, "CNDHW") * scale_one
    local_two = weight_grad(hidden_ext, delta_two, "CDHWN") * scale_two
    total_one, total_two = lax.psum((local_one, local_two), ("dp", "gx", "gy"))
    width_one = total_one.shape[4] // lax.axis_size("dp")
    width_two = total_two.shape[4] // lax.axis_size("dp")
    member = lax.axis_index("dp")
    grad_one = lax.dynamic_slice_in_dim(total_one, member * width_one, width_one, 4)
    grad_two = lax.dynamic_slice_in_dim(total_two, member * width_two, width_two, 4)
    return (features, level_grad, grad_one, grad_two)


def solution(mesh):
    in_specs = (P("dp", None, None, "gx", "gy"), P(), P(), P("dp", None, "gx", "gy"))
    out_specs = (
        P("dp", None, "gx", "gy"),
        P("dp", None, "gx", "gy"),
        P(None, None, None, None, "dp"),
        P(None, None, None, None, "dp"),
    )
    return jax.shard_map(body, mesh=mesh, in_specs=in_specs, out_specs=out_specs, check_vma=False)
```

profile of v0, /device:TPU:0, one launch (start us, length us, event | category | flops | bytes accessed | tf_op | source)
XLA Modules:
  0.0 264.5 jit_solution(11920203626201727006)
XLA Ops:
  8.1 2.4 collective-permute-start
  10.5 1.3 copy.182
  12.4 4.3 %collective-permute-start.1 = (bf16[1,3,8,33,1]{3,2,4,1,0:T(8,128)(2,1)S(1)}, bf16[1,3,8,33,1]{3,2,4,1,0:T(8,128)(2,1)S(1)}, u32[]{:S(2)}, u32[]{:S(2)}) collective-permute-start(bf16[1,3,8,33,1]{3,2,4,1,0:T(8,128)(2,1)S(1)} %pad_maximum_fusion.10), channel_id=1, source_target_pairs={{0,1},{1,2},{2,3},{4,5},{5,6},{6,7},{8,9},{9,10},{10,11},{12,13},{... | collective-permute-start | bytes 4760 | tf_op jit(solution)/shard_map/ppermute | solution.py:12
  16.7 0.9 reshape.70
  18.9 0.9 copy-done.2
  20.2 7.0 %copy.184 = bf16[3,8,33,1,8,18]{4,0,5,2,1,3:T(4,128)(2,1)} copy(bf16[3,8,33,1,8,18]{2,1,5,4,0,3:T(8,128)(2,1)S(1)} %bitcast.81) | data formatting | bytes 456192 | tf_op jit(solution)/shard_map/conv_general_dilated | solution.py:35
  27.2 1.4 slice.39
  28.6 11.0 %add_multiply_fusion = (f32[4,16,8,9,32]{4,2,3,1,0:T(8,128)}, bf16[4,16,8,9,32]{4,2,3,1,0:T(8,128)(2,1)S(1)}) fusion(pred[8,9]{0,1:T(8,128)(4,1)S(1)} %copy-done.9, bf16[3,3,3,3,32]{4,3,2,1,0:T(4,128)(2,1)} %param.5, bf16[3,8,33,1,7,2]{4,0,5,2,1,3:T(4,128)(2,1)S(1)} %slice.39, bf16[3,8,33,1,8,18]{4,0,5,2,1,3:T(4,128)(2,1)} %copy.184), kind=kOutput, calls=%fused_computation.19 | convolution fusion | flops 24132096 | bytes 1140264 | tf_op jit(solution)/shard_map/conv_general_dilated | solution.py:35
  40.5 1.9 collective-permute-start.2
  42.4 7.5 %copy.217 = bf16[3,8,33,1,8,19]{4,0,5,2,1,3:T(4,128)(2,1)} copy(bf16[3,8,33,1,8,19]{2,1,5,4,0,3:T(8,128)(2,1)S(1)} %slice.51) | data formatting | bytes 481536
  49.9 10.1 %fusion.64 = bf16[3,8,33,8,20,1]{3,0,5,4,2,1:T(4,128)(2,1)} fusion(bf16[3,8,33,1,7,1]{4,0,5,2,1,3:T(4,128)(2,1)S(1)} %copy.218, bf16[3,8,33,1,8,19]{4,0,5,2,1,3:T(4,128)(2,1)} %copy.217), kind=kLoop, calls=%fused_computation.75 | loop fusion | flops 760320 | bytes 505296 | tf_op jit(solution)/shard_map/concatenate | solution.py:30
  60.0 8.3 %fusion.6 = bf16[3,8,33,1,8,20]{4,0,5,2,1,3:T(4,128)(2,1)} fusion(bf16[3,8,33,1,7,1]{4,0,5,2,1,3:T(4,128)(2,1)S(1)} %copy.218, bf16[3,8,33,1,8,19]{4,0,5,2,1,3:T(4,128)(2,1)S(1)} %copy-done.1), kind=kLoop, calls=%fused_computation.9 | loop fusion | flops 760320 | bytes 505296 | tf_op jit(solution)/shard_map/concatenate | solution.py:30
  69.9 1.0 fusion.36
  71.4 4.4 %collective-permute-start.3 = (bf16[1,4,17,1,32]{4,1,3,2,0:T(4,128)(2,1)S(1)}, bf16[1,4,17,1,32]{4,1,3,2,0:T(4,128)(2,1)S(1)}, u32[]{:S(2)}, u32[]{:S(2)}) collective-permute-start(bf16[1,4,17,1,32]{4,1,3,2,0:T(4,128)(2,1)S(1)} %copy.215), channel_id=1, source_target_pairs={{0,1},{1,2},{2,3},{4,5},{5,6},{6,7},{8,9},{9,10},{10,11},{12,13},{... | collective-permute-start | bytes 13064 | tf_op jit(solution)/shard_map/ppermute | solution.py:12
  76.7 4.5 %copy.191 = bf16[1,4,17,64,32]{4,0,3,2,1:T(2,128)(2,1)} copy(bf16[1,4,17,64,32]{3,4,2,1,0:T(8,128)(2,1)S(1)} %pad_maximum_fusion.7) | data formatting | bytes 557056 | tf_op jit(solution)/shard_map/concatenate | solution.py:23
  81.2 5.1 %pad_maximum_fusion.2 = bf16[1,4,17,65,32]{4,0,3,2,1:T(2,128)(2,1)S(1)} fusion(bf16[1,4,17,64,32]{4,0,3,2,1:T(2,128)(2,1)} %copy.191, bf16[1,4,17,1,32]{4,0,3,2,1:T(2,128)(2,1)S(1)} %copy.190), kind=kLoop, calls=%fused_computation.22 | loop fusion | flops 141440 | bytes 565760 | tf_op jit(solution)/shard_map/concatenate | solution.py:30
  86.4 2.7 %copy.192 = bf16[1,4,17,65,32]{3,4,2,1,0:T(8,128)(2,1)S(1)} copy(bf16[1,4,17,65,32]{4,0,3,2,1:T(2,128)(2,1)S(1)} %pad_maximum_fusion.2) | data formatting | bytes 565760 | tf_op jit(solution)/shard_map/concatenate | solution.py:30
  89.1 1.7 copy.220
  90.7 2.0 pad.2.clone
  93.1 1.2 add_multiply_fusion.1
  94.5 1.6 collective-permute-start.4
  96.1 8.4 %fusion.8 = bf16[3,8,33,8,20,1]{3,0,5,4,2,1:T(4,128)(2,1)} fusion(bf16[3,8,33,1,7,1]{4,0,5,2,1,3:T(4,128)(2,1)S(1)} %copy.219, bf16[3,8,33,1,8,19]{4,0,5,2,1,3:T(4,128)(2,1)S(1)} %slice-done), kind=kLoop, calls=%fused_computation.11 | loop fusion | flops 760320 | bytes 505296 | tf_op jit(solution)/shard_map/concatenate | solution.py:30
  104.9 9.5 %copy.208 = bf16[3,8,33,8,20,1]{3,0,5,4,2,1:T(4,128)(2,1)} copy(bf16[3,8,33,8,20,1]{2,1,4,3,0,5:T(8,128)(2,1)} %bitcast.75) | data formatting | bytes 506880 | tf_op jit(solution)/shard_map/concatenate | solution.py:30
  114.4 1.8 pad.6
  116.1 1.6 collective-permute-start.5
  117.7 6.5 %convolution_multiply_fusion = f32[3,3,3,32,64]{3,4,2,1,0:T(8,128)} fusion(bf16[1,4,17,65,32]{4,0,3,2,1:T(2,128)(2,1)S(1)} %copy-done.4, bf16[1,2,8,32,64]{4,3,2,1,0:T(8,128)(2,1)S(1)} %fusion.39), kind=kOutput, calls=%fused_computation.32 | convolution fusion | flops 47241216 | bytes 569600 | tf_op jit(solution)/shard_map/transpose | solution.py:55
  125.6 1.3 select_convert_fusion
  127.7 1.9 reshape.30
  129.6 21.0 %fusion.31 = f32[3,3,3,3,32]{4,3,2,1,0:T(4,128)S(1)} fusion(f32[4,16,8,10,32]{4,1,3,2,0:T(8,128)} %bitcast.82, bf16[4,16,8,10,32]{4,2,3,1,0:T(8,128)(2,1)S(1)} %select_convert_fusion, pred[8,10]{0,1:T(8,128)(4,1)S(1)} %copy-done.8, bf16[3,8,33,8,20,1]{3,0,5,4,2,1:T(4,128)(2,1)} %fusion.8, bf16[3,8,33,8,20,1]{3,0,5,4,2,1:T(4,128)(2,1)} %fusion.64, ...), kind=kOutput, calls=%fused_computation.35 | convolution fusion | flops 27269152 | bytes 1753808 | tf_op jit(solution)/shard_map/transpose | solution.py:55
  150.6 42.2 %psum.14 = f32[3,3,3,3,32]{4,3,2,1,0:T(4,128)S(1)} all-reduce(f32[3,3,3,3,32]{4,3,2,1,0:T(4,128)S(1)} %fusion.31), channel_id=1, replica_groups=mesh['dp'=4,'gx'=2,'gy'=4] {'dp','gx','gy'}, use_global_device_ids=true, to_apply=%region_0.1 | all-reduce | flops 2592 | bytes 20736 | tf_op jit(solution)/shard_map/psum | solution.py:107
  193.5 62.5 %all-reduce.2.cloned.1.call-done = f32[3,3,3,32,64]{3,4,2,1,0:T(8,128)} async-done(((f32[3,3,3,32,64]{3,4,2,1,0:T(8,128)}), f32[3,3,3,32,64]{3,4,2,1,0:T(8,128)}) %all-reduce.2.cloned.1.call-update) | async-done | bytes 221200 | tf_op jit(solution)/shard_map/psum | solution.py:107
  256.0 1.6 constant_dynamic-slice_fusion
  (73 shorter events, 10.5 us)
Async XLA Ops:
  7.2 85.9 %copy-start = (bf16[3,3,3,32,64]{4,3,2,1,0:T(8,128)(2,1)S(1)}, bf16[3,3,3,32,64]{4,3,2,1,0:T(8,128)(2,1)}, u32[]{:S(2)}) copy-start(bf16[3,3,3,32,64]{4,3,2,1,0:T(8,128)(2,1)} %param.6) | copy-start | bytes 331780
  7.2 9.5 %copy-start.7 = (bf16[1,2,8,2048]{3,2,1,0:T(8,128)(2,1)S(1)}, bf16[1,2,8,2048]{3,2,1,0:T(8,128)(2,1)}, u32[]{:S(2)}) copy-start(bf16[1,2,8,2048]{3,2,1,0:T(8,128)(2,1)} %param.7) | copy-start | bytes 196612
  7.2 248.8 %all-reduce.2.cloned.1.call-start = ((), (), s32[]{:S(2)}) async-start(), calls=%async_computation | async-start | bytes 1769472 | tf_op jit(solution)/shard_map/psum | solution.py:107
  8.1 3.7 %collective-permute-start = (bf16[1,3,8,1,128]{4,2,3,1,0:T(8,128)(2,1)S(1)}, bf16[1,3,8,1,128]{4,2,3,1,0:T(8,128)(2,1)S(1)}, u32[]{:S(2)}, u32[]{:S(2)}) collective-permute-start(bf16[1,3,8,1,128]{4,2,3,1,0:T(8,128)(2,1)S(1)} %copy.214), channel_id=1, source_target_pairs={{0,4},{1,5},{2,6},{3,7},{8,12},{9,13},{10,14},{11,15},{16,20},{17,... | collective-permute-start | bytes 18440 | tf_op jit(solution)/shard_map/ppermute | solution.py:12
  12.4 5.6 %collective-permute-start.1 = (bf16[1,3,8,33,1]{3,2,4,1,0:T(8,128)(2,1)S(1)}, bf16[1,3,8,33,1]{3,2,4,1,0:T(8,128)(2,1)S(1)}, u32[]{:S(2)}, u32[]{:S(2)}) collective-permute-start(bf16[1,3,8,33,1]{3,2,4,1,0:T(8,128)(2,1)S(1)} %pad_maximum_fusion.10), channel_id=1, source_target_pairs={{0,1},{1,2},{2,3},{4,5},{5,6},{6,7},{8,9},{9,10},{10,11},{12,13},{... | collective-permute-start | bytes 4760 | tf_op jit(solution)/shard_map/ppermute | solution.py:12
  18.8 1.0 copy-start.2
  20.2 8.5 %copy-start.9 = (pred[8,9]{0,1:T(8,128)(4,1)S(1)}, pred[8,9]{0,1:T(8,128)(4,1)}, u32[]{:S(2)}) copy-start(pred[8,9]{0,1:T(8,128)(4,1)} %constant.47) | copy-start | bytes 220
  40.5 29.4 %collective-permute-start.2 = (bf16[1,4,1,64,32]{3,4,2,1,0:T(8,128)(2,1)}, bf16[1,4,1,64,32]{3,4,2,1,0:T(8,128)(2,1)}, u32[]{:S(2)}, u32[]{:S(2)}) collective-permute-start(bf16[1,4,1,64,32]{3,4,2,1,0:T(8,128)(2,1)} %bitcast.4), channel_id=1, source_target_pairs={{0,4},{1,5},{2,6},{3,7},{8,12},{9,13},{10,14},{11,15},{16,20},{17,... | collective-permute-start | bytes 49160 | tf_op jit(solution)/shard_map/ppermute | solution.py:12
  49.9 10.1 %copy-start.1 = (bf16[3,8,33,1,8,19]{4,0,5,2,1,3:T(4,128)(2,1)S(1)}, bf16[3,8,33,1,8,19]{4,0,5,2,1,3:T(4,128)(2,1)}, u32[]{:S(2)}) copy-start(bf16[3,8,33,1,8,19]{4,0,5,2,1,3:T(4,128)(2,1)} %copy.217) | copy-start | bytes 722308
  71.4 9.8 %collective-permute-start.3 = (bf16[1,4,17,1,32]{4,1,3,2,0:T(4,128)(2,1)S(1)}, bf16[1,4,17,1,32]{4,1,3,2,0:T(4,128)(2,1)S(1)}, u32[]{:S(2)}, u32[]{:S(2)}) collective-permute-start(bf16[1,4,17,1,32]{4,1,3,2,0:T(4,128)(2,1)S(1)} %copy.215), channel_id=1, source_target_pairs={{0,1},{1,2},{2,3},{4,5},{5,6},{6,7},{8,9},{9,10},{10,11},{12,13},{... | collective-permute-start | bytes 13064 | tf_op jit(solution)/shard_map/ppermute | solution.py:12
  86.4 6.4 %copy-start.3 = (bf16[1,4,17,65,32]{4,0,3,2,1:T(2,128)(2,1)}, bf16[1,4,17,65,32]{4,0,3,2,1:T(2,128)(2,1)S(1)}, u32[]{:S(2)}) copy-start(bf16[1,4,17,65,32]{4,0,3,2,1:T(2,128)(2,1)S(1)} %pad_maximum_fusion.2) | copy-start | bytes 848644
  90.7 2.3 copy-start.10
  93.0 1.4 copy-start.6
  93.1 3.0 %slice-start = ((bf16[3,8,33,1,8,20]{4,0,5,2,1,3:T(4,128)(2,1)}), bf16[3,8,33,1,8,19]{4,0,5,2,1,3:T(4,128)(2,1)S(1)}, s32[]{:S(2)}) async-start(bf16[3,8,33,1,8,20]{4,0,5,2,1,3:T(4,128)(2,1)} %fusion.6), calls=%async_computation.1 | async-start | bytes 10272768 | tf_op jit(solution)/shard_map/concatenate | solution.py:30
  94.5 9.9 %copy-start.5 = (f32[4,16,8,9,32]{4,2,3,1,0:T(8,128)S(1)}, f32[4,16,8,9,32]{4,2,3,1,0:T(8,128)}, u32[]{:S(2)}) copy-start(f32[4,16,8,9,32]{4,2,3,1,0:T(8,128)} %get-tuple-element.4) | copy-start | bytes 1769476
  94.5 21.6 %collective-permute-start.4 = (bf16[1,2,1,32,64]{4,3,2,1,0:T(8,128)(2,1)S(1)}, bf16[1,2,1,32,64]{4,3,2,1,0:T(8,128)(2,1)S(1)}, u32[]{:S(2)}, u32[]{:S(2)}) collective-permute-start(bf16[1,2,1,32,64]{4,3,2,1,0:T(8,128)(2,1)S(1)} %slice.48), channel_id=1, source_target_pairs={{4,0},{5,1},{6,2},{7,3},{12,8},{13,9},{14,10},{15,11},{20,16},{21,... | collective-permute-start | bytes 24584 | tf_op jit(solution)/shard_map/ppermute | solution.py:12
  114.4 3.3 %copy-start.4 = (bf16[1,4,17,65,32]{4,0,3,2,1:T(2,128)(2,1)S(1)}, bf16[1,4,17,65,32]{4,0,3,2,1:T(2,128)(2,1)}, u32[]{:S(2)}) copy-start(bf16[1,4,17,65,32]{4,0,3,2,1:T(2,128)(2,1)} %copy-done.3) | copy-start | bytes 848644
  116.1 9.0 %collective-permute-start.5 = (bf16[1,2,9,1,64]{4,3,2,1,0:T(2,128)(2,1)S(1)}, bf16[1,2,9,1,64]{4,3,2,1,0:T(2,128)(2,1)S(1)}, u32[]{:S(2)}, u32[]{:S(2)}) collective-permute-start(bf16[1,2,9,1,64]{4,3,2,1,0:T(2,128)(2,1)S(1)} %pad_maximum_fusion.9), channel_id=1, source_target_pairs={{1,0},{2,1},{3,2},{5,4},{6,5},{7,6},{9,8},{10,9},{11,10},{13,12},{... | collective-permute-start | bytes 6920 | tf_op jit(solution)/shard_map/ppermute | solution.py:12
  124.2 1.3 copy-start.8
Sparse Core Ops, SparseCore 0:
  124.4 131.6 all-reduce.1
where the time goes:
time: 266 us; the launch traced here: 265 us
  waiting for transfers between devices  63 us (24%)
  local copies, waits for them, and re-layouts  53.2 us (20%)
  blocking collectives  42.2 us (16%)
  matrix products  41.1 us (15%)
  other arithmetic  34.5 us (13%)
  starting transfers between devices  16.1 us (6%)
  between operations  14.5 us (5%)
    psum x1, waiting for transfers between devices, body(): total_one, total_two = lax.psum((local_one, local_two), ('dp', 'gx', 'gy'))  62.5 us
    psum x1, blocking collectives, body(): total_one, total_two = lax.psum((local_one, local_two), ('dp', 'gx', 'gy'))  42.2 us
    concatenate x5, other arithmetic, extend(): return jnp.concatenate([got_y, volume], axis=ydim)  32.4 us
    transpose x2, matrix products, weight_grad(): return jnp.transpose(result, (2, 3, 4, 0, 1))  27.5 us
    ppermute x6, starting transfers between devices, shifted(): lax.ppermute(value, axis, [(source, source + steps) for source in range(i...  16.1 us
    concatenate x9, local copies, waits for them, and re-layouts, extend(): return jnp.concatenate([got_y, volume], axis=ydim)  14.6 us
    unnamed x29, local copies, waits for them, and re-layouts  12.6 us
    conv_general_dilated x2, matrix products, conv_down(): lax.conv_general_dilated(inputs_ext, kernel, (2, 2, 2), ((1, 0), (0, 0),...  12.3 us
  transfers between devices with their start and end apart: 7, of which 2 were waited for; matrix products, arithmetic and copies ran while one was open for 33% of the time, Pallas kernels for 0%

commit v1 on v0

v1 whole, which is shorter than its diff:
```python
import math

import jax
import jax.numpy as jnp
from jax import lax
from jax.experimental import pallas as pl
from jax.experimental.pallas import tpu as pltpu
from jax.sharding import PartitionSpec as P

BF = jnp.bfloat16
F32 = jnp.float32
VMEM_LIMIT = 32 * 1024 * 1024


def iota(shape, dim):
    return lax.broadcasted_iota(jnp.int32, shape, dim)


def dot(lhs, rhs, contract=((1,), (0,))):
    return lax.dot_general(lhs, rhs, (contract, ((), ())), preferred_element_type=F32)


def swaps(axis):
    count, ranks = lax.axis_size(axis), lax.axis_size("dp")
    found = []
    for first in range(min(2, count - 1)):
        pairs = []
        for d in range(ranks):
            for i in range(count):
                other = i + 1 if i % 2 == first else i - 1
                if 0 <= other < count:
                    pairs.append((d * count + i, d * count + other))
                else:
                    pairs.append((d * count + i, (d ^ 1) % ranks * count + i))
        found.append(pairs)
    return found


def position(axis):
    index = lax.axis_index(axis)
    return lax.rem(index, 2) == 1, index == 0, index == lax.axis_size(axis) - 1


def from_low(place, got):
    odd, first, _ = place
    second = got[1] if len(got) > 1 else got[0]
    return jnp.where(first, 0.0, jnp.where(odd, got[0], second))


def from_high(place, got):
    odd, _, last = place
    second = got[1] if len(got) > 1 else got[0]
    return jnp.where(last, 0.0, jnp.where(odd, second, got[0]))


def edge_x_kernel(count, *refs):
    hbm, refs = refs[:4], refs[4:]
    held, outs, (stage, sems) = refs[:4], refs[4 : 4 + count], refs[4 + count :]
    fetches = [pltpu.make_async_copy(hbm[i], held[i], sems.at[i]) for i in range(4)]
    for fetch in fetches:
        fetch.start()
    mag_ref, cot_ref = held[:2]
    odd = position("gx")[0]
    planes = mag_ref.shape[0]
    blocks = cot_ref.shape[2] // 128
    for fetch in fetches:
        fetch.wait()
    field = mag_ref[...].astype(F32)
    low = field[:, 0:4, :]
    high = field[:, field.shape[1] - 4 :, :]
    cot = [cot_ref[k].astype(F32)[0:1, :] for k in range(2)]
    for turn in range(count):
        toward_high = odd if turn == 1 else jnp.logical_not(odd)
        picked = jnp.where(toward_high, high, low)
        for g in range(planes):
            stage[4 * g : 4 * g + 4, :] = picked[g]
        for k in range(2):
            for m in range(blocks):
                row = 4 * planes + 16 * k + m
                stage[row : row + 1, :] = cot[k][:, 128 * m : 128 * m + 128]
        outs[turn][...] = stage[...].astype(BF)


def edge_y_kernel(count_x, count_y, mag_ref, cot_ref, *refs):
    got_refs, refs = refs[:count_x], refs[count_x:]
    split_ref, outs = refs[0], refs[1 : 1 + count_y]
    tall, = refs[1 + count_y :]
    place_x, place_y = position("gx"), position("gy")
    planes = mag_ref.shape[0]
    got = [ref[...].astype(F32) for ref in got_refs]
    low = from_low(place_x, got)
    high = from_high(place_x, got)
    zeros = jnp.zeros((24, 128), F32)
    for g in range(planes):
        edge = low[4 * g : 4 * g + 4, :]
        tall[g, 0:8, :] = jnp.broadcast_to(edge[3:4, :], (8, 128))
        tall[g, 8:40, :] = mag_ref[g].astype(F32)
        tall[g, 40:44, :] = high[4 * g : 4 * g + 4, :]
        tall[g, 44:68, :] = zeros
        tall[g, 68:72, :] = edge
    starts = (8, 9, 10, 11, 7)
    split = []
    for slot in range(5):
        parts = [tall[g, pl.ds(starts[slot], 16, stride=4), :].astype(BF) for g in range(planes)]
        whole = jnp.concatenate(parts, axis=0)
        split_ref[slot] = whole
        split.append(whole)
    rows = planes // 3 * 16
    lhs = jnp.concatenate(
        [split[s][rows * c : rows * c + rows] for s in range(4) for c in range(3)], axis=1
    )
    lane = iota((128, 128), 1)
    cell = iota((128, 128), 0)
    slot = lane & 3
    wanted = jnp.where(lane < 64, 124 + slot, slot)
    group = (lane & 63) >> 2
    picks = []
    for s in range(4):
        for c in range(3):
            hit = (group == 4 * s + c) & (cell == wanted)
            picks.append(jnp.where(hit, 1.0, 0.0).astype(BF))
    both = dot(lhs, jnp.concatenate(picks, axis=0)).reshape(4, 2, 16, 128)
    lower, upper = both[:, 0].reshape(64, 128), both[:, 1].reshape(64, 128)
    left = iota((64, 128), 1) < 64
    toward = [
        jnp.where(left, lower, pltpu.roll(upper, 64, 1)),
        jnp.where(left, pltpu.roll(lower, 64, 1), upper),
    ]
    cot_rows = []
    for k in range(2):
        own = cot_ref[k].astype(F32)[:, 0:128]
        row = 4 * planes + 16 * k
        cot_rows.append(jnp.concatenate([own, high[row : row + 1, :], jnp.zeros((7, 128), F32)], axis=0))
    cot_rows = jnp.where(iota((16, 128), 1) < 64, cot_rows[0], pltpu.roll(cot_rows[1], 64, 1))
    odd = place_y[0]
    for turn in range(count_y):
        toward_high = odd if turn == 1 else jnp.logical_not(odd)
        outs[turn][0:64, :] = jnp.where(toward_high, toward[0], toward[1]).astype(BF)
        outs[turn][64:80, :] = cot_rows.astype(BF)


def weights_kernel(one_ref, two_ref, w_one, w_two, halo_ref, rows_one):
    lane = iota((32, 256), 1)
    spread = jnp.where(iota((32, 256), 0) == (lane & 31), 1.0, 0.0).astype(BF)
    rows_one[80:88, :] = jnp.zeros((8, 32), F32)
    for i in range(27):
        rows_one[3 * i : 3 * i + 3, :] = one_ref[i].astype(F32)
    wide = dot(rows_one[...].astype(BF), spread)
    window = iota((32, 256), 0) - 2 * (lane >> 5)
    for tap in range(9):
        for c in range(3):
            block = jnp.zeros((32, 256), F32)
            for e in range(3):
                row = (3 * tap + e) * 3 + c
                block = jnp.where(window == e, wide[row : row + 1, :], block)
            w_one[128 * tap + 32 * c : 128 * tap + 32 * c + 32, :] = block.astype(BF)
        w_one[128 * tap + 96 : 128 * tap + 128, :] = jnp.zeros((32, 256), BF)

    lane = iota((64, 128), 1)
    spread = jnp.where(iota((64, 128), 0) == (lane & 63), 1.0, 0.0).astype(BF)
    twice = dot(two_ref[...], spread)
    left = iota((32, 128), 1) < 64
    for tap in range(9):
        k0, k1, k2 = (twice[32 * (3 * tap + e) : 32 * (3 * tap + e) + 32] for e in range(3))
        base = 128 * tap
        w_two[base : base + 32, 0:128] = jnp.where(left, k1, 0.0).astype(BF)
        w_two[base + 32 : base + 64, 0:128] = jnp.where(left, k2, k0).astype(BF)
        w_two[base + 64 : base + 96, 0:128] = jnp.where(left, 0.0, k1).astype(BF)
        w_two[base + 96 : base + 128, 0:128] = jnp.where(left, 0.0, k2).astype(BF)
        w_two[base : base + 96, 128:256] = jnp.zeros((96, 128), BF)
        w_two[base + 96 : base + 128, 128:256] = jnp.where(left, k0, 0.0).astype(BF)

    lane = iota((256, 256), 1)
    code = iota((256, 256), 0)
    offset = lane & 31
    part = (lane & 127) >> 5
    wanted = jnp.where(
        lane < 128,
        jnp.where(offset == 0, 3, -999),
        jnp.where(
            (offset >= 1) & (offset <= 4), 127 + offset, jnp.where((offset >= 14) & (offset <= 16), offset - 13, -999)
        ),
    )
    wanted = jnp.where(part < 3, wanted + 4 * part, -999)
    for s in range(4):
        for parity in range(2):
            hit = code - (64 * parity + 16 * s) == wanted
            base = 256 * (2 * s + parity)
            halo_ref[:, base : base + 256] = jnp.where(hit, 1.0, 0.0).astype(BF)


SLOTS = ((4, 0, 1), (1, 2, 3))


def first_level(pre, t):
    sig = jax.nn.sigmoid(pre)
    hidden = pre * sig
    slope = sig * (1.0 + pre * (1.0 - sig))
    if t == 0:
        return [(1, hidden)], slope
    rows, width = hidden.shape
    later = hidden.reshape(rows // 16, 16, width)
    later = jnp.concatenate([later[:, 15:16], later[:, 0:15]], axis=1).reshape(rows, width)
    return [(2, hidden), (0, later)], slope


def second_level(pre, cot):
    sig = jax.nn.sigmoid(pre)
    return pre * sig, cot * (sig * (1.0 + pre * (1.0 - sig)))


def short_pair(value, row):
    return jnp.concatenate([value[row : row + 8, 0:128], value[row : row + 8, 128:256]], axis=0)


def windows_kernel(count_x, split_ref, w_one, w_two, cot_ref, *refs):
    gx_refs, refs = refs[:count_x], refs[count_x:]
    short_ref, outer_ref, short_act, slope_ref, cot_all = refs[:5]
    ends_ref, feat_ref, here_ref, after_ref, grad_ref, inner_ref, act_ref = refs[5:]
    high_x = from_high(position("gx"), [ref[96:128, :].astype(F32) for ref in gx_refs])
    for k in range(2):
        cot = cot_ref[k].astype(F32)
        for m in range(16):
            row = 16 * k + m
            cot_all[k, 16 * m : 16 * m + 8, :] = cot[:, 128 * m : 128 * m + 128]
            cot_all[k, 16 * m + 8 : 16 * m + 16, :] = jnp.where(
                iota((8, 128), 0) == 0, high_x[row : row + 1, :], 0.0
            )

    lane = iota((128, 1152), 1)
    cell = iota((128, 1152), 0)
    block = lane >> 7
    offset = lane & 31
    part = (lane & 127) >> 5
    wanted = jnp.where(offset <= 16, 16 * block - 1 + offset, -9)
    wanted = jnp.where(block == 8, jnp.where(offset == 0, 127, -9), wanted)
    hit = cell == wanted
    picks = jnp.concatenate(
        [jnp.where(hit & (part == c), 1.0, 0.0).astype(BF) for c in range(3)], axis=0
    )
    for s in range(5):
        lhs = jnp.concatenate([split_ref[s, 128 * c : 128 * c + 128, :] for c in range(3)], axis=1)
        exact = dot(lhs, picks)
        found = exact.astype(BF)
        for z in range(8):
            for q in range(4):
                first = exact[16 * z : 16 * z + 8, 256 * q + 128 : 256 * q + 256]
                if q < 3:
                    second = exact[16 * z : 16 * z + 8, 256 * q + 256 : 256 * q + 384]
                else:
                    second = jnp.zeros((8, 128), F32)
                short_ref[s, z, 16 * q : 16 * q + 16, :] = jnp.concatenate([first, second], axis=0).astype(BF)
        for n in range(1, 8):
            for z in range(8):
                inner_ref[s, z, 16 * n - 16 : 16 * n, :] = found[16 * z : 16 * z + 16, 128 * n : 128 * n + 128]
        outer_ref[s, :, 0:128] = found[:, 0:128]
        outer_ref[s, :, 128:256] = found[:, 1024:1152]
    weights = w_one[...]
    for p in range(4):
        for t in range(2):
            pieces = []
            for a in range(3):
                for b in range(3):
                    z = 2 * p + a - 1
                    pieces.append(inner_ref[SLOTS[t][b], z] if z >= 0 else jnp.zeros((112, 128), BF))
            versions, slope = first_level(dot(jnp.concatenate(pieces, axis=1), weights), t)
            for b, value in versions:
                for n in range(7):
                    short_act[b, p, 16 * n : 16 * n + 16, :] = short_pair(value, 16 * n).astype(BF)
                value = value.astype(BF)
                for n in range(7):
                    act_ref[b, p, 32 * n : 32 * n + 16, :] = value[16 * n : 16 * n + 16, 0:128]
                    act_ref[b, p, 32 * n + 16 : 32 * n + 32, :] = value[16 * n : 16 * n + 16, 128:256]
            for n in range(7):
                slope_ref[p, t, 16 * n : 16 * n + 16, :] = short_pair(slope, 16 * n)
    weights = w_two[...]
    delta, patches = [], []
    for k in range(2):
        planes = [(b, 2 * k + a - 1) for a in range(3) for b in range(3)]
        lhs = [act_ref[b, p] if p >= 0 else jnp.zeros((224, 128), BF) for b, p in planes]
        out = dot(jnp.concatenate(lhs, axis=1), weights)
        ends_ref[k, 0] = out[0:16, 0:128]
        ends_ref[k, 1] = out[208:224, 128:256]
        feat, value = second_level(out[16:224, 0:128] + out[0:208, 128:256], cot_all[k, 48:256, :])
        feat_ref[k] = jnp.concatenate([feat[16 * m : 16 * m + 8] for m in range(13)], axis=1).astype(BF)
        value = value.reshape(13, 16, 128)
        here = value[:, 0:8].reshape(104, 128)
        here_ref[k] = here
        after_ref[k] = value[:, 1:9].reshape(104, 128)
        zero = jnp.zeros((8, 128), F32)
        both = [jnp.concatenate([zero, here], axis=0), jnp.concatenate([here, zero], axis=0)]
        delta.append(jnp.concatenate(both, axis=1).astype(BF))
        short = [short_act[b, p] if p >= 0 else jnp.zeros((112, 128), BF) for b, p in planes]
        patches.append(jnp.concatenate(short, axis=1))
    grad_ref[...] = dot(jnp.concatenate(delta, axis=0), jnp.concatenate(patches, axis=0), ((0,), (0,)))[0:192]


def main_kernel(
    count_y,
    ranks,
    short_ref,
    outer_ref,
    short_act,
    slope_ref,
    cot_ref,
    ends_ref,
    feat_in,
    here_in,
    after_in,
    grad_in,
    halo_ref,
    w_one,
    w_two,
    *refs,
):
    gy_refs, refs = refs[:count_y], refs[count_y:]
    feat_hbm, level_hbm, refs = refs[0], refs[1], refs[2:]
    dealt, refs = refs[:ranks], refs[ranks:]
    edges, short_edges, outer_act, outer_short, outer_slope, rows_out, total, feat_ref, level_ref, sems = refs
    place_y = position("gy")
    copies = []

    got_y = [ref[...].astype(F32) for ref in gy_refs]
    low_y = from_low(place_y, got_y)
    high_y = from_high(place_y, got_y)
    halo = jnp.concatenate([low_y[0:64], high_y[0:64]], axis=1).astype(BF)
    first_half = iota((16, 128), 1) < 64
    cot_y = [jnp.where(first_half, value, 0.0) for value in (high_y[64:80], pltpu.roll(high_y[64:80], 64, 1))]
    brought = dot(halo, halo_ref[...])
    for s in range(5):
        base = 512 * min(s, 3)
        found = [brought[:, base + 256 * parity : base + 256 * parity + 256].reshape(4, 16, 256) for parity in range(2)]
        edge = jnp.stack(found, axis=1).reshape(8, 16, 256)
        if s == 4:
            edge = jnp.concatenate([edge[:, 15:16], edge[:, 0:15]], axis=1)
        exact = outer_ref[s].astype(F32) + edge.reshape(128, 256)
        value = exact.astype(BF)
        for z in range(8):
            edges[s, z, 0:16, :] = value[16 * z : 16 * z + 16, 0:128]
            edges[s, z, 16:32, :] = value[16 * z : 16 * z + 16, 128:256]
            other = short_ref[s, z, 48:64, :].astype(F32)
            short_edges[s, z] = jnp.concatenate([other[0:8], exact[16 * z : 16 * z + 8, 0:128]], axis=0).astype(BF)

    def window(s, z):
        if z < 0:
            return jnp.zeros((64, 128), BF)
        return jnp.concatenate([short_ref[s, z, 0:48, :], short_edges[s, z]], axis=0)

    weights = w_one[...]
    for t in range(2):
        rows = []
        for p in range(4):
            pieces = []
            for a in range(3):
                for b in range(3):
                    z = 2 * p + a - 1
                    pieces.append(edges[SLOTS[t][b], z] if z >= 0 else jnp.zeros((32, 128), BF))
            rows.append(jnp.concatenate(pieces, axis=1))
        versions, slope = first_level(dot(jnp.concatenate(rows, axis=0), weights), t)
        for p in range(4):
            first, second = 32 * p, 32 * p + 16
            for b, value in versions:
                before = jnp.concatenate([value[second : second + 8, 128:256], jnp.zeros((8, 128), F32)], axis=0)
                outer_short[b, p, 0:16, :] = before.astype(BF)
                outer_short[b, p, 16:32, :] = short_pair(value, first).astype(BF)
                outer_act[b, p, 0:16, :] = value[second : second + 16, 128:256].astype(BF)
                outer_act[b, p, 16:32, :] = value[first : first + 16, 0:128].astype(BF)
                outer_act[b, p, 32:48, :] = value[first : first + 16, 128:256].astype(BF)
                outer_act[b, p, 48:64, :] = value[second : second + 16, 0:128].astype(BF)
            outer_slope[p, t] = short_pair(slope, first)

    lhs = []
    for k in range(2):
        planes = [(b, 2 * k + a - 1) for a in range(3) for b in range(3)]
        lhs.append(
            jnp.concatenate([outer_act[b, p] if p >= 0 else jnp.zeros((64, 128), BF) for b, p in planes], axis=1)
        )
    out = dot(jnp.concatenate(lhs, axis=0), w_two[...])
    pairs, pairs_next, delta, patches = [], [], [], []
    for k in range(2):
        own = out[64 * k : 64 * k + 64]
        pre = jnp.concatenate(
            [own[16:48, 0:128], ends_ref[k, 0], own[48:64, 0:128]], axis=0
        ) + jnp.concatenate([own[0:48, 128:256], ends_ref[k, 1]], axis=0)
        feat, value = second_level(pre, jnp.concatenate([cot_ref[k, 0:48, :], cot_y[k]], axis=0))
        feat_ref[k, :, 0:384] = jnp.concatenate([feat[16 * m : 16 * m + 8] for m in range(3)], axis=1).astype(BF)
        feat_ref[k, :, 384:2048] = feat_in[k]
        copies.append(pltpu.make_async_copy(feat_ref.at[k], feat_hbm.at[k], sems.at[k]))
        copies[-1].start()
        value = value.reshape(4, 16, 128)
        outer = value[:, 0:8].reshape(32, 128)
        here = jnp.concatenate([outer[0:24], here_in[k], outer[24:32]], axis=0)
        outer_after = value[:, 1:9].reshape(32, 128)
        after = jnp.concatenate([outer_after[0:24], after_in[k], outer_after[24:32]], axis=0)
        pairs.append(jnp.concatenate([here[0:128], here[8:136]], axis=1).astype(BF))
        pairs_next.append(jnp.concatenate([after[0:128], after[8:136]], axis=1).astype(BF))
        zero = jnp.zeros((8, 128), F32)
        both = [
            jnp.concatenate([zero, zero, outer[0:24], zero], axis=0),
            jnp.concatenate([outer[0:8], zero, outer[8:24], zero, zero], axis=0),
        ]
        delta.append(jnp.concatenate(both, axis=1).astype(BF))
        short = []
        for a in range(3):
            for b in range(3):
                p = 2 * k + a - 1
                if p < 0:
                    short.append(jnp.zeros((48, 128), BF))
                else:
                    short.append(jnp.concatenate([outer_short[b, p], short_act[b, p, 0:16, :]], axis=0))
        patches.append(jnp.concatenate(short, axis=1))
    grad = dot(jnp.concatenate(delta, axis=0), jnp.concatenate(patches, axis=0), ((0,), (0,)))
    grad = grad_in[...] + grad[0:192]

    place = iota((64, 128), 1) >> 5
    turned = []
    for ab in range(9):
        a0, a1, a2 = (grad[64 * j : 64 * j + 64, 128 * ab : 128 * ab + 128] for j in range(3))
        across = pltpu.roll(jnp.where(place == 2, a1, jnp.where(place == 3, a2, a0)), 64, 1)
        joined = jnp.where(place == 0, a0, a1) + across
        shift = (3 * ab - 1) % 4
        other = (shift + 2) % 4
        outer = pltpu.roll(joined, 32 * shift, 1) if shift else joined
        inner = pltpu.roll(joined, 32 * other, 1) if other else joined
        turned += [outer, inner, outer]
    turned.append(jnp.zeros((64, 128), F32))
    for v in range(7):
        t0, t1, t2, t3 = turned[4 * v : 4 * v + 4]
        total[:, 128 * v : 128 * v + 128] = jnp.where(
            place < 2, jnp.where(place == 0, t0, t1), jnp.where(place == 2, t2, t3)
        )

    lhs_rows, rhs_rows = [], []
    for p in range(4):
        depth = [(1, p // 2)] if p % 2 == 0 else [(2, (p - 1) // 2), (0, (p + 1) // 2)]
        for t in range(2):
            width = [(1, pairs)] if t == 0 else [(2, pairs), (0, pairs_next)]
            taps = [(3 * a + b, source[k]) for a, k in depth if k < 2 for b, source in width]
            level = dot(
                jnp.concatenate([source for _, source in taps], axis=1),
                jnp.concatenate([w_two[128 * tap : 128 * tap + 128, :] for tap, _ in taps], axis=1),
                ((1,), (1,)),
            )
            level = level.astype(BF).astype(F32)
            for m in range(16):
                rows_out[m, pl.ds(t, 8, stride=2), :] = level[8 * m : 8 * m + 8]
            slope = jnp.concatenate([outer_slope[p, t], slope_ref[p, t]], axis=0)
            value = level * slope
            blocks = [
                jnp.concatenate([value[16 * n : 16 * n + 8], value[16 * n + 8 : 16 * n + 16]], axis=1)
                for n in (1, 2, 3, 4, 5, 6, 7, 0)
            ]
            lhs_rows.append(jnp.concatenate(blocks, axis=0).astype(BF))
            rhs_rows.append(
                jnp.concatenate([window(SLOTS[t][b], 2 * p + a - 1) for a in range(3) for b in range(3)], axis=1)
            )
        level_ref[p] = jnp.concatenate([rows_out[m] for m in range(16)], axis=1).astype(BF)
        copies.append(pltpu.make_async_copy(level_ref.at[p], level_hbm.at[p], sems.at[2 + p]))
        copies[-1].start()
    grad = dot(jnp.concatenate(lhs_rows, axis=0), jnp.concatenate(rhs_rows, axis=0), ((0,), (0,)))

    place = iota((32, 128), 1)
    found = jnp.zeros((32, 128), F32)
    for tap in range(9):
        some = jnp.zeros((32, 128), F32)
        for t in range(8):
            piece = grad[32 * t : 32 * t + 32, 128 * tap : 128 * tap + 128]
            shift = (3 * tap - 2 * t) % 128
            some = some + (pltpu.roll(piece, shift, 1) if shift else piece)
        local = place & 31
        found = jnp.where((local >= 3 * tap) & (local < 3 * tap + 3), some, found)
    total[:, 896:1024] = jnp.zeros((64, 128), F32)
    tall, short = 64 // ranks, 32 // ranks
    for d in range(ranks):
        total[tall * d : tall * d + short, 896:1024] = found[short * d : short * d + short]
    rank = lax.axis_index("dp")
    for step, out in enumerate(dealt):
        if tall % 8 == 0:
            start = pl.multiple_of((rank ^ step) * tall, tall)
            picked = total[pl.ds(start, tall), :]
        else:
            picked = total[0:tall, :]
            for d in range(1, ranks):
                picked = jnp.where((rank ^ step) == d, total[d * tall : d * tall + tall, :], picked)
        out[...] = picked.astype(BF)
    for copy in copies:
        copy.wait()


def sum_kernel(*refs):
    parts, out_ref = refs[:-1], refs[-1]
    values = [ref[...].astype(F32) for ref in parts]
    while len(values) > 1:
        values = [values[i] + values[i + 1] for i in range(0, len(values), 2)]
    out_ref[...] = values[0].astype(out_ref.dtype)


def share_kernel(mine_ref, first_ref, second_ref, out_ref):
    first = first_ref[...].astype(F32)
    odd = position("gx")[0]
    out_ref[...] = first + jnp.where(odd, second_ref[...], mine_ref[...]).astype(F32)


def last_kernel(scale_one, scale_two, *refs):
    parts, (two_hbm, one_ref, two_ref, sems) = refs[:-4], refs[-4:]
    values = [ref[...].astype(F32) for ref in parts]
    while len(values) > 1:
        values = [values[i] + values[i + 1] for i in range(0, len(values), 2)]
    value = values[0]
    tall = value.shape[0]
    short = tall // 2
    scaled = value[:, 0:896] * scale_two
    copies = []
    for tap in range(27):
        two_ref[tap] = scaled[:, 32 * tap : 32 * tap + 32]
        if tap % 9 == 8:
            part = pl.ds(tap - 8, 9)
            copies.append(pltpu.make_async_copy(two_ref.at[part], two_hbm.at[part], sems.at[tap // 9]))
            copies[-1].start()
    rows = value[0:short, 896:1024] * scale_one
    if short < 8:
        rows = jnp.concatenate([rows, jnp.zeros((8 - short, 128), F32)], axis=0)
    turned = rows.T
    for c in range(3):
        one_ref[:, c, :] = turned[32 * c : 32 * c + 27, 0:short]
    for copy in copies:
        copy.wait()


def call(kernel, outs, args, scratch=(), space=pltpu.VMEM, in_hbm=0, flops=0):
    spaces = [pltpu.HBM] * in_hbm + [pltpu.VMEM] * (len(outs) - in_hbm)
    return pl.pallas_call(
        kernel,
        out_shape=outs,
        in_specs=[pl.BlockSpec(memory_space=space)] * len(args),
        out_specs=[pl.BlockSpec(memory_space=kind) for kind in spaces],
        scratch_shapes=list(scratch),
        compiler_params=pltpu.CompilerParams(vmem_limit_bytes=VMEM_LIMIT),
        cost_estimate=pl.CostEstimate(flops=flops, bytes_accessed=1 << 20, transcendentals=0),
    )(*args)


def shape(dims, dtype):
    return jax.ShapeDtypeStruct(dims, dtype)


def exchange(value, axis, step):
    return lax.ppermute(value, axis, [(i, i ^ step) for i in range(lax.axis_size(axis))])


def trade_shared(value, steps):
    count, columns = lax.axis_size("gy"), lax.axis_size("gx")
    pairs = [(g * count + i, g * count + (i ^ steps[g % 2])) for g in range(columns) for i in range(count)]
    return lax.ppermute(value, ("gx", "gy"), pairs)


def body(magnetic, kernel_one, kernel_two, cotangent):
    ranks, count_gx, count_gy = (lax.axis_size(axis) for axis in ("dp", "gx", "gy"))
    depth = magnetic.shape[2]
    samples_all = magnetic.shape[0] * ranks
    cells_x = magnetic.shape[3] * count_gx
    cells_y = magnetic.shape[4] * count_gy
    scale_one = 1.0 / math.sqrt(samples_all * (depth // 2) * (cells_x // 2) * (cells_y // 2))
    scale_two = 1.0 / math.sqrt(samples_all * (depth // 4) * (cells_x // 4) * (cells_y // 4))
    field = magnetic.reshape(24, 32, 128)
    cot = cotangent.reshape(2, 8, 2048)
    one = kernel_one.reshape(27, 3, 32)
    two = kernel_two.reshape(864, 64)

    swaps_x, swaps_y = swaps("gx"), swaps("gy")
    nx, ny = len(swaps_x), len(swaps_y)
    operands = [pltpu.with_memory_space_constraint(array, pltpu.HBM) for array in (field, cot, one, two)]
    field, cot, one, two, *edges = call(
        lambda *refs: edge_x_kernel(nx, *refs),
        [shape(array.shape, BF) for array in operands] + [shape((128, 128), BF)] * nx,
        operands,
        [pltpu.VMEM((128, 128), F32), pltpu.SemaphoreType.DMA((4,))],
        space=pltpu.HBM,
    )
    got_x = [lax.ppermute(edge, ("dp", "gx"), pairs) for edge, pairs in zip(edges, swaps_x)]
    w_one, w_two, picks = call(
        weights_kernel,
        [shape((1152, 256), BF), shape((1152, 256), BF), shape((256, 2048), BF)],
        (one, two),
        [pltpu.VMEM((88, 32), F32)],
        flops=1 << 30,
    )
    split, *edges = call(
        lambda *refs: edge_y_kernel(nx, ny, *refs),
        [shape((5, 384, 128), BF)] + [shape((80, 128), BF)] * ny,
        (field, cot, *got_x),
        [pltpu.VMEM((24, 72, 128), F32)],
    )
    got_y = [lax.ppermute(edge, ("dp", "gy"), pairs) for edge, pairs in zip(edges, swaps_y)]
    first = call(
        lambda *refs: windows_kernel(nx, *refs),
        [
            shape((5, 8, 64, 128), BF),
            shape((5, 128, 256), BF),
            shape((3, 4, 112, 128), BF),
            shape((4, 2, 112, 128), F32),
            shape((2, 256, 128), F32),
            shape((2, 2, 16, 128), F32),
            shape((2, 8, 1664), BF),
            shape((2, 104, 128), F32),
            shape((2, 104, 128), F32),
            shape((192, 1152), F32),
        ],
        (split, w_one, w_two, cot, *got_x),
        [pltpu.VMEM((5, 8, 112, 128), BF), pltpu.VMEM((3, 4, 224, 128), BF)],
        flops=1 << 31,
    )
    tall = 64 // ranks
    features, level, *dealt = call(
        lambda *refs: main_kernel(ny, ranks, *refs),
        [shape((2, 8, 2048), BF), shape((4, 16, 2048), BF)] + [shape((tall, 1024), BF)] * ranks,
        (*first, picks, w_one, w_two, *got_y),
        [
            pltpu.VMEM((5, 8, 32, 128), BF),
            pltpu.VMEM((5, 8, 16, 128), BF),
            pltpu.VMEM((3, 4, 64, 128), BF),
            pltpu.VMEM((3, 4, 32, 128), BF),
            pltpu.VMEM((4, 2, 16, 128), F32),
            pltpu.VMEM((16, 16, 128), F32),
            pltpu.VMEM((64, 1024), F32),
            pltpu.VMEM((2, 8, 2048), BF),
            pltpu.VMEM((4, 16, 2048), BF),
            pltpu.SemaphoreType.DMA((6,)),
        ],
        in_hbm=2,
    )
    terms = dealt[:1] + [exchange(dealt[step], "dp", step) for step in range(1, ranks)]
    mine, = call(sum_kernel, [shape((tall, 1024), BF)], terms)
    step = 1
    while step < count_gx:
        mine, = call(sum_kernel, [shape((tall, 1024), BF)], (mine, exchange(mine, "gx", step)))
        step *= 2
    if count_gy == 4:
        terms = [mine, trade_shared(mine, (1, 2)), trade_shared(mine, (1, 3))]
        mine, = call(share_kernel, [shape((tall, 1024), F32)], terms)
        terms = [mine, exchange(mine, "gx", 1)]
    else:
        terms = [mine] + [exchange(mine, "gy", step) for step in range(1, count_gy)]
    grad_two, grad_one = call(
        lambda *refs: last_kernel(scale_one, scale_two, *refs),
        [shape((27, tall, 32), F32), shape((27, 3, tall // 2), F32)],
        terms,
        [pltpu.VMEM((27, tall, 32), F32), pltpu.SemaphoreType.DMA((3,))],
        in_hbm=1,
    )
    grad_one = grad_one.reshape(3, 3, 3, 3, tall // 2)
    grad_two = jnp.transpose(grad_two.reshape(3, 3, 3, tall, 32), (0, 1, 2, 4, 3))
    return (
        features.reshape(1, 2, 8, 2048),
        level.reshape(1, 4, 16, 2048),
        grad_one,
        grad_two,
    )


def solution(mesh):
    in_specs = (P("dp", None, None, "gx", "gy"), P(), P(), P("dp", None, "gx", "gy"))
    out_specs = (
        P("dp", None, "gx", "gy"),
        P("dp", None, "gx", "gy"),
        P(None, None, None, None, "dp"),
        P(None, None, None, None, "dp"),
    )
    return jax.shard_map(body, mesh=mesh, in_specs=in_specs, out_specs=out_specs, check_vma=False)
```

time: 266 us -> 31.4 us (0.12)
  local copies, waits for them, and re-layouts: 53.2 us -> 0 us
  waiting for transfers between devices: 63 us -> 10.1 us
  blocking collectives: 42.2 us -> 0 us
  matrix products: 41.1 us -> 0 us
  other arithmetic: 34.5 us -> 0 us
  between operations: 14.5 us -> 0.71 us
  Pallas kernels: 0 us -> 9.06 us
  starting transfers between devices: 16.1 us -> 11.3 us
    psum x1 -> x0, waiting for transfers between devices: 62.5 us -> none  [body(): total_one, total_two = lax.psum((local_one, local_two), ('dp', 'gx', 'gy'))]
    psum x1 -> x0, blocking collectives: 42.2 us -> none  [body(): total_one, total_two = lax.psum((local_one, local_two), ('dp', 'gx', 'gy'))]
    concatenate x10 -> x0, other arithmetic: 34.4 us -> none  [the longest x5 32.4 us: extend(): return jnp.concatenate([got_y, volume], axis=ydim)]
    transpose x2 -> x0, matrix products: 27.5 us -> none  [weight_grad(): return jnp.transpose(result, (2, 3, 4, 0, 1))]
    concatenate x12 -> x0, local copies, waits for them, and re-layouts: 19.4 us -> none  [the longest x9 14.6 us: extend(): return jnp.concatenate([got_y, volume], axis=ydim)]
    conv_general_dilated x3 -> x0, matrix products: 13.6 us -> none  [the longest x2 12.3 us: conv_down(): lax.conv_general_dilated(inputs_ext, kernel, (2, 2, 2), ((1, 0), (0, 0),...]
    unnamed x29 -> x0, local copies, waits for them, and re-layouts: 12.6 us -> none
    ppermute x6 -> x10, waiting for transfers between devices: 0.45 us -> 10.1 us  [the longest x5 6.24 us: exchange(): lax.ppermute(value, axis, [(i, i ^ step) for i in range(lax.axis_size(axi...]
  transfers between devices with their start and end apart: 7 -> 10, of which waited for: 2 -> 8; matrix products, arithmetic and copies ran while one was open for 33% -> 0% of each run, Pallas kernels for 0% -> 10%
where the time goes in v1:
time: 31.4 us; the launch traced here: 31.2 us
  starting transfers between devices  11.3 us (36%)
  waiting for transfers between devices  10.1 us (32%)
  Pallas kernels  9.06 us (29%)
  between operations  0.71 us (2%)
    pallas_call x9, Pallas kernels, call(): pl.pallas_call(kernel, out_shape=outs, in_specs=[pl.BlockSpec(memory_spac...  9.06 us
    ppermute x5, waiting for transfers between devices, exchange(): lax.ppermute(value, axis, [(i, i ^ step) for i in range(lax.axis_size(axi...  6.24 us
    ppermute x2, starting transfers between devices, body(): lax.ppermute(edge, ('dp', 'gy'), pairs)  4.47 us
    ppermute x5, starting transfers between devices, exchange(): lax.ppermute(value, axis, [(i, i ^ step) for i in range(lax.axis_size(axi...  4.24 us
    ppermute x2, waiting for transfers between devices, trade_shared(): return lax.ppermute(value, ('gx', 'gy'), pairs)  3.74 us
    ppermute x2, starting transfers between devices, trade_shared(): return lax.ppermute(value, ('gx', 'gy'), pairs)  2.09 us
  transfers between devices with their start and end apart: 10, of which 8 were waited for; matrix products, arithmetic and copies ran while one was open for 0% of the time, Pallas kernels for 10%

profile of v1, /device:TPU:0, one launch (start us, length us, event | category | flops | bytes accessed | tf_op | source)
XLA Modules:
  0.0 31.2 jit_solution(16516324561466706522)
XLA Ops:
  0.6 1.1 %shard_map.75 = (bf16[24,32,128]{2,1,0:T(8,128)(2,1)S(1)}, bf16[2,8,2048]{2,1,0:T(8,128)(2,1)S(1)}, bf16[27,3,32]{2,1,0:T(4,128)(2,1)S(1)}, bf16[864,64]{1,0:T(8,128)(2,1)S(1)}, bf16[128,128]{1,0:T(8,128)(2,1)S(1)}) custom-call(bf16[24,32,128]{2,1,0:T(8,128)(2,1)} %bitcast.11, bf16[2,8,2048]{2,1,0:T(8,128)(2,1)} %bitcast.12, bf16[27,3,32]{2,1,0:T(4,128)(2,1)} %bitcast.13, ...), custom_call_target="tpu_custom_call" | custom-call | bytes 1048576 | tf_op jit(solution)/shard_map/pallas_call | solution.py:532
  1.8 0.5 %collective-permute-start = (bf16[128,128]{1,0:T(8,128)(2,1)S(1)}, bf16[128,128]{1,0:T(8,128)(2,1)S(1)}, u32[]{:S(2)}, u32[]{:S(2)}) collective-permute-start(bf16[128,128]{1,0:T(8,128)(2,1)S(1)} %get-tuple-element.35), channel_id=1, source_target_pairs={{0,4},{4,0},{8,12},{12,8},{16,20},{20,16},{24,28},{28,24},{1,5},{5... | collective-permute-start | bytes 98312 | tf_op jit(solution)/shard_map/ppermute | solution.py:580
  2.3 0.7 %shard_map.77 = (bf16[1152,256]{1,0:T(8,128)(2,1)S(1)}, bf16[1152,256]{1,0:T(8,128)(2,1)S(1)}, bf16[256,2048]{1,0:T(8,128)(2,1)S(1)}) custom-call(bf16[27,3,32]{2,1,0:T(4,128)(2,1)S(1)} %get-tuple-element.37.one_ref, bf16[864,64]{1,0:T(8,128)(2,1)S(1)} %get-tuple-element.38.two_ref), custom_call_target="tpu_custom_call" | custom-call | flops 1073741824 | bytes 1048576 | tf_op jit(solution)/shard_map/pallas_call | solution.py:532
  3.0 0.2 collective-permute-done.refs_2_.refs_4_
  3.2 0.4 %shard_map.76 = (bf16[5,384,128]{2,1,0:T(8,128)(2,1)S(1)}, bf16[80,128]{1,0:T(8,128)(2,1)S(1)}, bf16[80,128]{1,0:T(8,128)(2,1)S(1)}) custom-call(bf16[24,32,128]{2,1,0:T(8,128)(2,1)S(1)} %get-tuple-element.33.refs_0_, bf16[2,8,2048]{2,1,0:T(8,128)(2,1)S(1)} %get-tuple-element.34.refs_1_.refs_3_, bf16[128,128]{1,0:T(8,128)(2,1)S(1)} %collective-permute-done.refs_2_.refs_4_), custom_call_target="tpu_custom_call" | custom-call | bytes 1048576 | tf_op jit(solution)/shard_map/pallas_call | solution.py:532
  3.5 3.0 %collective-permute-start.1 = (bf16[80,128]{1,0:T(8,128)(2,1)S(1)}, bf16[80,128]{1,0:T(8,128)(2,1)S(1)}, u32[]{:S(2)}, u32[]{:S(2)}) collective-permute-start(bf16[80,128]{1,0:T(8,128)(2,1)S(1)} %get-tuple-element.52), channel_id=1, source_target_pairs={{0,1},{1,0},{2,3},{3,2},{8,9},{9,8},{10,11},{11,10},{16,17},{17,16... | collective-permute-start | bytes 61448 | tf_op jit(solution)/shard_map/ppermute | solution.py:594
  6.5 1.5 %collective-permute-start.2 = (bf16[80,128]{1,0:T(8,128)(2,1)S(1)}, bf16[80,128]{1,0:T(8,128)(2,1)S(1)}, u32[]{:S(2)}, u32[]{:S(2)}) collective-permute-start(bf16[80,128]{1,0:T(8,128)(2,1)S(1)} %get-tuple-element.53), channel_id=1, source_target_pairs={{0,8},{1,2},{2,1},{3,11},{8,0},{9,10},{10,9},{11,3},{16,24},{17,18... | collective-permute-start | bytes 61448 | tf_op jit(solution)/shard_map/ppermute | solution.py:594
  8.0 2.5 %shard_map.78 = (bf16[5,8,64,128]{3,2,1,0:T(8,128)(2,1)S(1)}, bf16[5,128,256]{2,1,0:T(8,128)(2,1)S(1)}, bf16[3,4,112,128]{3,2,1,0:T(8,128)(2,1)S(1)}, f32[4,2,11...) custom-call(bf16[5,384,128]{2,1,0:T(8,128)(2,1)S(1)} %get-tuple-elem, ...), custom_call_target="tpu_custom_call" | custom-call | flops 2147483648 | bytes 1048576 | tf_op jit(solution)/shard_map/pallas_call | solution.py:532
  10.5 0.0 collective-permute-done.1.refs_13_
  10.5 0.0 collective-permute-done.2.refs_14_
  10.5 2.9 %shard_map.79 = (bf16[2,8,2048]{2,1,0:T(8,128)(2,1)}, bf16[4,16,2048]{2,1,0:T(8,128)(2,1)}, bf16[16,1024]{1,0:T(8,128)(2,1)S(1)}, bf16[16,1024]{1,0:T(8,128)(2,1...) custom-call(bf16[5,8,64,128]{3,2,1,0:T(8,128)(2,1)S(1)} %get-tuple-element.41.refs_0_, ...), custom_call_target="tpu_custom_call" | custom-call | bytes 1048576 | tf_op jit(solution)/shard_map/pallas_call | solution.py:532
  13.4 1.4 %collective-permute-start.3 = (bf16[16,1024]{1,0:T(8,128)(2,1)S(1)}, bf16[16,1024]{1,0:T(8,128)(2,1)S(1)}, u32[]{:S(2)}, u32[]{:S(2)}) collective-permute-start(bf16[16,1024]{1,0:T(8,128)(2,1)S(1)} %get-tuple-element.57), channel_id=1, source_target_pairs={{0,8},{8,0},{16,24},{24,16},{1,9},{9,1},{17,25},{25,17},{2,10},{10... | collective-permute-start | bytes 98312 | tf_op jit(solution)/shard_map/ppermute | solution.py:548
  14.8 1.5 %collective-permute-start.4 = (bf16[16,1024]{1,0:T(8,128)(2,1)S(1)}, bf16[16,1024]{1,0:T(8,128)(2,1)S(1)}, u32[]{:S(2)}, u32[]{:S(2)}) collective-permute-start(bf16[16,1024]{1,0:T(8,128)(2,1)S(1)} %get-tuple-element.58), channel_id=1, source_target_pairs={{0,16},{8,24},{16,0},{24,8},{1,17},{9,25},{17,1},{25,9},{2,18},{10... | collective-permute-start | bytes 98312 | tf_op jit(solution)/shard_map/ppermute | solution.py:548
  16.3 0.7 %collective-permute-start.5 = (bf16[16,1024]{1,0:T(8,128)(2,1)S(1)}, bf16[16,1024]{1,0:T(8,128)(2,1)S(1)}, u32[]{:S(2)}, u32[]{:S(2)}) collective-permute-start(bf16[16,1024]{1,0:T(8,128)(2,1)S(1)} %get-tuple-element.59), channel_id=1, source_target_pairs={{0,24},{8,16},{16,8},{24,0},{1,25},{9,17},{17,9},{25,1},{2,26},{10... | collective-permute-start | bytes 98312 | tf_op jit(solution)/shard_map/ppermute | solution.py:548
  17.0 0.7 %collective-permute-done.3.refs_1_ = bf16[16,1024]{1,0:T(8,128)(2,1)S(1)} collective-permute-done((bf16[16,1024]{1,0:T(8,128)(2,1)S(1)}, bf16[16,1024]{1,0:T(8,128)(2,1)S(1)}, u32[]{:S(2)}, u32[]{:S(2)}) %collective-permute-start.3) | collective-permute-done | bytes 32800 | tf_op jit(solution)/shard_map/ppermute | solution.py:548
  17.7 1.2 %collective-permute-done.4.refs_2_ = bf16[16,1024]{1,0:T(8,128)(2,1)S(1)} collective-permute-done((bf16[16,1024]{1,0:T(8,128)(2,1)S(1)}, bf16[16,1024]{1,0:T(8,128)(2,1)S(1)}, u32[]{:S(2)}, u32[]{:S(2)}) %collective-permute-start.4) | collective-permute-done | bytes 32800 | tf_op jit(solution)/shard_map/ppermute | solution.py:548
  18.9 2.2 %collective-permute-done.5.refs_3_ = bf16[16,1024]{1,0:T(8,128)(2,1)S(1)} collective-permute-done((bf16[16,1024]{1,0:T(8,128)(2,1)S(1)}, bf16[16,1024]{1,0:T(8,128)(2,1)S(1)}, u32[]{:S(2)}, u32[]{:S(2)}) %collective-permute-start.5) | collective-permute-done | bytes 32800 | tf_op jit(solution)/shard_map/ppermute | solution.py:548
  21.2 0.1 collective-permute-start.6
  21.2 1.2 %collective-permute-done.6.refs_1_ = bf16[16,1024]{1,0:T(8,128)(2,1)S(1)} collective-permute-done((bf16[16,1024]{1,0:T(8,128)(2,1)S(1)}, bf16[16,1024]{1,0:T(8,128)(2,1)S(1)}, u32[]{:S(2)}, u32[]{:S(2)}) %collective-permute-start.6) | collective-permute-done | bytes 32800 | tf_op jit(solution)/shard_map/ppermute | solution.py:548
  22.5 1.9 %collective-permute-start.8 = (bf16[16,1024]{1,0:T(8,128)(2,1)S(1)}, bf16[16,1024]{1,0:T(8,128)(2,1)S(1)}, u32[]{:S(2)}, u32[]{:S(2)}) collective-permute-start(bf16[16,1024]{1,0:T(8,128)(2,1)S(1)} %shard_map.81.mine_ref), channel_id=1, source_target_pairs={{0,1},{1,0},{2,3},{3,2},{4,7},{5,6},{6,5},{7,4},{8,9},{9,8},{10,11... | collective-permute-start | bytes 98312 | tf_op jit(solution)/shard_map/ppermute | solution.py:554
  24.4 0.2 collective-permute-start.7
  24.5 1.9 %collective-permute-done.8.second_ref = bf16[16,1024]{1,0:T(8,128)(2,1)S(1)} collective-permute-done((bf16[16,1024]{1,0:T(8,128)(2,1)S(1)}, bf16[16,1024]{1,0:T(8,128)(2,1)S(1)}, u32[]{:S(2)}, u32[]{:S(2)}) %collective-permute-start.8) | collective-permute-done | bytes 32800 | tf_op jit(solution)/shard_map/ppermute | solution.py:554
  26.4 1.9 %collective-permute-done.7.first_ref = bf16[16,1024]{1,0:T(8,128)(2,1)S(1)} collective-permute-done((bf16[16,1024]{1,0:T(8,128)(2,1)S(1)}, bf16[16,1024]{1,0:T(8,128)(2,1)S(1)}, u32[]{:S(2)}, u32[]{:S(2)}) %collective-permute-start.7) | collective-permute-done | bytes 32800 | tf_op jit(solution)/shard_map/ppermute | solution.py:554
  28.3 0.6 %collective-permute-start.9 = (f32[16,1024]{1,0:T(8,128)S(1)}, f32[16,1024]{1,0:T(8,128)S(1)}, u32[]{:S(2)}, u32[]{:S(2)}) collective-permute-start(f32[16,1024]{1,0:T(8,128)S(1)} %shard_map.82.refs_0_), channel_id=1, source_target_pairs={{0,4},{4,0},{1,5},{5,1},{2,6},{6,2},{3,7},{7,3},{8,12},{12,8},{9,1... | collective-permute-start | bytes 196616 | tf_op jit(solution)/shard_map/ppermute | solution.py:548
  28.9 0.9 %collective-permute-done.9.refs_1_ = f32[16,1024]{1,0:T(8,128)S(1)} collective-permute-done((f32[16,1024]{1,0:T(8,128)S(1)}, f32[16,1024]{1,0:T(8,128)S(1)}, u32[]{:S(2)}, u32[]{:S(2)}) %collective-permute-start.9) | collective-permute-done | bytes 65568 | tf_op jit(solution)/shard_map/ppermute | solution.py:548
  29.8 1.4 %shard_map.83 = (f32[27,16,32]{2,1,0:T(8,128)}, f32[27,3,8]{2,1,0:T(4,128)}) custom-call(f32[16,1024]{1,0:T(8,128)S(1)} %shard_map.82.refs_0_, f32[16,1024]{1,0:T(8,128)S(1)} %collective-permute-done.9.refs_1_), custom_call_target="tpu_custom_call" | custom-call | bytes 1048576 | tf_op jit(solution)/shard_map/pallas_call | solution.py:532
  (3 shorter events, 0.0 us)
Async XLA Ops:
  1.8 1.4 %collective-permute-start = (bf16[128,128]{1,0:T(8,128)(2,1)S(1)}, bf16[128,128]{1,0:T(8,128)(2,1)S(1)}, u32[]{:S(2)}, u32[]{:S(2)}) collective-permute-start(bf16[128,128]{1,0:T(8,128)(2,1)S(1)} %get-tuple-element.35), channel_id=1, source_target_pairs={{0,4},{4,0},{8,12},{12,8},{16,20},{20,16},{24,28},{28,24},{1,5},{5... | collective-permute-start | bytes 98312 | tf_op jit(solution)/shard_map/ppermute | solution.py:580
  3.5 6.9 %collective-permute-start.1 = (bf16[80,128]{1,0:T(8,128)(2,1)S(1)}, bf16[80,128]{1,0:T(8,128)(2,1)S(1)}, u32[]{:S(2)}, u32[]{:S(2)}) collective-permute-start(bf16[80,128]{1,0:T(8,128)(2,1)S(1)} %get-tuple-element.52), channel_id=1, source_target_pairs={{0,1},{1,0},{2,3},{3,2},{8,9},{9,8},{10,11},{11,10},{16,17},{17,16... | collective-permute-start | bytes 61448 | tf_op jit(solution)/shard_map/ppermute | solution.py:594
  6.5 4.0 %collective-permute-start.2 = (bf16[80,128]{1,0:T(8,128)(2,1)S(1)}, bf16[80,128]{1,0:T(8,128)(2,1)S(1)}, u32[]{:S(2)}, u32[]{:S(2)}) collective-permute-start(bf16[80,128]{1,0:T(8,128)(2,1)S(1)} %get-tuple-element.53), channel_id=1, source_target_pairs={{0,8},{1,2},{2,1},{3,11},{8,0},{9,10},{10,9},{11,3},{16,24},{17,18... | collective-permute-start | bytes 61448 | tf_op jit(solution)/shard_map/ppermute | solution.py:594
  13.4 4.3 %collective-permute-start.3 = (bf16[16,1024]{1,0:T(8,128)(2,1)S(1)}, bf16[16,1024]{1,0:T(8,128)(2,1)S(1)}, u32[]{:S(2)}, u32[]{:S(2)}) collective-permute-start(bf16[16,1024]{1,0:T(8,128)(2,1)S(1)} %get-tuple-element.57), channel_id=1, source_target_pairs={{0,8},{8,0},{16,24},{24,16},{1,9},{9,1},{17,25},{25,17},{2,10},{10... | collective-permute-start | bytes 98312 | tf_op jit(solution)/shard_map/ppermute | solution.py:548
  14.8 4.1 %collective-permute-start.4 = (bf16[16,1024]{1,0:T(8,128)(2,1)S(1)}, bf16[16,1024]{1,0:T(8,128)(2,1)S(1)}, u32[]{:S(2)}, u32[]{:S(2)}) collective-permute-start(bf16[16,1024]{1,0:T(8,128)(2,1)S(1)} %get-tuple-element.58), channel_id=1, source_target_pairs={{0,16},{8,24},{16,0},{24,8},{1,17},{9,25},{17,1},{25,9},{2,18},{10... | collective-permute-start | bytes 98312 | tf_op jit(solution)/shard_map/ppermute | solution.py:548
  16.3 4.8 %collective-permute-start.5 = (bf16[16,1024]{1,0:T(8,128)(2,1)S(1)}, bf16[16,1024]{1,0:T(8,128)(2,1)S(1)}, u32[]{:S(2)}, u32[]{:S(2)}) collective-permute-start(bf16[16,1024]{1,0:T(8,128)(2,1)S(1)} %get-tuple-element.59), channel_id=1, source_target_pairs={{0,24},{8,16},{16,8},{24,0},{1,25},{9,17},{17,9},{25,1},{2,26},{10... | collective-permute-start | bytes 98312 | tf_op jit(solution)/shard_map/ppermute | solution.py:548
  21.2 1.3 %collective-permute-start.6 = (bf16[16,1024]{1,0:T(8,128)(2,1)S(1)}, bf16[16,1024]{1,0:T(8,128)(2,1)S(1)}, u32[]{:S(2)}, u32[]{:S(2)}) collective-permute-start(bf16[16,1024]{1,0:T(8,128)(2,1)S(1)} %shard_map.80.refs_0_), channel_id=1, source_target_pairs={{0,4},{4,0},{1,5},{5,1},{2,6},{6,2},{3,7},{7,3},{8,12},{12,8},{9,1... | collective-permute-start | bytes 98312 | tf_op jit(solution)/shard_map/ppermute | solution.py:548
  22.5 4.0 %collective-permute-start.8 = (bf16[16,1024]{1,0:T(8,128)(2,1)S(1)}, bf16[16,1024]{1,0:T(8,128)(2,1)S(1)}, u32[]{:S(2)}, u32[]{:S(2)}) collective-permute-start(bf16[16,1024]{1,0:T(8,128)(2,1)S(1)} %shard_map.81.mine_ref), channel_id=1, source_target_pairs={{0,1},{1,0},{2,3},{3,2},{4,7},{5,6},{6,5},{7,4},{8,9},{9,8},{10,11... | collective-permute-start | bytes 98312 | tf_op jit(solution)/shard_map/ppermute | solution.py:554
  24.4 3.9 %collective-permute-start.7 = (bf16[16,1024]{1,0:T(8,128)(2,1)S(1)}, bf16[16,1024]{1,0:T(8,128)(2,1)S(1)}, u32[]{:S(2)}, u32[]{:S(2)}) collective-permute-start(bf16[16,1024]{1,0:T(8,128)(2,1)S(1)} %shard_map.81.mine_ref), channel_id=1, source_target_pairs={{0,1},{1,0},{2,3},{3,2},{4,6},{5,7},{6,4},{7,5},{8,9},{9,8},{10,11... | collective-permute-start | bytes 98312 | tf_op jit(solution)/shard_map/ppermute | solution.py:554
  28.3 1.5 %collective-permute-start.9 = (f32[16,1024]{1,0:T(8,128)S(1)}, f32[16,1024]{1,0:T(8,128)S(1)}, u32[]{:S(2)}, u32[]{:S(2)}) collective-permute-start(f32[16,1024]{1,0:T(8,128)S(1)} %shard_map.82.refs_0_), channel_id=1, source_target_pairs={{0,4},{4,0},{1,5},{5,1},{2,6},{6,2},{3,7},{7,3},{8,12},{12,8},{9,1... | collective-permute-start | bytes 196616 | tf_op jit(solution)/shard_map/ppermute | solution.py:548

commit v2 on v1

--- a/solution.py
+++ b/solution.py
@@ -292,7 +292,7 @@
         delta.append(jnp.concatenate(both, axis=1).astype(BF))
         short = [short_act[b, p] if p >= 0 else jnp.zeros((112, 128), BF) for b, p in planes]
         patches.append(jnp.concatenate(short, axis=1))
-    grad_ref[...] = dot(jnp.concatenate(delta, axis=0), jnp.concatenate(patches, axis=0), ((0,), (0,)))[0:192]
+    grad_ref[...] = dot(jnp.concatenate(delta, axis=0), jnp.concatenate(patches, axis=0), ((0,), (0,)))
 
 
 def main_kernel(
@@ -409,15 +409,14 @@
                 else:
                     short.append(jnp.concatenate([outer_short[b, p], short_act[b, p, 0:16, :]], axis=0))
         patches.append(jnp.concatenate(short, axis=1))
-    grad = dot(jnp.concatenate(delta, axis=0), jnp.concatenate(patches, axis=0), ((0,), (0,)))
-    grad = grad_in[...] + grad[0:192]
+    grad = grad_in[...] + dot(jnp.concatenate(delta, axis=0), jnp.concatenate(patches, axis=0), ((0,), (0,)))
 
     place = iota((64, 128), 1) >> 5
     turned = []
     for ab in range(9):
         a0, a1, a2 = (grad[64 * j : 64 * j + 64, 128 * ab : 128 * ab + 128] for j in range(3))
-        across = pltpu.roll(jnp.where(place == 2, a1, jnp.where(place == 3, a2, a0)), 64, 1)
-        joined = jnp.where(place == 0, a0, a1) + across
+        r0, r1, r2 = (pltpu.roll(a, 64, 1) for a in (a0, a1, a2))
+        joined = jnp.where(place == 0, a0 + r1, jnp.where(place == 1, a1 + r2, a1 + r0))
         shift = (3 * ab - 1) % 4
         other = (shift + 2) % 4
         outer = pltpu.roll(joined, 32 * shift, 1) if shift else joined
@@ -502,7 +501,7 @@
 
 
 def last_kernel(scale_one, scale_two, *refs):
-    parts, (two_hbm, one_ref, two_ref, sems) = refs[:-4], refs[-4:]
+    parts, (one_ref, two_ref) = refs[:-2], refs[-2:]
     values = [ref[...].astype(F32) for ref in parts]
     while len(values) > 1:
         values = [values[i] + values[i + 1] for i in range(0, len(values), 2)]
@@ -510,21 +509,14 @@
     tall = value.shape[0]
     short = tall // 2
     scaled = value[:, 0:896] * scale_two
-    copies = []
     for tap in range(27):
         two_ref[tap] = scaled[:, 32 * tap : 32 * tap + 32]
-        if tap % 9 == 8:
-            part = pl.ds(tap - 8, 9)
-            copies.append(pltpu.make_async_copy(two_ref.at[part], two_hbm.at[part], sems.at[tap // 9]))
-            copies[-1].start()
     rows = value[0:short, 896:1024] * scale_one
     if short < 8:
         rows = jnp.concatenate([rows, jnp.zeros((8 - short, 128), F32)], axis=0)
     turned = rows.T
     for c in range(3):
         one_ref[:, c, :] = turned[32 * c : 32 * c + 27, 0:short]
-    for copy in copies:
-        copy.wait()
 
 
 def call(kernel, outs, args, scratch=(), space=pltpu.VMEM, in_hbm=0, flops=0):
@@ -548,10 +540,17 @@
     return lax.ppermute(value, axis, [(i, i ^ step) for i in range(lax.axis_size(axis))])
 
 
-def trade_shared(value, steps):
-    count, columns = lax.axis_size("gy"), lax.axis_size("gx")
-    pairs = [(g * count + i, g * count + (i ^ steps[g % 2])) for g in range(columns) for i in range(count)]
-    return lax.ppermute(value, ("gx", "gy"), pairs)
+def trade_shared(value, even_step, odd_step):
+    count, columns, ranks = lax.axis_size("gy"), lax.axis_size("gx"), lax.axis_size("dp")
+    pairs = []
+    for d in range(ranks):
+        for g in range(columns):
+            for i in range(count):
+                to_d, to_i = d, i ^ (odd_step if g % 2 else even_step)
+                if g % 2 == 0 and even_step == 0:
+                    to_d = (d ^ 1) % ranks
+                pairs.append(((d * columns + g) * count + i, (to_d * columns + g) * count + to_i))
+    return lax.ppermute(value, ("dp", "gx", "gy"), pairs)
 
 
 def body(magnetic, kernel_one, kernel_two, cotangent):
@@ -604,7 +603,7 @@
             shape((2, 8, 1664), BF),
             shape((2, 104, 128), F32),
             shape((2, 104, 128), F32),
-            shape((192, 1152), F32),
+            shape((256, 1152), F32),
         ],
         (split, w_one, w_two, cot, *got_x),
         [pltpu.VMEM((5, 8, 112, 128), BF), pltpu.VMEM((3, 4, 224, 128), BF)],
@@ -629,24 +628,22 @@
         ],
         in_hbm=2,
     )
-    terms = dealt[:1] + [exchange(dealt[step], "dp", step) for step in range(1, ranks)]
+    terms = [exchange(dealt[step], "dp", step) for step in (ranks - 1, *range(1, ranks - 1))] + dealt[:1]
     mine, = call(sum_kernel, [shape((tall, 1024), BF)], terms)
     step = 1
     while step < count_gx:
         mine, = call(sum_kernel, [shape((tall, 1024), BF)], (mine, exchange(mine, "gx", step)))
         step *= 2
     if count_gy == 4:
-        terms = [mine, trade_shared(mine, (1, 2)), trade_shared(mine, (1, 3))]
+        terms = [mine, trade_shared(mine, 1, 2), trade_shared(mine, 0, 3)]
         mine, = call(share_kernel, [shape((tall, 1024), F32)], terms)
         terms = [mine, exchange(mine, "gx", 1)]
     else:
         terms = [mine] + [exchange(mine, "gy", step) for step in range(1, count_gy)]
-    grad_two, grad_one = call(
+    grad_one, grad_two = call(
         lambda *refs: last_kernel(scale_one, scale_two, *refs),
-        [shape((27, tall, 32), F32), shape((27, 3, tall // 2), F32)],
+        [shape((27, 3, tall // 2), F32), shape((27, tall, 32), F32)],
         terms,
-        [pltpu.VMEM((27, tall, 32), F32), pltpu.SemaphoreType.DMA((3,))],
-        in_hbm=1,
     )
     grad_one = grad_one.reshape(3, 3, 3, 3, tall // 2)
     grad_two = jnp.transpose(grad_two.reshape(3, 3, 3, tall, 32), (0, 1, 2, 4, 3))

time: 31.4 us -> 29.9 us (0.952)
  waiting for transfers between devices: 10.1 us -> 7.76 us
  starting transfers between devices: 11.3 us -> 12.9 us
  Pallas kernels: 9.06 us -> 8.35 us
    ppermute x2, waiting for transfers between devices: 3.74 us -> 2.1 us  [trade_shared(): return lax.ppermute(value, ('dp', 'gx', 'gy'), pairs)]
    ppermute x2, starting transfers between devices: 2.09 us -> 3.22 us  [trade_shared(): return lax.ppermute(value, ('dp', 'gx', 'gy'), pairs)]
    ppermute x5, waiting for transfers between devices: 6.24 us -> 5.5 us  [exchange(): lax.ppermute(value, axis, [(i, i ^ step) for i in range(lax.axis_size(axi...]
    pallas_call x9, Pallas kernels: 9.06 us -> 8.35 us  [call(): pl.pallas_call(kernel, out_shape=outs, in_specs=[pl.BlockSpec(memory_spac...]
    ppermute x5, starting transfers between devices: 4.24 us -> 4.72 us  [exchange(): lax.ppermute(value, axis, [(i, i ^ step) for i in range(lax.axis_size(axi...]
  transfers between devices with their start and end apart: 10 -> 10, of which waited for: 8 -> 8; matrix products, arithmetic and copies ran while one was open for 0% -> 0% of each run, Pallas kernels for 10% -> 11%
where the time goes in v2:
time: 29.9 us; the launch traced here: 29.8 us
  starting transfers between devices  12.9 us (43%)
  Pallas kernels  8.35 us (28%)
  waiting for transfers between devices  7.76 us (26%)
  between operations  0.71 us (2%)
    pallas_call x9, Pallas kernels, call(): pl.pallas_call(kernel, out_shape=outs, in_specs=[pl.BlockSpec(memory_spac...  8.35 us
    ppermute x5, waiting for transfers between devices, exchange(): lax.ppermute(value, axis, [(i, i ^ step) for i in range(lax.axis_size(axi...  5.5 us
    ppermute x5, starting transfers between devices, exchange(): lax.ppermute(value, axis, [(i, i ^ step) for i in range(lax.axis_size(axi...  4.72 us
    ppermute x2, starting transfers between devices, body(): lax.ppermute(edge, ('dp', 'gy'), pairs)  4.47 us
    ppermute x2, starting transfers between devices, trade_shared(): return lax.ppermute(value, ('dp', 'gx', 'gy'), pairs)  3.22 us
    ppermute x2, waiting for transfers between devices, trade_shared(): return lax.ppermute(value, ('dp', 'gx', 'gy'), pairs)  2.1 us
  transfers between devices with their start and end apart: 10, of which 8 were waited for; matrix products, arithmetic and copies ran while one was open for 0% of the time, Pallas kernels for 11%

profile of v2, /device:TPU:0, one launch (start us, length us, event | category | flops | bytes accessed | tf_op | source)
XLA Modules:
  0.0 29.8 jit_solution(6035451671717285012)
XLA Ops:
  0.6 1.1 %shard_map.75 = (bf16[24,32,128]{2,1,0:T(8,128)(2,1)S(1)}, bf16[2,8,2048]{2,1,0:T(8,128)(2,1)S(1)}, bf16[27,3,32]{2,1,0:T(4,128)(2,1)S(1)}, bf16[864,64]{1,0:T(8,128)(2,1)S(1)}, bf16[128,128]{1,0:T(8,128)(2,1)S(1)}) custom-call(bf16[24,32,128]{2,1,0:T(8,128)(2,1)} %bitcast.11, bf16[2,8,2048]{2,1,0:T(8,128)(2,1)} %bitcast.12, bf16[27,3,32]{2,1,0:T(4,128)(2,1)} %bitcast.13, ...), custom_call_target="tpu_custom_call" | custom-call | bytes 1048576 | tf_op jit(solution)/shard_map/pallas_call | solution.py:524
  1.8 0.5 %collective-permute-start = (bf16[128,128]{1,0:T(8,128)(2,1)S(1)}, bf16[128,128]{1,0:T(8,128)(2,1)S(1)}, u32[]{:S(2)}, u32[]{:S(2)}) collective-permute-start(bf16[128,128]{1,0:T(8,128)(2,1)S(1)} %get-tuple-element.35), channel_id=1, source_target_pairs={{0,4},{4,0},{8,12},{12,8},{16,20},{20,16},{24,28},{28,24},{1,5},{5... | collective-permute-start | bytes 98312 | tf_op jit(solution)/shard_map/ppermute | solution.py:579
  2.3 0.7 %shard_map.77 = (bf16[1152,256]{1,0:T(8,128)(2,1)S(1)}, bf16[1152,256]{1,0:T(8,128)(2,1)S(1)}, bf16[256,2048]{1,0:T(8,128)(2,1)S(1)}) custom-call(bf16[27,3,32]{2,1,0:T(4,128)(2,1)S(1)} %get-tuple-element.37.one_ref, bf16[864,64]{1,0:T(8,128)(2,1)S(1)} %get-tuple-element.38.two_ref), custom_call_target="tpu_custom_call" | custom-call | flops 1073741824 | bytes 1048576 | tf_op jit(solution)/shard_map/pallas_call | solution.py:524
  3.0 0.2 collective-permute-done.refs_2_.refs_4_
  3.2 0.4 %shard_map.76 = (bf16[5,384,128]{2,1,0:T(8,128)(2,1)S(1)}, bf16[80,128]{1,0:T(8,128)(2,1)S(1)}, bf16[80,128]{1,0:T(8,128)(2,1)S(1)}) custom-call(bf16[24,32,128]{2,1,0:T(8,128)(2,1)S(1)} %get-tuple-element.33.refs_0_, bf16[2,8,2048]{2,1,0:T(8,128)(2,1)S(1)} %get-tuple-element.34.refs_1_.refs_3_, bf16[128,128]{1,0:T(8,128)(2,1)S(1)} %collective-permute-done.refs_2_.refs_4_), custom_call_target="tpu_custom_call" | custom-call | bytes 1048576 | tf_op jit(solution)/shard_map/pallas_call | solution.py:524
  3.5 3.0 %collective-permute-start.1 = (bf16[80,128]{1,0:T(8,128)(2,1)S(1)}, bf16[80,128]{1,0:T(8,128)(2,1)S(1)}, u32[]{:S(2)}, u32[]{:S(2)}) collective-permute-start(bf16[80,128]{1,0:T(8,128)(2,1)S(1)} %get-tuple-element.52), channel_id=1, source_target_pairs={{0,1},{1,0},{2,3},{3,2},{8,9},{9,8},{10,11},{11,10},{16,17},{17,16... | collective-permute-start | bytes 61448 | tf_op jit(solution)/shard_map/ppermute | solution.py:593
  6.5 1.5 %collective-permute-start.2 = (bf16[80,128]{1,0:T(8,128)(2,1)S(1)}, bf16[80,128]{1,0:T(8,128)(2,1)S(1)}, u32[]{:S(2)}, u32[]{:S(2)}) collective-permute-start(bf16[80,128]{1,0:T(8,128)(2,1)S(1)} %get-tuple-element.53), channel_id=1, source_target_pairs={{0,8},{1,2},{2,1},{3,11},{8,0},{9,10},{10,9},{11,3},{16,24},{17,18... | collective-permute-start | bytes 61448 | tf_op jit(solution)/shard_map/ppermute | solution.py:593
  8.0 2.5 %shard_map.78 = (bf16[5,8,64,128]{3,2,1,0:T(8,128)(2,1)S(1)}, bf16[5,128,256]{2,1,0:T(8,128)(2,1)S(1)}, bf16[3,4,112,128]{3,2,1,0:T(8,128)(2,1)S(1)}, f32[4,2,11...) custom-call(bf16[5,384,128]{2,1,0:T(8,128)(2,1)S(1)} %get-tuple-elem, ...), custom_call_target="tpu_custom_call" | custom-call | flops 2147483648 | bytes 1048576 | tf_op jit(solution)/shard_map/pallas_call | solution.py:524
  10.5 0.0 collective-permute-done.1.refs_13_
  10.5 0.0 collective-permute-done.2.refs_14_
  10.5 2.8 %shard_map.79 = (bf16[2,8,2048]{2,1,0:T(8,128)(2,1)}, bf16[4,16,2048]{2,1,0:T(8,128)(2,1)}, bf16[16,1024]{1,0:T(8,128)(2,1)S(1)}, bf16[16,1024]{1,0:T(8,128)(2,1...) custom-call(bf16[5,8,64,128]{3,2,1,0:T(8,128)(2,1)S(1)} %get-tuple-element.41.refs_0_, ...), custom_call_target="tpu_custom_call" | custom-call | bytes 1048576 | tf_op jit(solution)/shard_map/pallas_call | solution.py:524
  13.3 2.3 %collective-permute-start.3 = (bf16[16,1024]{1,0:T(8,128)(2,1)S(1)}, bf16[16,1024]{1,0:T(8,128)(2,1)S(1)}, u32[]{:S(2)}, u32[]{:S(2)}) collective-permute-start(bf16[16,1024]{1,0:T(8,128)(2,1)S(1)} %get-tuple-element.56), channel_id=1, source_target_pairs={{0,24},{8,16},{16,8},{24,0},{1,25},{9,17},{17,9},{25,1},{2,26},{10... | collective-permute-start | bytes 98312 | tf_op jit(solution)/shard_map/ppermute | solution.py:540
  15.7 0.7 %collective-permute-start.4 = (bf16[16,1024]{1,0:T(8,128)(2,1)S(1)}, bf16[16,1024]{1,0:T(8,128)(2,1)S(1)}, u32[]{:S(2)}, u32[]{:S(2)}) collective-permute-start(bf16[16,1024]{1,0:T(8,128)(2,1)S(1)} %get-tuple-element.57), channel_id=1, source_target_pairs={{0,8},{8,0},{16,24},{24,16},{1,9},{9,1},{17,25},{25,17},{2,10},{10... | collective-permute-start | bytes 98312 | tf_op jit(solution)/shard_map/ppermute | solution.py:540
  16.4 0.5 %collective-permute-start.5 = (bf16[16,1024]{1,0:T(8,128)(2,1)S(1)}, bf16[16,1024]{1,0:T(8,128)(2,1)S(1)}, u32[]{:S(2)}, u32[]{:S(2)}) collective-permute-start(bf16[16,1024]{1,0:T(8,128)(2,1)S(1)} %get-tuple-element.58), channel_id=1, source_target_pairs={{0,16},{8,24},{16,0},{24,8},{1,17},{9,25},{17,1},{25,9},{2,18},{10... | collective-permute-start | bytes 98312 | tf_op jit(solution)/shard_map/ppermute | solution.py:540
  16.9 1.3 %collective-permute-done.3.refs_0_ = bf16[16,1024]{1,0:T(8,128)(2,1)S(1)} collective-permute-done((bf16[16,1024]{1,0:T(8,128)(2,1)S(1)}, bf16[16,1024]{1,0:T(8,128)(2,1)S(1)}, u32[]{:S(2)}, u32[]{:S(2)}) %collective-permute-start.3) | collective-permute-done | bytes 32800 | tf_op jit(solution)/shard_map/ppermute | solution.py:540
  18.2 1.3 %collective-permute-done.4.refs_1_ = bf16[16,1024]{1,0:T(8,128)(2,1)S(1)} collective-permute-done((bf16[16,1024]{1,0:T(8,128)(2,1)S(1)}, bf16[16,1024]{1,0:T(8,128)(2,1)S(1)}, u32[]{:S(2)}, u32[]{:S(2)}) %collective-permute-start.4) | collective-permute-done | bytes 32800 | tf_op jit(solution)/shard_map/ppermute | solution.py:540
  19.6 0.7 %collective-permute-done.5.refs_2_ = bf16[16,1024]{1,0:T(8,128)(2,1)S(1)} collective-permute-done((bf16[16,1024]{1,0:T(8,128)(2,1)S(1)}, bf16[16,1024]{1,0:T(8,128)(2,1)S(1)}, u32[]{:S(2)}, u32[]{:S(2)}) %collective-permute-start.5) | collective-permute-done | bytes 32800 | tf_op jit(solution)/shard_map/ppermute | solution.py:540
  20.3 0.1 collective-permute-start.6
  20.4 1.2 %collective-permute-done.6.refs_1_ = bf16[16,1024]{1,0:T(8,128)(2,1)S(1)} collective-permute-done((bf16[16,1024]{1,0:T(8,128)(2,1)S(1)}, bf16[16,1024]{1,0:T(8,128)(2,1)S(1)}, u32[]{:S(2)}, u32[]{:S(2)}) %collective-permute-start.6) | collective-permute-done | bytes 32800 | tf_op jit(solution)/shard_map/ppermute | solution.py:540
  21.6 1.4 %collective-permute-start.8 = (bf16[16,1024]{1,0:T(8,128)(2,1)S(1)}, bf16[16,1024]{1,0:T(8,128)(2,1)S(1)}, u32[]{:S(2)}, u32[]{:S(2)}) collective-permute-start(bf16[16,1024]{1,0:T(8,128)(2,1)S(1)} %shard_map.81.mine_ref), channel_id=1, source_target_pairs={{0,8},{1,9},{2,10},{3,11},{4,7},{5,6},{6,5},{7,4},{8,0},{9,1},{10,... | collective-permute-start | bytes 98312 | tf_op jit(solution)/shard_map/ppermute | solution.py:553
  23.0 1.9 %collective-permute-start.7 = (bf16[16,1024]{1,0:T(8,128)(2,1)S(1)}, bf16[16,1024]{1,0:T(8,128)(2,1)S(1)}, u32[]{:S(2)}, u32[]{:S(2)}) collective-permute-start(bf16[16,1024]{1,0:T(8,128)(2,1)S(1)} %shard_map.81.mine_ref), channel_id=1, source_target_pairs={{0,1},{1,0},{2,3},{3,2},{4,6},{5,7},{6,4},{7,5},{8,9},{9,8},{10,11... | collective-permute-start | bytes 98312 | tf_op jit(solution)/shard_map/ppermute | solution.py:553
  24.8 0.8 %collective-permute-done.8.second_ref = bf16[16,1024]{1,0:T(8,128)(2,1)S(1)} collective-permute-done((bf16[16,1024]{1,0:T(8,128)(2,1)S(1)}, bf16[16,1024]{1,0:T(8,128)(2,1)S(1)}, u32[]{:S(2)}, u32[]{:S(2)}) %collective-permute-start.8) | collective-permute-done | bytes 32800 | tf_op jit(solution)/shard_map/ppermute | solution.py:553
  25.6 1.3 %collective-permute-done.7.first_ref = bf16[16,1024]{1,0:T(8,128)(2,1)S(1)} collective-permute-done((bf16[16,1024]{1,0:T(8,128)(2,1)S(1)}, bf16[16,1024]{1,0:T(8,128)(2,1)S(1)}, u32[]{:S(2)}, u32[]{:S(2)}) %collective-permute-start.7) | collective-permute-done | bytes 32800 | tf_op jit(solution)/shard_map/ppermute | solution.py:553
  26.9 1.1 %collective-permute-start.9 = (f32[16,1024]{1,0:T(8,128)S(1)}, f32[16,1024]{1,0:T(8,128)S(1)}, u32[]{:S(2)}, u32[]{:S(2)}) collective-permute-start(f32[16,1024]{1,0:T(8,128)S(1)} %shard_map.82.refs_0_), channel_id=1, source_target_pairs={{0,4},{4,0},{1,5},{5,1},{2,6},{6,2},{3,7},{7,3},{8,12},{12,8},{9,1... | collective-permute-start | bytes 196616 | tf_op jit(solution)/shard_map/ppermute | solution.py:540
  28.0 0.9 %collective-permute-done.9.refs_1_ = f32[16,1024]{1,0:T(8,128)S(1)} collective-permute-done((f32[16,1024]{1,0:T(8,128)S(1)}, f32[16,1024]{1,0:T(8,128)S(1)}, u32[]{:S(2)}, u32[]{:S(2)}) %collective-permute-start.9) | collective-permute-done | bytes 65568 | tf_op jit(solution)/shard_map/ppermute | solution.py:540
  28.9 0.8 %shard_map.83 = (f32[27,3,8]{2,1,0:T(4,128)}, f32[27,16,32]{2,1,0:T(8,128)}) custom-call(f32[16,1024]{1,0:T(8,128)S(1)} %shard_map.82.refs_0_, f32[16,1024]{1,0:T(8,128)S(1)} %collective-permute-done.9.refs_1_), custom_call_target="tpu_custom_call" | custom-call | bytes 1048576 | tf_op jit(solution)/shard_map/pallas_call | solution.py:524
  (3 shorter events, 0.0 us)
Async XLA Ops:
  1.8 1.4 %collective-permute-start = (bf16[128,128]{1,0:T(8,128)(2,1)S(1)}, bf16[128,128]{1,0:T(8,128)(2,1)S(1)}, u32[]{:S(2)}, u32[]{:S(2)}) collective-permute-start(bf16[128,128]{1,0:T(8,128)(2,1)S(1)} %get-tuple-element.35), channel_id=1, source_target_pairs={{0,4},{4,0},{8,12},{12,8},{16,20},{20,16},{24,28},{28,24},{1,5},{5... | collective-permute-start | bytes 98312 | tf_op jit(solution)/shard_map/ppermute | solution.py:579
  3.5 6.9 %collective-permute-start.1 = (bf16[80,128]{1,0:T(8,128)(2,1)S(1)}, bf16[80,128]{1,0:T(8,128)(2,1)S(1)}, u32[]{:S(2)}, u32[]{:S(2)}) collective-permute-start(bf16[80,128]{1,0:T(8,128)(2,1)S(1)} %get-tuple-element.52), channel_id=1, source_target_pairs={{0,1},{1,0},{2,3},{3,2},{8,9},{9,8},{10,11},{11,10},{16,17},{17,16... | collective-permute-start | bytes 61448 | tf_op jit(solution)/shard_map/ppermute | solution.py:593
  6.5 4.0 %collective-permute-start.2 = (bf16[80,128]{1,0:T(8,128)(2,1)S(1)}, bf16[80,128]{1,0:T(8,128)(2,1)S(1)}, u32[]{:S(2)}, u32[]{:S(2)}) collective-permute-start(bf16[80,128]{1,0:T(8,128)(2,1)S(1)} %get-tuple-element.53), channel_id=1, source_target_pairs={{0,8},{1,2},{2,1},{3,11},{8,0},{9,10},{10,9},{11,3},{16,24},{17,18... | collective-permute-start | bytes 61448 | tf_op jit(solution)/shard_map/ppermute | solution.py:593
  13.3 4.9 %collective-permute-start.3 = (bf16[16,1024]{1,0:T(8,128)(2,1)S(1)}, bf16[16,1024]{1,0:T(8,128)(2,1)S(1)}, u32[]{:S(2)}, u32[]{:S(2)}) collective-permute-start(bf16[16,1024]{1,0:T(8,128)(2,1)S(1)} %get-tuple-element.56), channel_id=1, source_target_pairs={{0,24},{8,16},{16,8},{24,0},{1,25},{9,17},{17,9},{25,1},{2,26},{10... | collective-permute-start | bytes 98312 | tf_op jit(solution)/shard_map/ppermute | solution.py:540
  15.7 3.9 %collective-permute-start.4 = (bf16[16,1024]{1,0:T(8,128)(2,1)S(1)}, bf16[16,1024]{1,0:T(8,128)(2,1)S(1)}, u32[]{:S(2)}, u32[]{:S(2)}) collective-permute-start(bf16[16,1024]{1,0:T(8,128)(2,1)S(1)} %get-tuple-element.57), channel_id=1, source_target_pairs={{0,8},{8,0},{16,24},{24,16},{1,9},{9,1},{17,25},{25,17},{2,10},{10... | collective-permute-start | bytes 98312 | tf_op jit(solution)/shard_map/ppermute | solution.py:540
  16.4 3.9 %collective-permute-start.5 = (bf16[16,1024]{1,0:T(8,128)(2,1)S(1)}, bf16[16,1024]{1,0:T(8,128)(2,1)S(1)}, u32[]{:S(2)}, u32[]{:S(2)}) collective-permute-start(bf16[16,1024]{1,0:T(8,128)(2,1)S(1)} %get-tuple-element.58), channel_id=1, source_target_pairs={{0,16},{8,24},{16,0},{24,8},{1,17},{9,25},{17,1},{25,9},{2,18},{10... | collective-permute-start | bytes 98312 | tf_op jit(solution)/shard_map/ppermute | solution.py:540
  20.3 1.3 %collective-permute-start.6 = (bf16[16,1024]{1,0:T(8,128)(2,1)S(1)}, bf16[16,1024]{1,0:T(8,128)(2,1)S(1)}, u32[]{:S(2)}, u32[]{:S(2)}) collective-permute-start(bf16[16,1024]{1,0:T(8,128)(2,1)S(1)} %shard_map.80.refs_0_), channel_id=1, source_target_pairs={{0,4},{4,0},{1,5},{5,1},{2,6},{6,2},{3,7},{7,3},{8,12},{12,8},{9,1... | collective-permute-start | bytes 98312 | tf_op jit(solution)/shard_map/ppermute | solution.py:540
  21.6 4.0 %collective-permute-start.8 = (bf16[16,1024]{1,0:T(8,128)(2,1)S(1)}, bf16[16,1024]{1,0:T(8,128)(2,1)S(1)}, u32[]{:S(2)}, u32[]{:S(2)}) collective-permute-start(bf16[16,1024]{1,0:T(8,128)(2,1)S(1)} %shard_map.81.mine_ref), channel_id=1, source_target_pairs={{0,8},{1,9},{2,10},{3,11},{4,7},{5,6},{6,5},{7,4},{8,0},{9,1},{10,... | collective-permute-start | bytes 98312 | tf_op jit(solution)/shard_map/ppermute | solution.py:553
  23.0 4.0 %collective-permute-start.7 = (bf16[16,1024]{1,0:T(8,128)(2,1)S(1)}, bf16[16,1024]{1,0:T(8,128)(2,1)S(1)}, u32[]{:S(2)}, u32[]{:S(2)}) collective-permute-start(bf16[16,1024]{1,0:T(8,128)(2,1)S(1)} %shard_map.81.mine_ref), channel_id=1, source_target_pairs={{0,1},{1,0},{2,3},{3,2},{4,6},{5,7},{6,4},{7,5},{8,9},{9,8},{10,11... | collective-permute-start | bytes 98312 | tf_op jit(solution)/shard_map/ppermute | solution.py:553
  26.9 2.0 %collective-permute-start.9 = (f32[16,1024]{1,0:T(8,128)S(1)}, f32[16,1024]{1,0:T(8,128)S(1)}, u32[]{:S(2)}, u32[]{:S(2)}) collective-permute-start(f32[16,1024]{1,0:T(8,128)S(1)} %shard_map.82.refs_0_), channel_id=1, source_target_pairs={{0,4},{4,0},{1,5},{5,1},{2,6},{6,2},{3,7},{7,3},{8,12},{12,8},{9,1... | collective-permute-start | bytes 196616 | tf_op jit(solution)/shard_map/ppermute | solution.py:540

commit v3 on v2

--- a/solution.py
+++ b/solution.py
@@ -292,7 +292,10 @@
         delta.append(jnp.concatenate(both, axis=1).astype(BF))
         short = [short_act[b, p] if p >= 0 else jnp.zeros((112, 128), BF) for b, p in planes]
         patches.append(jnp.concatenate(short, axis=1))
-    grad_ref[...] = dot(jnp.concatenate(delta, axis=0), jnp.concatenate(patches, axis=0), ((0,), (0,)))
+    delta, patches = jnp.concatenate(delta, axis=0), jnp.concatenate(patches, axis=0)
+    for first in range(0, 1152, 256):
+        last = min(first + 256, 1152)
+        grad_ref[:, first:last] = dot(delta, patches[:, first:last], ((0,), (0,)))[0:192]
 
 
 def main_kernel(
@@ -409,12 +412,16 @@
                 else:
                     short.append(jnp.concatenate([outer_short[b, p], short_act[b, p, 0:16, :]], axis=0))
         patches.append(jnp.concatenate(short, axis=1))
-    grad = grad_in[...] + dot(jnp.concatenate(delta, axis=0), jnp.concatenate(patches, axis=0), ((0,), (0,)))
+    delta, patches = jnp.concatenate(delta, axis=0), jnp.concatenate(patches, axis=0)
 
     place = iota((64, 128), 1) >> 5
     turned = []
     for ab in range(9):
-        a0, a1, a2 = (grad[64 * j : 64 * j + 64, 128 * ab : 128 * ab + 128] for j in range(3))
+        if ab % 2 == 0:
+            first, last = 128 * ab, min(128 * ab + 256, 1152)
+            grad = dot(delta, patches[:, first:last], ((0,), (0,)))[0:192] + grad_in[:, first:last]
+        column = 128 * (ab % 2)
+        a0, a1, a2 = (grad[64 * j : 64 * j + 64, column : column + 128] for j in range(3))
         r0, r1, r2 = (pltpu.roll(a, 64, 1) for a in (a0, a1, a2))
         joined = jnp.where(place == 0, a0 + r1, jnp.where(place == 1, a1 + r2, a1 + r0))
         shift = (3 * ab - 1) % 4
@@ -456,14 +463,18 @@
         level_ref[p] = jnp.concatenate([rows_out[m] for m in range(16)], axis=1).astype(BF)
         copies.append(pltpu.make_async_copy(level_ref.at[p], level_hbm.at[p], sems.at[2 + p]))
         copies[-1].start()
-    grad = dot(jnp.concatenate(lhs_rows, axis=0), jnp.concatenate(rhs_rows, axis=0), ((0,), (0,)))
+    delta_one = jnp.concatenate(lhs_rows, axis=0).T
+    windows = jnp.concatenate(rhs_rows, axis=0)
 
     place = iota((32, 128), 1)
     found = jnp.zeros((32, 128), F32)
     for tap in range(9):
+        if tap % 2 == 0:
+            grad = dot(delta_one, windows[:, 128 * tap : min(128 * tap + 256, 1152)])
+        column = 128 * (tap % 2)
         some = jnp.zeros((32, 128), F32)
         for t in range(8):
-            piece = grad[32 * t : 32 * t + 32, 128 * tap : 128 * tap + 128]
+            piece = grad[32 * t : 32 * t + 32, column : column + 128]
             shift = (3 * tap - 2 * t) % 128
             some = some + (pltpu.roll(piece, shift, 1) if shift else piece)
         local = place & 31
@@ -603,7 +614,7 @@
             shape((2, 8, 1664), BF),
             shape((2, 104, 128), F32),
             shape((2, 104, 128), F32),
-            shape((256, 1152), F32),
+            shape((192, 1152), F32),
         ],
         (split, w_one, w_two, cot, *got_x),
         [pltpu.VMEM((5, 8, 112, 128), BF), pltpu.VMEM((3, 4, 224, 128), BF)],

time: 29.9 us -> 29.9 us (level)
  no operation moved by 1% of the time
where the time goes in v3:
time: 29.9 us; the launch traced here: 29.8 us
  starting transfers between devices  12.9 us (43%)
  Pallas kernels  8.35 us (28%)
  waiting for transfers between devices  7.76 us (26%)
  between operations  0.71 us (2%)
    pallas_call x9, Pallas kernels, call(): pl.pallas_call(kernel, out_shape=outs, in_specs=[pl.BlockSpec(memory_spac...  8.35 us
    ppermute x5, waiting for transfers between devices, exchange(): lax.ppermute(value, axis, [(i, i ^ step) for i in range(lax.axis_size(axi...  5.5 us
    ppermute x5, starting transfers between devices, exchange(): lax.ppermute(value, axis, [(i, i ^ step) for i in range(lax.axis_size(axi...  4.72 us
    ppermute x2, starting transfers between devices, body(): lax.ppermute(edge, ('dp', 'gy'), pairs)  4.47 us
    ppermute x2, starting transfers between devices, trade_shared(): return lax.ppermute(value, ('dp', 'gx', 'gy'), pairs)  3.22 us
    ppermute x2, waiting for transfers between devices, trade_shared(): return lax.ppermute(value, ('dp', 'gx', 'gy'), pairs)  2.1 us
  transfers between devices with their start and end apart: 10, of which 8 were waited for; matrix products, arithmetic and copies ran while one was open for 0% of the time, Pallas kernels for 11%

profile of v3, /device:TPU:0, one launch (start us, length us, event | category | flops | bytes accessed | tf_op | source)
XLA Modules:
  0.0 29.8 jit_solution(3996636710441474232)
XLA Ops:
  0.6 1.1 %shard_map.75 = (bf16[24,32,128]{2,1,0:T(8,128)(2,1)S(1)}, bf16[2,8,2048]{2,1,0:T(8,128)(2,1)S(1)}, bf16[27,3,32]{2,1,0:T(4,128)(2,1)S(1)}, bf16[864,64]{1,0:T(8,128)(2,1)S(1)}, bf16[128,128]{1,0:T(8,128)(2,1)S(1)}) custom-call(bf16[24,32,128]{2,1,0:T(8,128)(2,1)} %bitcast.11, bf16[2,8,2048]{2,1,0:T(8,128)(2,1)} %bitcast.12, bf16[27,3,32]{2,1,0:T(4,128)(2,1)} %bitcast.13, ...), custom_call_target="tpu_custom_call" | custom-call | bytes 1048576 | tf_op jit(solution)/shard_map/pallas_call | solution.py:535
  1.8 0.5 %collective-permute-start = (bf16[128,128]{1,0:T(8,128)(2,1)S(1)}, bf16[128,128]{1,0:T(8,128)(2,1)S(1)}, u32[]{:S(2)}, u32[]{:S(2)}) collective-permute-start(bf16[128,128]{1,0:T(8,128)(2,1)S(1)} %get-tuple-element.35), channel_id=1, source_target_pairs={{0,4},{4,0},{8,12},{12,8},{16,20},{20,16},{24,28},{28,24},{1,5},{5... | collective-permute-start | bytes 98312 | tf_op jit(solution)/shard_map/ppermute | solution.py:590
  2.3 0.7 %shard_map.77 = (bf16[1152,256]{1,0:T(8,128)(2,1)S(1)}, bf16[1152,256]{1,0:T(8,128)(2,1)S(1)}, bf16[256,2048]{1,0:T(8,128)(2,1)S(1)}) custom-call(bf16[27,3,32]{2,1,0:T(4,128)(2,1)S(1)} %get-tuple-element.37.one_ref, bf16[864,64]{1,0:T(8,128)(2,1)S(1)} %get-tuple-element.38.two_ref), custom_call_target="tpu_custom_call" | custom-call | flops 1073741824 | bytes 1048576 | tf_op jit(solution)/shard_map/pallas_call | solution.py:535
  3.0 0.2 collective-permute-done.refs_2_.refs_4_
  3.2 0.4 %shard_map.76 = (bf16[5,384,128]{2,1,0:T(8,128)(2,1)S(1)}, bf16[80,128]{1,0:T(8,128)(2,1)S(1)}, bf16[80,128]{1,0:T(8,128)(2,1)S(1)}) custom-call(bf16[24,32,128]{2,1,0:T(8,128)(2,1)S(1)} %get-tuple-element.33.refs_0_, bf16[2,8,2048]{2,1,0:T(8,128)(2,1)S(1)} %get-tuple-element.34.refs_1_.refs_3_, bf16[128,128]{1,0:T(8,128)(2,1)S(1)} %collective-permute-done.refs_2_.refs_4_), custom_call_target="tpu_custom_call" | custom-call | bytes 1048576 | tf_op jit(solution)/shard_map/pallas_call | solution.py:535
  3.5 3.0 %collective-permute-start.1 = (bf16[80,128]{1,0:T(8,128)(2,1)S(1)}, bf16[80,128]{1,0:T(8,128)(2,1)S(1)}, u32[]{:S(2)}, u32[]{:S(2)}) collective-permute-start(bf16[80,128]{1,0:T(8,128)(2,1)S(1)} %get-tuple-element.52), channel_id=1, source_target_pairs={{0,1},{1,0},{2,3},{3,2},{8,9},{9,8},{10,11},{11,10},{16,17},{17,16... | collective-permute-start | bytes 61448 | tf_op jit(solution)/shard_map/ppermute | solution.py:604
  6.5 1.5 %collective-permute-start.2 = (bf16[80,128]{1,0:T(8,128)(2,1)S(1)}, bf16[80,128]{1,0:T(8,128)(2,1)S(1)}, u32[]{:S(2)}, u32[]{:S(2)}) collective-permute-start(bf16[80,128]{1,0:T(8,128)(2,1)S(1)} %get-tuple-element.53), channel_id=1, source_target_pairs={{0,8},{1,2},{2,1},{3,11},{8,0},{9,10},{10,9},{11,3},{16,24},{17,18... | collective-permute-start | bytes 61448 | tf_op jit(solution)/shard_map/ppermute | solution.py:604
  8.0 2.5 %shard_map.78 = (bf16[5,8,64,128]{3,2,1,0:T(8,128)(2,1)S(1)}, bf16[5,128,256]{2,1,0:T(8,128)(2,1)S(1)}, bf16[3,4,112,128]{3,2,1,0:T(8,128)(2,1)S(1)}, f32[4,2,11...) custom-call(bf16[5,384,128]{2,1,0:T(8,128)(2,1)S(1)} %get-tuple-elem, ...), custom_call_target="tpu_custom_call" | custom-call | flops 2147483648 | bytes 1048576 | tf_op jit(solution)/shard_map/pallas_call | solution.py:535
  10.5 0.0 collective-permute-done.1.refs_13_
  10.5 0.0 collective-permute-done.2.refs_14_
  10.5 2.8 %shard_map.79 = (bf16[2,8,2048]{2,1,0:T(8,128)(2,1)}, bf16[4,16,2048]{2,1,0:T(8,128)(2,1)}, bf16[16,1024]{1,0:T(8,128)(2,1)S(1)}, bf16[16,1024]{1,0:T(8,128)(2,1...) custom-call(bf16[5,8,64,128]{3,2,1,0:T(8,128)(2,1)S(1)} %get-tuple-element.41.refs_0_, ...), custom_call_target="tpu_custom_call" | custom-call | bytes 1048576 | tf_op jit(solution)/shard_map/pallas_call | solution.py:535
  13.3 2.3 %collective-permute-start.3 = (bf16[16,1024]{1,0:T(8,128)(2,1)S(1)}, bf16[16,1024]{1,0:T(8,128)(2,1)S(1)}, u32[]{:S(2)}, u32[]{:S(2)}) collective-permute-start(bf16[16,1024]{1,0:T(8,128)(2,1)S(1)} %get-tuple-element.56), channel_id=1, source_target_pairs={{0,24},{8,16},{16,8},{24,0},{1,25},{9,17},{17,9},{25,1},{2,26},{10... | collective-permute-start | bytes 98312 | tf_op jit(solution)/shard_map/ppermute | solution.py:551
  15.7 0.7 %collective-permute-start.4 = (bf16[16,1024]{1,0:T(8,128)(2,1)S(1)}, bf16[16,1024]{1,0:T(8,128)(2,1)S(1)}, u32[]{:S(2)}, u32[]{:S(2)}) collective-permute-start(bf16[16,1024]{1,0:T(8,128)(2,1)S(1)} %get-tuple-element.57), channel_id=1, source_target_pairs={{0,8},{8,0},{16,24},{24,16},{1,9},{9,1},{17,25},{25,17},{2,10},{10... | collective-permute-start | bytes 98312 | tf_op jit(solution)/shard_map/ppermute | solution.py:551
  16.4 0.5 %collective-permute-start.5 = (bf16[16,1024]{1,0:T(8,128)(2,1)S(1)}, bf16[16,1024]{1,0:T(8,128)(2,1)S(1)}, u32[]{:S(2)}, u32[]{:S(2)}) collective-permute-start(bf16[16,1024]{1,0:T(8,128)(2,1)S(1)} %get-tuple-element.58), channel_id=1, source_target_pairs={{0,16},{8,24},{16,0},{24,8},{1,17},{9,25},{17,1},{25,9},{2,18},{10... | collective-permute-start | bytes 98312 | tf_op jit(solution)/shard_map/ppermute | solution.py:551
  16.9 1.3 %collective-permute-done.3.refs_0_ = bf16[16,1024]{1,0:T(8,128)(2,1)S(1)} collective-permute-done((bf16[16,1024]{1,0:T(8,128)(2,1)S(1)}, bf16[16,1024]{1,0:T(8,128)(2,1)S(1)}, u32[]{:S(2)}, u32[]{:S(2)}) %collective-permute-start.3) | collective-permute-done | bytes 32800 | tf_op jit(solution)/shard_map/ppermute | solution.py:551
  18.2 1.3 %collective-permute-done.4.refs_1_ = bf16[16,1024]{1,0:T(8,128)(2,1)S(1)} collective-permute-done((bf16[16,1024]{1,0:T(8,128)(2,1)S(1)}, bf16[16,1024]{1,0:T(8,128)(2,1)S(1)}, u32[]{:S(2)}, u32[]{:S(2)}) %collective-permute-start.4) | collective-permute-done | bytes 32800 | tf_op jit(solution)/shard_map/ppermute | solution.py:551
  19.6 0.7 %collective-permute-done.5.refs_2_ = bf16[16,1024]{1,0:T(8,128)(2,1)S(1)} collective-permute-done((bf16[16,1024]{1,0:T(8,128)(2,1)S(1)}, bf16[16,1024]{1,0:T(8,128)(2,1)S(1)}, u32[]{:S(2)}, u32[]{:S(2)}) %collective-permute-start.5) | collective-permute-done | bytes 32800 | tf_op jit(solution)/shard_map/ppermute | solution.py:551
  20.3 0.1 collective-permute-start.6
  20.4 1.2 %collective-permute-done.6.refs_1_ = bf16[16,1024]{1,0:T(8,128)(2,1)S(1)} collective-permute-done((bf16[16,1024]{1,0:T(8,128)(2,1)S(1)}, bf16[16,1024]{1,0:T(8,128)(2,1)S(1)}, u32[]{:S(2)}, u32[]{:S(2)}) %collective-permute-start.6) | collective-permute-done | bytes 32800 | tf_op jit(solution)/shard_map/ppermute | solution.py:551
  21.6 1.4 %collective-permute-start.8 = (bf16[16,1024]{1,0:T(8,128)(2,1)S(1)}, bf16[16,1024]{1,0:T(8,128)(2,1)S(1)}, u32[]{:S(2)}, u32[]{:S(2)}) collective-permute-start(bf16[16,1024]{1,0:T(8,128)(2,1)S(1)} %shard_map.81.mine_ref), channel_id=1, source_target_pairs={{0,8},{1,9},{2,10},{3,11},{4,7},{5,6},{6,5},{7,4},{8,0},{9,1},{10,... | collective-permute-start | bytes 98312 | tf_op jit(solution)/shard_map/ppermute | solution.py:564
  23.0 1.9 %collective-permute-start.7 = (bf16[16,1024]{1,0:T(8,128)(2,1)S(1)}, bf16[16,1024]{1,0:T(8,128)(2,1)S(1)}, u32[]{:S(2)}, u32[]{:S(2)}) collective-permute-start(bf16[16,1024]{1,0:T(8,128)(2,1)S(1)} %shard_map.81.mine_ref), channel_id=1, source_target_pairs={{0,1},{1,0},{2,3},{3,2},{4,6},{5,7},{6,4},{7,5},{8,9},{9,8},{10,11... | collective-permute-start | bytes 98312 | tf_op jit(solution)/shard_map/ppermute | solution.py:564
  24.8 0.8 %collective-permute-done.8.second_ref = bf16[16,1024]{1,0:T(8,128)(2,1)S(1)} collective-permute-done((bf16[16,1024]{1,0:T(8,128)(2,1)S(1)}, bf16[16,1024]{1,0:T(8,128)(2,1)S(1)}, u32[]{:S(2)}, u32[]{:S(2)}) %collective-permute-start.8) | collective-permute-done | bytes 32800 | tf_op jit(solution)/shard_map/ppermute | solution.py:564
  25.6 1.3 %collective-permute-done.7.first_ref = bf16[16,1024]{1,0:T(8,128)(2,1)S(1)} collective-permute-done((bf16[16,1024]{1,0:T(8,128)(2,1)S(1)}, bf16[16,1024]{1,0:T(8,128)(2,1)S(1)}, u32[]{:S(2)}, u32[]{:S(2)}) %collective-permute-start.7) | collective-permute-done | bytes 32800 | tf_op jit(solution)/shard_map/ppermute | solution.py:564
  26.9 1.1 %collective-permute-start.9 = (f32[16,1024]{1,0:T(8,128)S(1)}, f32[16,1024]{1,0:T(8,128)S(1)}, u32[]{:S(2)}, u32[]{:S(2)}) collective-permute-start(f32[16,1024]{1,0:T(8,128)S(1)} %shard_map.82.refs_0_), channel_id=1, source_target_pairs={{0,4},{4,0},{1,5},{5,1},{2,6},{6,2},{3,7},{7,3},{8,12},{12,8},{9,1... | collective-permute-start | bytes 196616 | tf_op jit(solution)/shard_map/ppermute | solution.py:551
  28.0 0.9 %collective-permute-done.9.refs_1_ = f32[16,1024]{1,0:T(8,128)S(1)} collective-permute-done((f32[16,1024]{1,0:T(8,128)S(1)}, f32[16,1024]{1,0:T(8,128)S(1)}, u32[]{:S(2)}, u32[]{:S(2)}) %collective-permute-start.9) | collective-permute-done | bytes 65568 | tf_op jit(solution)/shard_map/ppermute | solution.py:551
  28.9 0.8 %shard_map.83 = (f32[27,3,8]{2,1,0:T(4,128)}, f32[27,16,32]{2,1,0:T(8,128)}) custom-call(f32[16,1024]{1,0:T(8,128)S(1)} %shard_map.82.refs_0_, f32[16,1024]{1,0:T(8,128)S(1)} %collective-permute-done.9.refs_1_), custom_call_target="tpu_custom_call" | custom-call | bytes 1048576 | tf_op jit(solution)/shard_map/pallas_call | solution.py:535
  (3 shorter events, 0.0 us)
Async XLA Ops:
  1.8 1.4 %collective-permute-start = (bf16[128,128]{1,0:T(8,128)(2,1)S(1)}, bf16[128,128]{1,0:T(8,128)(2,1)S(1)}, u32[]{:S(2)}, u32[]{:S(2)}) collective-permute-start(bf16[128,128]{1,0:T(8,128)(2,1)S(1)} %get-tuple-element.35), channel_id=1, source_target_pairs={{0,4},{4,0},{8,12},{12,8},{16,20},{20,16},{24,28},{28,24},{1,5},{5... | collective-permute-start | bytes 98312 | tf_op jit(solution)/shard_map/ppermute | solution.py:590
  3.5 6.9 %collective-permute-start.1 = (bf16[80,128]{1,0:T(8,128)(2,1)S(1)}, bf16[80,128]{1,0:T(8,128)(2,1)S(1)}, u32[]{:S(2)}, u32[]{:S(2)}) collective-permute-start(bf16[80,128]{1,0:T(8,128)(2,1)S(1)} %get-tuple-element.52), channel_id=1, source_target_pairs={{0,1},{1,0},{2,3},{3,2},{8,9},{9,8},{10,11},{11,10},{16,17},{17,16... | collective-permute-start | bytes 61448 | tf_op jit(solution)/shard_map/ppermute | solution.py:604
  6.5 4.0 %collective-permute-start.2 = (bf16[80,128]{1,0:T(8,128)(2,1)S(1)}, bf16[80,128]{1,0:T(8,128)(2,1)S(1)}, u32[]{:S(2)}, u32[]{:S(2)}) collective-permute-start(bf16[80,128]{1,0:T(8,128)(2,1)S(1)} %get-tuple-element.53), channel_id=1, source_target_pairs={{0,8},{1,2},{2,1},{3,11},{8,0},{9,10},{10,9},{11,3},{16,24},{17,18... | collective-permute-start | bytes 61448 | tf_op jit(solution)/shard_map/ppermute | solution.py:604
  13.3 4.9 %collective-permute-start.3 = (bf16[16,1024]{1,0:T(8,128)(2,1)S(1)}, bf16[16,1024]{1,0:T(8,128)(2,1)S(1)}, u32[]{:S(2)}, u32[]{:S(2)}) collective-permute-start(bf16[16,1024]{1,0:T(8,128)(2,1)S(1)} %get-tuple-element.56), channel_id=1, source_target_pairs={{0,24},{8,16},{16,8},{24,0},{1,25},{9,17},{17,9},{25,1},{2,26},{10... | collective-permute-start | bytes 98312 | tf_op jit(solution)/shard_map/ppermute | solution.py:551
  15.7 3.9 %collective-permute-start.4 = (bf16[16,1024]{1,0:T(8,128)(2,1)S(1)}, bf16[16,1024]{1,0:T(8,128)(2,1)S(1)}, u32[]{:S(2)}, u32[]{:S(2)}) collective-permute-start(bf16[16,1024]{1,0:T(8,128)(2,1)S(1)} %get-tuple-element.57), channel_id=1, source_target_pairs={{0,8},{8,0},{16,24},{24,16},{1,9},{9,1},{17,25},{25,17},{2,10},{10... | collective-permute-start | bytes 98312 | tf_op jit(solution)/shard_map/ppermute | solution.py:551
  16.4 3.9 %collective-permute-start.5 = (bf16[16,1024]{1,0:T(8,128)(2,1)S(1)}, bf16[16,1024]{1,0:T(8,128)(2,1)S(1)}, u32[]{:S(2)}, u32[]{:S(2)}) collective-permute-start(bf16[16,1024]{1,0:T(8,128)(2,1)S(1)} %get-tuple-element.58), channel_id=1, source_target_pairs={{0,16},{8,24},{16,0},{24,8},{1,17},{9,25},{17,1},{25,9},{2,18},{10... | collective-permute-start | bytes 98312 | tf_op jit(solution)/shard_map/ppermute | solution.py:551
  20.3 1.3 %collective-permute-start.6 = (bf16[16,1024]{1,0:T(8,128)(2,1)S(1)}, bf16[16,1024]{1,0:T(8,128)(2,1)S(1)}, u32[]{:S(2)}, u32[]{:S(2)}) collective-permute-start(bf16[16,1024]{1,0:T(8,128)(2,1)S(1)} %shard_map.80.refs_0_), channel_id=1, source_target_pairs={{0,4},{4,0},{1,5},{5,1},{2,6},{6,2},{3,7},{7,3},{8,12},{12,8},{9,1... | collective-permute-start | bytes 98312 | tf_op jit(solution)/shard_map/ppermute | solution.py:551
  21.6 4.0 %collective-permute-start.8 = (bf16[16,1024]{1,0:T(8,128)(2,1)S(1)}, bf16[16,1024]{1,0:T(8,128)(2,1)S(1)}, u32[]{:S(2)}, u32[]{:S(2)}) collective-permute-start(bf16[16,1024]{1,0:T(8,128)(2,1)S(1)} %shard_map.81.mine_ref), channel_id=1, source_target_pairs={{0,8},{1,9},{2,10},{3,11},{4,7},{5,6},{6,5},{7,4},{8,0},{9,1},{10,... | collective-permute-start | bytes 98312 | tf_op jit(solution)/shard_map/ppermute | solution.py:564
  23.0 4.0 %collective-permute-start.7 = (bf16[16,1024]{1,0:T(8,128)(2,1)S(1)}, bf16[16,1024]{1,0:T(8,128)(2,1)S(1)}, u32[]{:S(2)}, u32[]{:S(2)}) collective-permute-start(bf16[16,1024]{1,0:T(8,128)(2,1)S(1)} %shard_map.81.mine_ref), channel_id=1, source_target_pairs={{0,1},{1,0},{2,3},{3,2},{4,6},{5,7},{6,4},{7,5},{8,9},{9,8},{10,11... | collective-permute-start | bytes 98312 | tf_op jit(solution)/shard_map/ppermute | solution.py:564
  26.9 2.0 %collective-permute-start.9 = (f32[16,1024]{1,0:T(8,128)S(1)}, f32[16,1024]{1,0:T(8,128)S(1)}, u32[]{:S(2)}, u32[]{:S(2)}) collective-permute-start(f32[16,1024]{1,0:T(8,128)S(1)} %shard_map.82.refs_0_), channel_id=1, source_target_pairs={{0,4},{4,0},{1,5},{5,1},{2,6},{6,2},{3,7},{7,3},{8,12},{12,8},{9,1... | collective-permute-start | bytes 196616 | tf_op jit(solution)/shard_map/ppermute | solution.py:551

commit v4 on v3

--- a/solution.py
+++ b/solution.py
@@ -318,7 +318,8 @@
 ):
     gy_refs, refs = refs[:count_y], refs[count_y:]
     feat_hbm, level_hbm, refs = refs[0], refs[1], refs[2:]
-    dealt, refs = refs[:ranks], refs[ranks:]
+    parts = 2 if ranks == 4 else ranks
+    dealt, refs = refs[:parts], refs[parts:]
     edges, short_edges, outer_act, outer_short, outer_slope, rows_out, total, feat_ref, level_ref, sems = refs
     place_y = position("gy")
     copies = []
@@ -484,15 +485,24 @@
     for d in range(ranks):
         total[tall * d : tall * d + short, 896:1024] = found[short * d : short * d + short]
     rank = lax.axis_index("dp")
-    for step, out in enumerate(dealt):
+    picked = []
+    for step in range(ranks):
         if tall % 8 == 0:
             start = pl.multiple_of((rank ^ step) * tall, tall)
-            picked = total[pl.ds(start, tall), :]
+            picked.append(total[pl.ds(start, tall), :])
         else:
-            picked = total[0:tall, :]
+            value = total[0:tall, :]
             for d in range(1, ranks):
-                picked = jnp.where((rank ^ step) == d, total[d * tall : d * tall + tall, :], picked)
-        out[...] = picked.astype(BF)
+                value = jnp.where((rank ^ step) == d, total[d * tall : d * tall + tall, :], value)
+            picked.append(value)
+    if ranks == 4:
+        odd = position("gx")[0]
+        near, far = jnp.concatenate(picked[:2], axis=0), jnp.concatenate(picked[2:], axis=0)
+        dealt[0][...] = jnp.where(odd, far, near).astype(BF)
+        dealt[1][...] = jnp.where(odd, near, far).astype(BF)
+    else:
+        for out, value in zip(dealt, picked):
+            out[...] = value.astype(BF)
     for copy in copies:
         copy.wait()
 
@@ -505,10 +515,20 @@
     out_ref[...] = values[0].astype(out_ref.dtype)
 
 
+def part_kernel(mine_ref, got_ref, own_ref, first_ref, second_ref):
+    value = mine_ref[...].astype(F32) + got_ref[...].astype(F32)
+    tall = value.shape[0] // 2
+    upper, lower = value[:tall].astype(BF), value[tall:].astype(BF)
+    own_ref[...] = upper
+    first_ref[...] = jnp.where(position("gx")[0], upper, lower)
+    second_ref[...] = lower
+
+
 def share_kernel(mine_ref, first_ref, second_ref, out_ref):
     first = first_ref[...].astype(F32)
     odd = position("gx")[0]
-    out_ref[...] = first + jnp.where(odd, second_ref[...], mine_ref[...]).astype(F32)
+    value = first + jnp.where(odd, second_ref[...].astype(F32), mine_ref[...].astype(F32))
+    out_ref[...] = value.astype(out_ref.dtype)
 
 
 def last_kernel(scale_one, scale_two, *refs):
@@ -562,6 +582,16 @@
                     to_d = (d ^ 1) % ranks
                 pairs.append(((d * columns + g) * count + i, (to_d * columns + g) * count + to_i))
     return lax.ppermute(value, ("dp", "gx", "gy"), pairs)
+
+
+def trade_ranks(value, even_step, odd_step):
+    ranks, columns = lax.axis_size("dp"), lax.axis_size("gx")
+    pairs = [
+        (d * columns + g, (d ^ (odd_step if g % 2 else even_step)) * columns + g)
+        for d in range(ranks)
+        for g in range(columns)
+    ]
+    return lax.ppermute(value, ("dp", "gx"), pairs)
 
 
 def body(magnetic, kernel_one, kernel_two, cotangent):
@@ -623,7 +653,8 @@
     tall = 64 // ranks
     features, level, *dealt = call(
         lambda *refs: main_kernel(ny, ranks, *refs),
-        [shape((2, 8, 2048), BF), shape((4, 16, 2048), BF)] + [shape((tall, 1024), BF)] * ranks,
+        [shape((2, 8, 2048), BF), shape((4, 16, 2048), BF)]
+        + ([shape((32, 1024), BF)] * 2 if ranks == 4 else [shape((tall, 1024), BF)] * ranks),
         (*first, picks, w_one, w_two, *got_y),
         [
             pltpu.VMEM((5, 8, 32, 128), BF),
@@ -639,8 +670,15 @@
         ],
         in_hbm=2,
     )
-    terms = [exchange(dealt[step], "dp", step) for step in (ranks - 1, *range(1, ranks - 1))] + dealt[:1]
-    mine, = call(sum_kernel, [shape((tall, 1024), BF)], terms)
+    if ranks == 4:
+        own, one_more, two_more = call(
+            part_kernel, [shape((tall, 1024), BF)] * 3, (dealt[0], exchange(dealt[1], "gx", 1))
+        )
+        terms = [own, trade_ranks(one_more, 1, 2), trade_ranks(two_more, 2, 3)]
+        mine, = call(share_kernel, [shape((tall, 1024), BF)], terms)
+    else:
+        terms = [exchange(dealt[step], "dp", step) for step in range(1, ranks)] + dealt[:1]
+        mine, = call(sum_kernel, [shape((tall, 1024), BF)], terms)
     step = 1
     while step < count_gx:
         mine, = call(sum_kernel, [shape((tall, 1024), BF)], (mine, exchange(mine, "gx", step)))

time: 29.9 us -> 30 us (level)
  waiting for transfers between devices: 7.76 us -> 8.31 us
  starting transfers between devices: 12.9 us -> 12.4 us
    ppermute x0 -> x2, starting transfers between devices: none -> 2.88 us  [trade_ranks(): return lax.ppermute(value, ('dp', 'gx'), pairs)]
    ppermute x0 -> x2, waiting for transfers between devices: none -> 2.75 us  [trade_ranks(): return lax.ppermute(value, ('dp', 'gx'), pairs)]
    ppermute x5 -> x3, starting transfers between devices: 4.72 us -> 2.16 us  [exchange(): lax.ppermute(value, axis, [(i, i ^ step) for i in range(lax.axis_size(axi...]
    ppermute x5 -> x3, waiting for transfers between devices: 5.5 us -> 3.34 us  [exchange(): lax.ppermute(value, axis, [(i, i ^ step) for i in range(lax.axis_size(axi...]
    ppermute x2, starting transfers between devices: 3.22 us -> 2.36 us  [trade_shared(): return lax.ppermute(value, ('dp', 'gx', 'gy'), pairs)]
    pallas_call x9 -> x10, Pallas kernels: 8.35 us -> 8.48 us  [call(): pl.pallas_call(kernel, out_shape=outs, in_specs=[pl.BlockSpec(memory_spac...]
where the time goes in v4:
time: 30 us; the launch traced here: 29.9 us
  starting transfers between devices  12.4 us (41%)
  Pallas kernels  8.48 us (28%)
  waiting for transfers between devices  8.31 us (28%)
  between operations  0.72 us (2%)
    pallas_call x10, Pallas kernels, call(): pl.pallas_call(kernel, out_shape=outs, in_specs=[pl.BlockSpec(memory_spac...  8.48 us
    ppermute x2, starting transfers between devices, body(): lax.ppermute(edge, ('dp', 'gy'), pairs)  4.47 us
    ppermute x3, waiting for transfers between devices, exchange(): lax.ppermute(value, axis, [(i, i ^ step) for i in range(lax.axis_size(axi...  3.34 us
    ppermute x2, starting transfers between devices, trade_ranks(): return lax.ppermute(value, ('dp', 'gx'), pairs)  2.88 us
    ppermute x2, waiting for transfers between devices, trade_ranks(): return lax.ppermute(value, ('dp', 'gx'), pairs)  2.75 us
    ppermute x2, starting transfers between devices, trade_shared(): return lax.ppermute(value, ('dp', 'gx', 'gy'), pairs)  2.36 us
    ppermute x3, starting transfers between devices, exchange(): lax.ppermute(value, axis, [(i, i ^ step) for i in range(lax.axis_size(axi...  2.16 us
    ppermute x2, waiting for transfers between devices, trade_shared(): return lax.ppermute(value, ('dp', 'gx', 'gy'), pairs)  2.06 us
  transfers between devices with their start and end apart: 10, of which 8 were waited for; matrix products, arithmetic and copies ran while one was open for 0% of the time, Pallas kernels for 11%

profile of v4, /device:TPU:0, one launch (start us, length us, event | category | flops | bytes accessed | tf_op | source)
XLA Modules:
  0.0 29.9 jit_solution(11204347462023856239)
XLA Ops:
  0.6 1.1 %shard_map.75 = (bf16[24,32,128]{2,1,0:T(8,128)(2,1)S(1)}, bf16[2,8,2048]{2,1,0:T(8,128)(2,1)S(1)}, bf16[27,3,32]{2,1,0:T(4,128)(2,1)S(1)}, bf16[864,64]{1,0:T(8,128)(2,1)S(1)}, bf16[128,128]{1,0:T(8,128)(2,1)S(1)}) custom-call(bf16[24,32,128]{2,1,0:T(8,128)(2,1)} %bitcast.11, bf16[2,8,2048]{2,1,0:T(8,128)(2,1)} %bitcast.12, bf16[27,3,32]{2,1,0:T(4,128)(2,1)} %bitcast.13, ...), custom_call_target="tpu_custom_call" | custom-call | bytes 1048576 | tf_op jit(solution)/shard_map/pallas_call | solution.py:555
  1.8 0.5 %collective-permute-start = (bf16[128,128]{1,0:T(8,128)(2,1)S(1)}, bf16[128,128]{1,0:T(8,128)(2,1)S(1)}, u32[]{:S(2)}, u32[]{:S(2)}) collective-permute-start(bf16[128,128]{1,0:T(8,128)(2,1)S(1)} %get-tuple-element.36), channel_id=1, source_target_pairs={{0,4},{4,0},{8,12},{12,8},{16,20},{20,16},{24,28},{28,24},{1,5},{5... | collective-permute-start | bytes 98312 | tf_op jit(solution)/shard_map/ppermute | solution.py:620
  2.3 0.7 %shard_map.77 = (bf16[1152,256]{1,0:T(8,128)(2,1)S(1)}, bf16[1152,256]{1,0:T(8,128)(2,1)S(1)}, bf16[256,2048]{1,0:T(8,128)(2,1)S(1)}) custom-call(bf16[27,3,32]{2,1,0:T(4,128)(2,1)S(1)} %get-tuple-element.38.one_ref, bf16[864,64]{1,0:T(8,128)(2,1)S(1)} %get-tuple-element.39.two_ref), custom_call_target="tpu_custom_call" | custom-call | flops 1073741824 | bytes 1048576 | tf_op jit(solution)/shard_map/pallas_call | solution.py:555
  3.0 0.2 collective-permute-done.refs_2_.refs_4_
  3.2 0.4 %shard_map.76 = (bf16[5,384,128]{2,1,0:T(8,128)(2,1)S(1)}, bf16[80,128]{1,0:T(8,128)(2,1)S(1)}, bf16[80,128]{1,0:T(8,128)(2,1)S(1)}) custom-call(bf16[24,32,128]{2,1,0:T(8,128)(2,1)S(1)} %get-tuple-element.34.refs_0_, bf16[2,8,2048]{2,1,0:T(8,128)(2,1)S(1)} %get-tuple-element.35.refs_1_.refs_3_, bf16[128,128]{1,0:T(8,128)(2,1)S(1)} %collective-permute-done.refs_2_.refs_4_), custom_call_target="tpu_custom_call" | custom-call | bytes 1048576 | tf_op jit(solution)/shard_map/pallas_call | solution.py:555
  3.5 3.0 %collective-permute-start.1 = (bf16[80,128]{1,0:T(8,128)(2,1)S(1)}, bf16[80,128]{1,0:T(8,128)(2,1)S(1)}, u32[]{:S(2)}, u32[]{:S(2)}) collective-permute-start(bf16[80,128]{1,0:T(8,128)(2,1)S(1)} %get-tuple-element.53), channel_id=1, source_target_pairs={{0,1},{1,0},{2,3},{3,2},{8,9},{9,8},{10,11},{11,10},{16,17},{17,16... | collective-permute-start | bytes 61448 | tf_op jit(solution)/shard_map/ppermute | solution.py:634
  6.5 1.5 %collective-permute-start.2 = (bf16[80,128]{1,0:T(8,128)(2,1)S(1)}, bf16[80,128]{1,0:T(8,128)(2,1)S(1)}, u32[]{:S(2)}, u32[]{:S(2)}) collective-permute-start(bf16[80,128]{1,0:T(8,128)(2,1)S(1)} %get-tuple-element.54), channel_id=1, source_target_pairs={{0,8},{1,2},{2,1},{3,11},{8,0},{9,10},{10,9},{11,3},{16,24},{17,18... | collective-permute-start | bytes 61448 | tf_op jit(solution)/shard_map/ppermute | solution.py:634
  8.0 2.5 %shard_map.78 = (bf16[5,8,64,128]{3,2,1,0:T(8,128)(2,1)S(1)}, bf16[5,128,256]{2,1,0:T(8,128)(2,1)S(1)}, bf16[3,4,112,128]{3,2,1,0:T(8,128)(2,1)S(1)}, f32[4,2,11...) custom-call(bf16[5,384,128]{2,1,0:T(8,128)(2,1)S(1)} %get-tuple-elem, ...), custom_call_target="tpu_custom_call" | custom-call | flops 2147483648 | bytes 1048576 | tf_op jit(solution)/shard_map/pallas_call | solution.py:555
  10.5 0.0 collective-permute-done.1.refs_13_
  10.5 0.0 collective-permute-done.2.refs_14_
  10.5 2.9 %shard_map.79 = (bf16[2,8,2048]{2,1,0:T(8,128)(2,1)}, bf16[4,16,2048]{2,1,0:T(8,128)(2,1)}, bf16[32,1024]{1,0:T(8,128)(2,1)S(1)}, bf16[32,1024]{1,0:T(8,128)(2,1)S(1)}) custom-call(bf16[5,8,64,128]{3,2,1,0:T(8,128)(2,1)S(1)} %get-tuple-element.42.refs_0_, bf16[5,128,256]{2,1,0:T(8,128)(2,1)S(1)} %get-tuple-element.43.refs_1_, ...), custom_call_target="tpu_custom_call" | custom-call | bytes 1048576 | tf_op jit(solution)/shard_map/pallas_call | solution.py:555
  13.4 0.1 collective-permute-start.3
  13.5 1.2 %collective-permute-done.3.got_ref = bf16[32,1024]{1,0:T(8,128)(2,1)S(1)} collective-permute-done((bf16[32,1024]{1,0:T(8,128)(2,1)S(1)}, bf16[32,1024]{1,0:T(8,128)(2,1)S(1)}, u32[]{:S(2)}, u32[]{:S(2)}) %collective-permute-start.3) | collective-permute-done | bytes 65568 | tf_op jit(solution)/shard_map/ppermute | solution.py:571
  14.8 1.4 %collective-permute-start.4 = (bf16[16,1024]{1,0:T(8,128)(2,1)S(1)}, bf16[16,1024]{1,0:T(8,128)(2,1)S(1)}, u32[]{:S(2)}, u32[]{:S(2)}) collective-permute-start(bf16[16,1024]{1,0:T(8,128)(2,1)S(1)} %get-tuple-element.60), channel_id=1, source_target_pairs={{0,8},{4,20},{8,0},{12,28},{16,24},{20,4},{24,16},{28,12},{1,9},{5... | collective-permute-start | bytes 98312 | tf_op jit(solution)/shard_map/ppermute | solution.py:594
  16.2 1.5 %collective-permute-start.5 = (bf16[16,1024]{1,0:T(8,128)(2,1)S(1)}, bf16[16,1024]{1,0:T(8,128)(2,1)S(1)}, u32[]{:S(2)}, u32[]{:S(2)}) collective-permute-start(bf16[16,1024]{1,0:T(8,128)(2,1)S(1)} %get-tuple-element.61), channel_id=1, source_target_pairs={{0,16},{4,28},{8,24},{12,20},{16,0},{20,12},{24,8},{28,4},{1,17},{... | collective-permute-start | bytes 98312 | tf_op jit(solution)/shard_map/ppermute | solution.py:594
  17.7 1.1 %collective-permute-done.4.first_ref = bf16[16,1024]{1,0:T(8,128)(2,1)S(1)} collective-permute-done((bf16[16,1024]{1,0:T(8,128)(2,1)S(1)}, bf16[16,1024]{1,0:T(8,128)(2,1)S(1)}, u32[]{:S(2)}, u32[]{:S(2)}) %collective-permute-start.4) | collective-permute-done | bytes 32800 | tf_op jit(solution)/shard_map/ppermute | solution.py:594
  18.8 1.6 %collective-permute-done.5.second_ref = bf16[16,1024]{1,0:T(8,128)(2,1)S(1)} collective-permute-done((bf16[16,1024]{1,0:T(8,128)(2,1)S(1)}, bf16[16,1024]{1,0:T(8,128)(2,1)S(1)}, u32[]{:S(2)}, u32[]{:S(2)}) %collective-permute-start.5) | collective-permute-done | bytes 32800 | tf_op jit(solution)/shard_map/ppermute | solution.py:594
  20.4 0.1 collective-permute-start.6
  20.5 1.2 %collective-permute-done.6.refs_1_ = bf16[16,1024]{1,0:T(8,128)(2,1)S(1)} collective-permute-done((bf16[16,1024]{1,0:T(8,128)(2,1)S(1)}, bf16[16,1024]{1,0:T(8,128)(2,1)S(1)}, u32[]{:S(2)}, u32[]{:S(2)}) %collective-permute-start.6) | collective-permute-done | bytes 32800 | tf_op jit(solution)/shard_map/ppermute | solution.py:571
  21.7 0.5 %collective-permute-start.8 = (bf16[16,1024]{1,0:T(8,128)(2,1)S(1)}, bf16[16,1024]{1,0:T(8,128)(2,1)S(1)}, u32[]{:S(2)}, u32[]{:S(2)}) collective-permute-start(bf16[16,1024]{1,0:T(8,128)(2,1)S(1)} %shard_map.82.mine_ref), channel_id=1, source_target_pairs={{0,8},{1,9},{2,10},{3,11},{4,7},{5,6},{6,5},{7,4},{8,0},{9,1},{10,... | collective-permute-start | bytes 98312 | tf_op jit(solution)/shard_map/ppermute | solution.py:584
  22.2 1.9 %collective-permute-start.7 = (bf16[16,1024]{1,0:T(8,128)(2,1)S(1)}, bf16[16,1024]{1,0:T(8,128)(2,1)S(1)}, u32[]{:S(2)}, u32[]{:S(2)}) collective-permute-start(bf16[16,1024]{1,0:T(8,128)(2,1)S(1)} %shard_map.82.mine_ref), channel_id=1, source_target_pairs={{0,1},{1,0},{2,3},{3,2},{4,6},{5,7},{6,4},{7,5},{8,9},{9,8},{10,11... | collective-permute-start | bytes 98312 | tf_op jit(solution)/shard_map/ppermute | solution.py:584
  24.1 1.6 %collective-permute-done.8.second_ref = bf16[16,1024]{1,0:T(8,128)(2,1)S(1)} collective-permute-done((bf16[16,1024]{1,0:T(8,128)(2,1)S(1)}, bf16[16,1024]{1,0:T(8,128)(2,1)S(1)}, u32[]{:S(2)}, u32[]{:S(2)}) %collective-permute-start.8) | collective-permute-done | bytes 32800 | tf_op jit(solution)/shard_map/ppermute | solution.py:584
  25.7 0.4 %collective-permute-done.7.first_ref = bf16[16,1024]{1,0:T(8,128)(2,1)S(1)} collective-permute-done((bf16[16,1024]{1,0:T(8,128)(2,1)S(1)}, bf16[16,1024]{1,0:T(8,128)(2,1)S(1)}, u32[]{:S(2)}, u32[]{:S(2)}) %collective-permute-start.7) | collective-permute-done | bytes 32800 | tf_op jit(solution)/shard_map/ppermute | solution.py:584
  26.2 2.0 %collective-permute-start.9 = (f32[16,1024]{1,0:T(8,128)S(1)}, f32[16,1024]{1,0:T(8,128)S(1)}, u32[]{:S(2)}, u32[]{:S(2)}) collective-permute-start(f32[16,1024]{1,0:T(8,128)S(1)} %shard_map.83.refs_0_), channel_id=1, source_target_pairs={{0,4},{4,0},{1,5},{5,1},{2,6},{6,2},{3,7},{7,3},{8,12},{12,8},{9,1... | collective-permute-start | bytes 196616 | tf_op jit(solution)/shard_map/ppermute | solution.py:571
  28.2 0.9 %collective-permute-done.9.refs_1_ = f32[16,1024]{1,0:T(8,128)S(1)} collective-permute-done((f32[16,1024]{1,0:T(8,128)S(1)}, f32[16,1024]{1,0:T(8,128)S(1)}, u32[]{:S(2)}, u32[]{:S(2)}) %collective-permute-start.9) | collective-permute-done | bytes 65568 | tf_op jit(solution)/shard_map/ppermute | solution.py:571
  29.1 0.8 %shard_map.84 = (f32[27,3,8]{2,1,0:T(4,128)}, f32[27,16,32]{2,1,0:T(8,128)}) custom-call(f32[16,1024]{1,0:T(8,128)S(1)} %shard_map.83.refs_0_, f32[16,1024]{1,0:T(8,128)S(1)} %collective-permute-done.9.refs_1_), custom_call_target="tpu_custom_call" | custom-call | bytes 1048576 | tf_op jit(solution)/shard_map/pallas_call | solution.py:555
  (4 shorter events, 0.1 us)
Async XLA Ops:
  1.8 1.4 %collective-permute-start = (bf16[128,128]{1,0:T(8,128)(2,1)S(1)}, bf16[128,128]{1,0:T(8,128)(2,1)S(1)}, u32[]{:S(2)}, u32[]{:S(2)}) collective-permute-start(bf16[128,128]{1,0:T(8,128)(2,1)S(1)} %get-tuple-element.36), channel_id=1, source_target_pairs={{0,4},{4,0},{8,12},{12,8},{16,20},{20,16},{24,28},{28,24},{1,5},{5... | collective-permute-start | bytes 98312 | tf_op jit(solution)/shard_map/ppermute | solution.py:620
  3.5 6.9 %collective-permute-start.1 = (bf16[80,128]{1,0:T(8,128)(2,1)S(1)}, bf16[80,128]{1,0:T(8,128)(2,1)S(1)}, u32[]{:S(2)}, u32[]{:S(2)}) collective-permute-start(bf16[80,128]{1,0:T(8,128)(2,1)S(1)} %get-tuple-element.53), channel_id=1, source_target_pairs={{0,1},{1,0},{2,3},{3,2},{8,9},{9,8},{10,11},{11,10},{16,17},{17,16... | collective-permute-start | bytes 61448 | tf_op jit(solution)/shard_map/ppermute | solution.py:634
  6.5 4.0 %collective-permute-start.2 = (bf16[80,128]{1,0:T(8,128)(2,1)S(1)}, bf16[80,128]{1,0:T(8,128)(2,1)S(1)}, u32[]{:S(2)}, u32[]{:S(2)}) collective-permute-start(bf16[80,128]{1,0:T(8,128)(2,1)S(1)} %get-tuple-element.54), channel_id=1, source_target_pairs={{0,8},{1,2},{2,1},{3,11},{8,0},{9,10},{10,9},{11,3},{16,24},{17,18... | collective-permute-start | bytes 61448 | tf_op jit(solution)/shard_map/ppermute | solution.py:634
  13.4 1.3 %collective-permute-start.3 = (bf16[32,1024]{1,0:T(8,128)(2,1)S(1)}, bf16[32,1024]{1,0:T(8,128)(2,1)S(1)}, u32[]{:S(2)}, u32[]{:S(2)}) collective-permute-start(bf16[32,1024]{1,0:T(8,128)(2,1)S(1)} %get-tuple-element.58), channel_id=1, source_target_pairs={{0,4},{4,0},{1,5},{5,1},{2,6},{6,2},{3,7},{7,3},{8,12},{12,8},{9,1... | collective-permute-start | bytes 196616 | tf_op jit(solution)/shard_map/ppermute | solution.py:571
  14.8 4.0 %collective-permute-start.4 = (bf16[16,1024]{1,0:T(8,128)(2,1)S(1)}, bf16[16,1024]{1,0:T(8,128)(2,1)S(1)}, u32[]{:S(2)}, u32[]{:S(2)}) collective-permute-start(bf16[16,1024]{1,0:T(8,128)(2,1)S(1)} %get-tuple-element.60), channel_id=1, source_target_pairs={{0,8},{4,20},{8,0},{12,28},{16,24},{20,4},{24,16},{28,12},{1,9},{5... | collective-permute-start | bytes 98312 | tf_op jit(solution)/shard_map/ppermute | solution.py:594
  16.2 4.3 %collective-permute-start.5 = (bf16[16,1024]{1,0:T(8,128)(2,1)S(1)}, bf16[16,1024]{1,0:T(8,128)(2,1)S(1)}, u32[]{:S(2)}, u32[]{:S(2)}) collective-permute-start(bf16[16,1024]{1,0:T(8,128)(2,1)S(1)} %get-tuple-element.61), channel_id=1, source_target_pairs={{0,16},{4,28},{8,24},{12,20},{16,0},{20,12},{24,8},{28,4},{1,17},{... | collective-permute-start | bytes 98312 | tf_op jit(solution)/shard_map/ppermute | solution.py:594
  20.4 1.3 %collective-permute-start.6 = (bf16[16,1024]{1,0:T(8,128)(2,1)S(1)}, bf16[16,1024]{1,0:T(8,128)(2,1)S(1)}, u32[]{:S(2)}, u32[]{:S(2)}) collective-permute-start(bf16[16,1024]{1,0:T(8,128)(2,1)S(1)} %shard_map.81.refs_0_), channel_id=1, source_target_pairs={{0,4},{4,0},{1,5},{5,1},{2,6},{6,2},{3,7},{7,3},{8,12},{12,8},{9,1... | collective-permute-start | bytes 98312 | tf_op jit(solution)/shard_map/ppermute | solution.py:571
  21.7 4.0 %collective-permute-start.8 = (bf16[16,1024]{1,0:T(8,128)(2,1)S(1)}, bf16[16,1024]{1,0:T(8,128)(2,1)S(1)}, u32[]{:S(2)}, u32[]{:S(2)}) collective-permute-start(bf16[16,1024]{1,0:T(8,128)(2,1)S(1)} %shard_map.82.mine_ref), channel_id=1, source_target_pairs={{0,8},{1,9},{2,10},{3,11},{4,7},{5,6},{6,5},{7,4},{8,0},{9,1},{10,... | collective-permute-start | bytes 98312 | tf_op jit(solution)/shard_map/ppermute | solution.py:584
  22.2 3.9 %collective-permute-start.7 = (bf16[16,1024]{1,0:T(8,128)(2,1)S(1)}, bf16[16,1024]{1,0:T(8,128)(2,1)S(1)}, u32[]{:S(2)}, u32[]{:S(2)}) collective-permute-start(bf16[16,1024]{1,0:T(8,128)(2,1)S(1)} %shard_map.82.mine_ref), channel_id=1, source_target_pairs={{0,1},{1,0},{2,3},{3,2},{4,6},{5,7},{6,4},{7,5},{8,9},{9,8},{10,11... | collective-permute-start | bytes 98312 | tf_op jit(solution)/shard_map/ppermute | solution.py:584
  26.2 2.9 %collective-permute-start.9 = (f32[16,1024]{1,0:T(8,128)S(1)}, f32[16,1024]{1,0:T(8,128)S(1)}, u32[]{:S(2)}, u32[]{:S(2)}) collective-permute-start(f32[16,1024]{1,0:T(8,128)S(1)} %shard_map.83.refs_0_), channel_id=1, source_target_pairs={{0,4},{4,0},{1,5},{5,1},{2,6},{6,2},{3,7},{7,3},{8,12},{12,8},{9,1... | collective-permute-start | bytes 196616 | tf_op jit(solution)/shard_map/ppermute | solution.py:571

commit v5 on v3

--- a/solution.py
+++ b/solution.py
@@ -63,7 +63,7 @@
     odd = position("gx")[0]
     planes = mag_ref.shape[0]
     blocks = cot_ref.shape[2] // 128
-    for fetch in fetches:
+    for fetch in fetches[:2]:
         fetch.wait()
     field = mag_ref[...].astype(F32)
     low = field[:, 0:4, :]
@@ -79,6 +79,8 @@
                 row = 4 * planes + 16 * k + m
                 stage[row : row + 1, :] = cot[k][:, 128 * m : 128 * m + 128]
         outs[turn][...] = stage[...].astype(BF)
+    for fetch in fetches[2:]:
+        fetch.wait()
 
 
 def edge_y_kernel(count_x, count_y, mag_ref, cot_ref, *refs):
@@ -414,28 +416,6 @@
         patches.append(jnp.concatenate(short, axis=1))
     delta, patches = jnp.concatenate(delta, axis=0), jnp.concatenate(patches, axis=0)
 
-    place = iota((64, 128), 1) >> 5
-    turned = []
-    for ab in range(9):
-        if ab % 2 == 0:
-            first, last = 128 * ab, min(128 * ab + 256, 1152)
-            grad = dot(delta, patches[:, first:last], ((0,), (0,)))[0:192] + grad_in[:, first:last]
-        column = 128 * (ab % 2)
-        a0, a1, a2 = (grad[64 * j : 64 * j + 64, column : column + 128] for j in range(3))
-        r0, r1, r2 = (pltpu.roll(a, 64, 1) for a in (a0, a1, a2))
-        joined = jnp.where(place == 0, a0 + r1, jnp.where(place == 1, a1 + r2, a1 + r0))
-        shift = (3 * ab - 1) % 4
-        other = (shift + 2) % 4
-        outer = pltpu.roll(joined, 32 * shift, 1) if shift else joined
-        inner = pltpu.roll(joined, 32 * other, 1) if other else joined
-        turned += [outer, inner, outer]
-    turned.append(jnp.zeros((64, 128), F32))
-    for v in range(7):
-        t0, t1, t2, t3 = turned[4 * v : 4 * v + 4]
-        total[:, 128 * v : 128 * v + 128] = jnp.where(
-            place < 2, jnp.where(place == 0, t0, t1), jnp.where(place == 2, t2, t3)
-        )
-
     lhs_rows, rhs_rows = [], []
     for p in range(4):
         depth = [(1, p // 2)] if p % 2 == 0 else [(2, (p - 1) // 2), (0, (p + 1) // 2)]
@@ -466,6 +446,28 @@
     delta_one = jnp.concatenate(lhs_rows, axis=0).T
     windows = jnp.concatenate(rhs_rows, axis=0)
 
+    place = iota((64, 128), 1) >> 5
+    turned = []
+    for ab in range(9):
+        if ab % 2 == 0:
+            first, last = 128 * ab, min(128 * ab + 256, 1152)
+            grad = dot(delta, patches[:, first:last], ((0,), (0,)))[0:192] + grad_in[:, first:last]
+        column = 128 * (ab % 2)
+        a0, a1, a2 = (grad[64 * j : 64 * j + 64, column : column + 128] for j in range(3))
+        r0, r1, r2 = (pltpu.roll(a, 64, 1) for a in (a0, a1, a2))
+        joined = jnp.where(place == 0, a0 + r1, jnp.where(place == 1, a1 + r2, a1 + r0))
+        shift = (3 * ab - 1) % 4
+        other = (shift + 2) % 4
+        outer = pltpu.roll(joined, 32 * shift, 1) if shift else joined
+        inner = pltpu.roll(joined, 32 * other, 1) if other else joined
+        turned += [outer, inner, outer]
+    turned.append(jnp.zeros((64, 128), F32))
+    for v in range(7):
+        t0, t1, t2, t3 = turned[4 * v : 4 * v + 4]
+        total[:, 128 * v : 128 * v + 128] = jnp.where(
+            place < 2, jnp.where(place == 0, t0, t1), jnp.where(place == 2, t2, t3)
+        )
+
     place = iota((32, 128), 1)
     found = jnp.zeros((32, 128), F32)
     for tap in range(9):

time: 29.9 us -> 29.7 us (level)
  no operation moved by 1% of the time
where the time goes in v5:
time: 29.7 us; the launch traced here: 29.5 us
  starting transfers between devices  12.9 us (43%)
  Pallas kernels  8.11 us (27%)
  waiting for transfers between devices  7.76 us (26%)
  between operations  0.71 us (2%)
    pallas_call x9, Pallas kernels, call(): pl.pallas_call(kernel, out_shape=outs, in_specs=[pl.BlockSpec(memory_spac...  8.11 us
    ppermute x5, waiting for transfers between devices, exchange(): lax.ppermute(value, axis, [(i, i ^ step) for i in range(lax.axis_size(axi...  5.5 us
    ppermute x5, starting transfers between devices, exchange(): lax.ppermute(value, axis, [(i, i ^ step) for i in range(lax.axis_size(axi...  4.72 us
    ppermute x2, starting transfers between devices, body(): lax.ppermute(edge, ('dp', 'gy'), pairs)  4.47 us
    ppermute x2, starting transfers between devices, trade_shared(): return lax.ppermute(value, ('dp', 'gx', 'gy'), pairs)  3.22 us
    ppermute x2, waiting for transfers between devices, trade_shared(): return lax.ppermute(value, ('dp', 'gx', 'gy'), pairs)  2.1 us
  transfers between devices with their start and end apart: 10, of which 8 were waited for; matrix products, arithmetic and copies ran while one was open for 0% of the time, Pallas kernels for 11%

profile of v5, /device:TPU:0, one launch (start us, length us, event | category | flops | bytes accessed | tf_op | source)
XLA Modules:
  0.0 29.5 jit_solution(17794324770408247565)
XLA Ops:
  0.6 1.1 %shard_map.75 = (bf16[24,32,128]{2,1,0:T(8,128)(2,1)S(1)}, bf16[2,8,2048]{2,1,0:T(8,128)(2,1)S(1)}, bf16[27,3,32]{2,1,0:T(4,128)(2,1)S(1)}, bf16[864,64]{1,0:T(8,128)(2,1)S(1)}, bf16[128,128]{1,0:T(8,128)(2,1)S(1)}) custom-call(bf16[24,32,128]{2,1,0:T(8,128)(2,1)} %bitcast.11, bf16[2,8,2048]{2,1,0:T(8,128)(2,1)} %bitcast.12, bf16[27,3,32]{2,1,0:T(4,128)(2,1)} %bitcast.13, ...), custom_call_target="tpu_custom_call" | custom-call | bytes 1048576 | tf_op jit(solution)/shard_map/pallas_call | solution.py:537
  1.8 0.5 %collective-permute-start = (bf16[128,128]{1,0:T(8,128)(2,1)S(1)}, bf16[128,128]{1,0:T(8,128)(2,1)S(1)}, u32[]{:S(2)}, u32[]{:S(2)}) collective-permute-start(bf16[128,128]{1,0:T(8,128)(2,1)S(1)} %get-tuple-element.35), channel_id=1, source_target_pairs={{0,4},{4,0},{8,12},{12,8},{16,20},{20,16},{24,28},{28,24},{1,5},{5... | collective-permute-start | bytes 98312 | tf_op jit(solution)/shard_map/ppermute | solution.py:592
  2.3 0.7 %shard_map.77 = (bf16[1152,256]{1,0:T(8,128)(2,1)S(1)}, bf16[1152,256]{1,0:T(8,128)(2,1)S(1)}, bf16[256,2048]{1,0:T(8,128)(2,1)S(1)}) custom-call(bf16[27,3,32]{2,1,0:T(4,128)(2,1)S(1)} %get-tuple-element.37.one_ref, bf16[864,64]{1,0:T(8,128)(2,1)S(1)} %get-tuple-element.38.two_ref), custom_call_target="tpu_custom_call" | custom-call | flops 1073741824 | bytes 1048576 | tf_op jit(solution)/shard_map/pallas_call | solution.py:537
  3.0 0.2 collective-permute-done.refs_2_.refs_4_
  3.1 0.4 %shard_map.76 = (bf16[5,384,128]{2,1,0:T(8,128)(2,1)S(1)}, bf16[80,128]{1,0:T(8,128)(2,1)S(1)}, bf16[80,128]{1,0:T(8,128)(2,1)S(1)}) custom-call(bf16[24,32,128]{2,1,0:T(8,128)(2,1)S(1)} %get-tuple-element.33.refs_0_, bf16[2,8,2048]{2,1,0:T(8,128)(2,1)S(1)} %get-tuple-element.34.refs_1_.refs_3_, bf16[128,128]{1,0:T(8,128)(2,1)S(1)} %collective-permute-done.refs_2_.refs_4_), custom_call_target="tpu_custom_call" | custom-call | bytes 1048576 | tf_op jit(solution)/shard_map/pallas_call | solution.py:537
  3.5 3.0 %collective-permute-start.1 = (bf16[80,128]{1,0:T(8,128)(2,1)S(1)}, bf16[80,128]{1,0:T(8,128)(2,1)S(1)}, u32[]{:S(2)}, u32[]{:S(2)}) collective-permute-start(bf16[80,128]{1,0:T(8,128)(2,1)S(1)} %get-tuple-element.52), channel_id=1, source_target_pairs={{0,1},{1,0},{2,3},{3,2},{8,9},{9,8},{10,11},{11,10},{16,17},{17,16... | collective-permute-start | bytes 61448 | tf_op jit(solution)/shard_map/ppermute | solution.py:606
  6.5 1.5 %collective-permute-start.2 = (bf16[80,128]{1,0:T(8,128)(2,1)S(1)}, bf16[80,128]{1,0:T(8,128)(2,1)S(1)}, u32[]{:S(2)}, u32[]{:S(2)}) collective-permute-start(bf16[80,128]{1,0:T(8,128)(2,1)S(1)} %get-tuple-element.53), channel_id=1, source_target_pairs={{0,8},{1,2},{2,1},{3,11},{8,0},{9,10},{10,9},{11,3},{16,24},{17,18... | collective-permute-start | bytes 61448 | tf_op jit(solution)/shard_map/ppermute | solution.py:606
  8.0 2.5 %shard_map.78 = (bf16[5,8,64,128]{3,2,1,0:T(8,128)(2,1)S(1)}, bf16[5,128,256]{2,1,0:T(8,128)(2,1)S(1)}, bf16[3,4,112,128]{3,2,1,0:T(8,128)(2,1)S(1)}, f32[4,2,11...) custom-call(bf16[5,384,128]{2,1,0:T(8,128)(2,1)S(1)} %get-tuple-elem, ...), custom_call_target="tpu_custom_call" | custom-call | flops 2147483648 | bytes 1048576 | tf_op jit(solution)/shard_map/pallas_call | solution.py:537
  10.4 0.0 collective-permute-done.1.refs_13_
  10.4 0.0 collective-permute-done.2.refs_14_
  10.5 2.6 %shard_map.79 = (bf16[2,8,2048]{2,1,0:T(8,128)(2,1)}, bf16[4,16,2048]{2,1,0:T(8,128)(2,1)}, bf16[16,1024]{1,0:T(8,128)(2,1)S(1)}, bf16[16,1024]{1,0:T(8,128)(2,1...) custom-call(bf16[5,8,64,128]{3,2,1,0:T(8,128)(2,1)S(1)} %get-tuple-element.41.refs_0_, ...), custom_call_target="tpu_custom_call" | custom-call | bytes 1048576 | tf_op jit(solution)/shard_map/pallas_call | solution.py:537
  13.1 2.3 %collective-permute-start.3 = (bf16[16,1024]{1,0:T(8,128)(2,1)S(1)}, bf16[16,1024]{1,0:T(8,128)(2,1)S(1)}, u32[]{:S(2)}, u32[]{:S(2)}) collective-permute-start(bf16[16,1024]{1,0:T(8,128)(2,1)S(1)} %get-tuple-element.56), channel_id=1, source_target_pairs={{0,24},{8,16},{16,8},{24,0},{1,25},{9,17},{17,9},{25,1},{2,26},{10... | collective-permute-start | bytes 98312 | tf_op jit(solution)/shard_map/ppermute | solution.py:553
  15.4 0.7 %collective-permute-start.4 = (bf16[16,1024]{1,0:T(8,128)(2,1)S(1)}, bf16[16,1024]{1,0:T(8,128)(2,1)S(1)}, u32[]{:S(2)}, u32[]{:S(2)}) collective-permute-start(bf16[16,1024]{1,0:T(8,128)(2,1)S(1)} %get-tuple-element.57), channel_id=1, source_target_pairs={{0,8},{8,0},{16,24},{24,16},{1,9},{9,1},{17,25},{25,17},{2,10},{10... | collective-permute-start | bytes 98312 | tf_op jit(solution)/shard_map/ppermute | solution.py:553
  16.1 0.5 %collective-permute-start.5 = (bf16[16,1024]{1,0:T(8,128)(2,1)S(1)}, bf16[16,1024]{1,0:T(8,128)(2,1)S(1)}, u32[]{:S(2)}, u32[]{:S(2)}) collective-permute-start(bf16[16,1024]{1,0:T(8,128)(2,1)S(1)} %get-tuple-element.58), channel_id=1, source_target_pairs={{0,16},{8,24},{16,0},{24,8},{1,17},{9,25},{17,1},{25,9},{2,18},{10... | collective-permute-start | bytes 98312 | tf_op jit(solution)/shard_map/ppermute | solution.py:553
  16.7 1.3 %collective-permute-done.3.refs_0_ = bf16[16,1024]{1,0:T(8,128)(2,1)S(1)} collective-permute-done((bf16[16,1024]{1,0:T(8,128)(2,1)S(1)}, bf16[16,1024]{1,0:T(8,128)(2,1)S(1)}, u32[]{:S(2)}, u32[]{:S(2)}) %collective-permute-start.3) | collective-permute-done | bytes 32800 | tf_op jit(solution)/shard_map/ppermute | solution.py:553
  18.0 1.3 %collective-permute-done.4.refs_1_ = bf16[16,1024]{1,0:T(8,128)(2,1)S(1)} collective-permute-done((bf16[16,1024]{1,0:T(8,128)(2,1)S(1)}, bf16[16,1024]{1,0:T(8,128)(2,1)S(1)}, u32[]{:S(2)}, u32[]{:S(2)}) %collective-permute-start.4) | collective-permute-done | bytes 32800 | tf_op jit(solution)/shard_map/ppermute | solution.py:553
  19.3 0.7 %collective-permute-done.5.refs_2_ = bf16[16,1024]{1,0:T(8,128)(2,1)S(1)} collective-permute-done((bf16[16,1024]{1,0:T(8,128)(2,1)S(1)}, bf16[16,1024]{1,0:T(8,128)(2,1)S(1)}, u32[]{:S(2)}, u32[]{:S(2)}) %collective-permute-start.5) | collective-permute-done | bytes 32800 | tf_op jit(solution)/shard_map/ppermute | solution.py:553
  20.1 0.1 collective-permute-start.6
  20.2 1.2 %collective-permute-done.6.refs_1_ = bf16[16,1024]{1,0:T(8,128)(2,1)S(1)} collective-permute-done((bf16[16,1024]{1,0:T(8,128)(2,1)S(1)}, bf16[16,1024]{1,0:T(8,128)(2,1)S(1)}, u32[]{:S(2)}, u32[]{:S(2)}) %collective-permute-start.6) | collective-permute-done | bytes 32800 | tf_op jit(solution)/shard_map/ppermute | solution.py:553
  21.4 1.4 %collective-permute-start.8 = (bf16[16,1024]{1,0:T(8,128)(2,1)S(1)}, bf16[16,1024]{1,0:T(8,128)(2,1)S(1)}, u32[]{:S(2)}, u32[]{:S(2)}) collective-permute-start(bf16[16,1024]{1,0:T(8,128)(2,1)S(1)} %shard_map.81.mine_ref), channel_id=1, source_target_pairs={{0,8},{1,9},{2,10},{3,11},{4,7},{5,6},{6,5},{7,4},{8,0},{9,1},{10,... | collective-permute-start | bytes 98312 | tf_op jit(solution)/shard_map/ppermute | solution.py:566
  22.7 1.9 %collective-permute-start.7 = (bf16[16,1024]{1,0:T(8,128)(2,1)S(1)}, bf16[16,1024]{1,0:T(8,128)(2,1)S(1)}, u32[]{:S(2)}, u32[]{:S(2)}) collective-permute-start(bf16[16,1024]{1,0:T(8,128)(2,1)S(1)} %shard_map.81.mine_ref), channel_id=1, source_target_pairs={{0,1},{1,0},{2,3},{3,2},{4,6},{5,7},{6,4},{7,5},{8,9},{9,8},{10,11... | collective-permute-start | bytes 98312 | tf_op jit(solution)/shard_map/ppermute | solution.py:566
  24.6 0.8 %collective-permute-done.8.second_ref = bf16[16,1024]{1,0:T(8,128)(2,1)S(1)} collective-permute-done((bf16[16,1024]{1,0:T(8,128)(2,1)S(1)}, bf16[16,1024]{1,0:T(8,128)(2,1)S(1)}, u32[]{:S(2)}, u32[]{:S(2)}) %collective-permute-start.8) | collective-permute-done | bytes 32800 | tf_op jit(solution)/shard_map/ppermute | solution.py:566
  25.3 1.3 %collective-permute-done.7.first_ref = bf16[16,1024]{1,0:T(8,128)(2,1)S(1)} collective-permute-done((bf16[16,1024]{1,0:T(8,128)(2,1)S(1)}, bf16[16,1024]{1,0:T(8,128)(2,1)S(1)}, u32[]{:S(2)}, u32[]{:S(2)}) %collective-permute-start.7) | collective-permute-done | bytes 32800 | tf_op jit(solution)/shard_map/ppermute | solution.py:566
  26.7 1.1 %collective-permute-start.9 = (f32[16,1024]{1,0:T(8,128)S(1)}, f32[16,1024]{1,0:T(8,128)S(1)}, u32[]{:S(2)}, u32[]{:S(2)}) collective-permute-start(f32[16,1024]{1,0:T(8,128)S(1)} %shard_map.82.refs_0_), channel_id=1, source_target_pairs={{0,4},{4,0},{1,5},{5,1},{2,6},{6,2},{3,7},{7,3},{8,12},{12,8},{9,1... | collective-permute-start | bytes 196616 | tf_op jit(solution)/shard_map/ppermute | solution.py:553
  27.8 0.9 %collective-permute-done.9.refs_1_ = f32[16,1024]{1,0:T(8,128)S(1)} collective-permute-done((f32[16,1024]{1,0:T(8,128)S(1)}, f32[16,1024]{1,0:T(8,128)S(1)}, u32[]{:S(2)}, u32[]{:S(2)}) %collective-permute-start.9) | collective-permute-done | bytes 65568 | tf_op jit(solution)/shard_map/ppermute | solution.py:553
  28.7 0.8 %shard_map.83 = (f32[27,3,8]{2,1,0:T(4,128)}, f32[27,16,32]{2,1,0:T(8,128)}) custom-call(f32[16,1024]{1,0:T(8,128)S(1)} %shard_map.82.refs_0_, f32[16,1024]{1,0:T(8,128)S(1)} %collective-permute-done.9.refs_1_), custom_call_target="tpu_custom_call" | custom-call | bytes 1048576 | tf_op jit(solution)/shard_map/pallas_call | solution.py:537
  (3 shorter events, 0.0 us)
Async XLA Ops:
  1.8 1.4 %collective-permute-start = (bf16[128,128]{1,0:T(8,128)(2,1)S(1)}, bf16[128,128]{1,0:T(8,128)(2,1)S(1)}, u32[]{:S(2)}, u32[]{:S(2)}) collective-permute-start(bf16[128,128]{1,0:T(8,128)(2,1)S(1)} %get-tuple-element.35), channel_id=1, source_target_pairs={{0,4},{4,0},{8,12},{12,8},{16,20},{20,16},{24,28},{28,24},{1,5},{5... | collective-permute-start | bytes 98312 | tf_op jit(solution)/shard_map/ppermute | solution.py:592
  3.5 6.9 %collective-permute-start.1 = (bf16[80,128]{1,0:T(8,128)(2,1)S(1)}, bf16[80,128]{1,0:T(8,128)(2,1)S(1)}, u32[]{:S(2)}, u32[]{:S(2)}) collective-permute-start(bf16[80,128]{1,0:T(8,128)(2,1)S(1)} %get-tuple-element.52), channel_id=1, source_target_pairs={{0,1},{1,0},{2,3},{3,2},{8,9},{9,8},{10,11},{11,10},{16,17},{17,16... | collective-permute-start | bytes 61448 | tf_op jit(solution)/shard_map/ppermute | solution.py:606
  6.5 4.0 %collective-permute-start.2 = (bf16[80,128]{1,0:T(8,128)(2,1)S(1)}, bf16[80,128]{1,0:T(8,128)(2,1)S(1)}, u32[]{:S(2)}, u32[]{:S(2)}) collective-permute-start(bf16[80,128]{1,0:T(8,128)(2,1)S(1)} %get-tuple-element.53), channel_id=1, source_target_pairs={{0,8},{1,2},{2,1},{3,11},{8,0},{9,10},{10,9},{11,3},{16,24},{17,18... | collective-permute-start | bytes 61448 | tf_op jit(solution)/shard_map/ppermute | solution.py:606
  13.1 4.9 %collective-permute-start.3 = (bf16[16,1024]{1,0:T(8,128)(2,1)S(1)}, bf16[16,1024]{1,0:T(8,128)(2,1)S(1)}, u32[]{:S(2)}, u32[]{:S(2)}) collective-permute-start(bf16[16,1024]{1,0:T(8,128)(2,1)S(1)} %get-tuple-element.56), channel_id=1, source_target_pairs={{0,24},{8,16},{16,8},{24,0},{1,25},{9,17},{17,9},{25,1},{2,26},{10... | collective-permute-start | bytes 98312 | tf_op jit(solution)/shard_map/ppermute | solution.py:553
  15.4 3.9 %collective-permute-start.4 = (bf16[16,1024]{1,0:T(8,128)(2,1)S(1)}, bf16[16,1024]{1,0:T(8,128)(2,1)S(1)}, u32[]{:S(2)}, u32[]{:S(2)}) collective-permute-start(bf16[16,1024]{1,0:T(8,128)(2,1)S(1)} %get-tuple-element.57), channel_id=1, source_target_pairs={{0,8},{8,0},{16,24},{24,16},{1,9},{9,1},{17,25},{25,17},{2,10},{10... | collective-permute-start | bytes 98312 | tf_op jit(solution)/shard_map/ppermute | solution.py:553
  16.1 3.9 %collective-permute-start.5 = (bf16[16,1024]{1,0:T(8,128)(2,1)S(1)}, bf16[16,1024]{1,0:T(8,128)(2,1)S(1)}, u32[]{:S(2)}, u32[]{:S(2)}) collective-permute-start(bf16[16,1024]{1,0:T(8,128)(2,1)S(1)} %get-tuple-element.58), channel_id=1, source_target_pairs={{0,16},{8,24},{16,0},{24,8},{1,17},{9,25},{17,1},{25,9},{2,18},{10... | collective-permute-start | bytes 98312 | tf_op jit(solution)/shard_map/ppermute | solution.py:553
  20.1 1.3 %collective-permute-start.6 = (bf16[16,1024]{1,0:T(8,128)(2,1)S(1)}, bf16[16,1024]{1,0:T(8,128)(2,1)S(1)}, u32[]{:S(2)}, u32[]{:S(2)}) collective-permute-start(bf16[16,1024]{1,0:T(8,128)(2,1)S(1)} %shard_map.80.refs_0_), channel_id=1, source_target_pairs={{0,4},{4,0},{1,5},{5,1},{2,6},{6,2},{3,7},{7,3},{8,12},{12,8},{9,1... | collective-permute-start | bytes 98312 | tf_op jit(solution)/shard_map/ppermute | solution.py:553
  21.4 4.0 %collective-permute-start.8 = (bf16[16,1024]{1,0:T(8,128)(2,1)S(1)}, bf16[16,1024]{1,0:T(8,128)(2,1)S(1)}, u32[]{:S(2)}, u32[]{:S(2)}) collective-permute-start(bf16[16,1024]{1,0:T(8,128)(2,1)S(1)} %shard_map.81.mine_ref), channel_id=1, source_target_pairs={{0,8},{1,9},{2,10},{3,11},{4,7},{5,6},{6,5},{7,4},{8,0},{9,1},{10,... | collective-permute-start | bytes 98312 | tf_op jit(solution)/shard_map/ppermute | solution.py:566
  22.7 4.0 %collective-permute-start.7 = (bf16[16,1024]{1,0:T(8,128)(2,1)S(1)}, bf16[16,1024]{1,0:T(8,128)(2,1)S(1)}, u32[]{:S(2)}, u32[]{:S(2)}) collective-permute-start(bf16[16,1024]{1,0:T(8,128)(2,1)S(1)} %shard_map.81.mine_ref), channel_id=1, source_target_pairs={{0,1},{1,0},{2,3},{3,2},{4,6},{5,7},{6,4},{7,5},{8,9},{9,8},{10,11... | collective-permute-start | bytes 98312 | tf_op jit(solution)/shard_map/ppermute | solution.py:566
  26.7 2.0 %collective-permute-start.9 = (f32[16,1024]{1,0:T(8,128)S(1)}, f32[16,1024]{1,0:T(8,128)S(1)}, u32[]{:S(2)}, u32[]{:S(2)}) collective-permute-start(f32[16,1024]{1,0:T(8,128)S(1)} %shard_map.82.refs_0_), channel_id=1, source_target_pairs={{0,4},{4,0},{1,5},{5,1},{2,6},{6,2},{3,7},{7,3},{8,12},{12,8},{9,1... | collective-permute-start | bytes 196616 | tf_op jit(solution)/shard_map/ppermute | solution.py:553

commit v6 on v5

--- a/solution.py
+++ b/solution.py
@@ -447,13 +447,16 @@
     windows = jnp.concatenate(rhs_rows, axis=0)
 
     place = iota((64, 128), 1) >> 5
+    local = iota((32, 128), 1) & 31
     turned = []
+    found = jnp.zeros((32, 128), F32)
     for ab in range(9):
         if ab % 2 == 0:
             first, last = 128 * ab, min(128 * ab + 256, 1152)
-            grad = dot(delta, patches[:, first:last], ((0,), (0,)))[0:192] + grad_in[:, first:last]
+            grad_two = dot(delta, patches[:, first:last], ((0,), (0,)))[0:192] + grad_in[:, first:last]
+            grad_one = dot(delta_one, windows[:, first:last])
         column = 128 * (ab % 2)
-        a0, a1, a2 = (grad[64 * j : 64 * j + 64, column : column + 128] for j in range(3))
+        a0, a1, a2 = (grad_two[64 * j : 64 * j + 64, column : column + 128] for j in range(3))
         r0, r1, r2 = (pltpu.roll(a, 64, 1) for a in (a0, a1, a2))
         joined = jnp.where(place == 0, a0 + r1, jnp.where(place == 1, a1 + r2, a1 + r0))
         shift = (3 * ab - 1) % 4
@@ -461,26 +464,18 @@
         outer = pltpu.roll(joined, 32 * shift, 1) if shift else joined
         inner = pltpu.roll(joined, 32 * other, 1) if other else joined
         turned += [outer, inner, outer]
+        some = jnp.zeros((32, 128), F32)
+        for t in range(8):
+            piece = grad_one[32 * t : 32 * t + 32, column : column + 128]
+            shift = (3 * ab - 2 * t) % 128
+            some = some + (pltpu.roll(piece, shift, 1) if shift else piece)
+        found = jnp.where((local >= 3 * ab) & (local < 3 * ab + 3), some, found)
     turned.append(jnp.zeros((64, 128), F32))
     for v in range(7):
         t0, t1, t2, t3 = turned[4 * v : 4 * v + 4]
         total[:, 128 * v : 128 * v + 128] = jnp.where(
             place < 2, jnp.where(place == 0, t0, t1), jnp.where(place == 2, t2, t3)
         )
-
-    place = iota((32, 128), 1)
-    found = jnp.zeros((32, 128), F32)
-    for tap in range(9):
-        if tap % 2 == 0:
-            grad = dot(delta_one, windows[:, 128 * tap : min(128 * tap + 256, 1152)])
-        column = 128 * (tap % 2)
-        some = jnp.zeros((32, 128), F32)
-        for t in range(8):
-            piece = grad[32 * t : 32 * t + 32, column : column + 128]
-            shift = (3 * tap - 2 * t) % 128
-            some = some + (pltpu.roll(piece, shift, 1) if shift else piece)
-        local = place & 31
-        found = jnp.where((local >= 3 * tap) & (local < 3 * tap + 3), some, found)
     total[:, 896:1024] = jnp.zeros((64, 128), F32)
     tall, short = 64 // ranks, 32 // ranks
     for d in range(ranks):

time: 29.7 us -> 29.8 us (level)
  no operation moved by 1% of the time
where the time goes in v6:
time: 29.8 us; the launch traced here: 29.7 us
  starting transfers between devices  12.9 us (43%)
  Pallas kernels  8.28 us (28%)
  waiting for transfers between devices  7.76 us (26%)
  between operations  0.71 us (2%)
    pallas_call x9, Pallas kernels, call(): pl.pallas_call(kernel, out_shape=outs, in_specs=[pl.BlockSpec(memory_spac...  8.28 us
    ppermute x5, waiting for transfers between devices, exchange(): lax.ppermute(value, axis, [(i, i ^ step) for i in range(lax.axis_size(axi...  5.5 us
    ppermute x5, starting transfers between devices, exchange(): lax.ppermute(value, axis, [(i, i ^ step) for i in range(lax.axis_size(axi...  4.72 us
    ppermute x2, starting transfers between devices, body(): lax.ppermute(edge, ('dp', 'gy'), pairs)  4.47 us
    ppermute x2, starting transfers between devices, trade_shared(): return lax.ppermute(value, ('dp', 'gx', 'gy'), pairs)  3.22 us
    ppermute x2, waiting for transfers between devices, trade_shared(): return lax.ppermute(value, ('dp', 'gx', 'gy'), pairs)  2.1 us
  transfers between devices with their start and end apart: 10, of which 8 were waited for; matrix products, arithmetic and copies ran while one was open for 0% of the time, Pallas kernels for 11%

profile of v6, /device:TPU:0, one launch (start us, length us, event | category | flops | bytes accessed | tf_op | source)
XLA Modules:
  0.0 29.7 jit_solution(731789113010835388)
XLA Ops:
  0.6 1.1 %shard_map.75 = (bf16[24,32,128]{2,1,0:T(8,128)(2,1)S(1)}, bf16[2,8,2048]{2,1,0:T(8,128)(2,1)S(1)}, bf16[27,3,32]{2,1,0:T(4,128)(2,1)S(1)}, bf16[864,64]{1,0:T(8,128)(2,1)S(1)}, bf16[128,128]{1,0:T(8,128)(2,1)S(1)}) custom-call(bf16[24,32,128]{2,1,0:T(8,128)(2,1)} %bitcast.11, bf16[2,8,2048]{2,1,0:T(8,128)(2,1)} %bitcast.12, bf16[27,3,32]{2,1,0:T(4,128)(2,1)} %bitcast.13, ...), custom_call_target="tpu_custom_call" | custom-call | bytes 1048576 | tf_op jit(solution)/shard_map/pallas_call | solution.py:532
  1.8 0.5 %collective-permute-start = (bf16[128,128]{1,0:T(8,128)(2,1)S(1)}, bf16[128,128]{1,0:T(8,128)(2,1)S(1)}, u32[]{:S(2)}, u32[]{:S(2)}) collective-permute-start(bf16[128,128]{1,0:T(8,128)(2,1)S(1)} %get-tuple-element.35), channel_id=1, source_target_pairs={{0,4},{4,0},{8,12},{12,8},{16,20},{20,16},{24,28},{28,24},{1,5},{5... | collective-permute-start | bytes 98312 | tf_op jit(solution)/shard_map/ppermute | solution.py:587
  2.3 0.7 %shard_map.77 = (bf16[1152,256]{1,0:T(8,128)(2,1)S(1)}, bf16[1152,256]{1,0:T(8,128)(2,1)S(1)}, bf16[256,2048]{1,0:T(8,128)(2,1)S(1)}) custom-call(bf16[27,3,32]{2,1,0:T(4,128)(2,1)S(1)} %get-tuple-element.37.one_ref, bf16[864,64]{1,0:T(8,128)(2,1)S(1)} %get-tuple-element.38.two_ref), custom_call_target="tpu_custom_call" | custom-call | flops 1073741824 | bytes 1048576 | tf_op jit(solution)/shard_map/pallas_call | solution.py:532
  3.0 0.2 collective-permute-done.refs_2_.refs_4_
  3.1 0.4 %shard_map.76 = (bf16[5,384,128]{2,1,0:T(8,128)(2,1)S(1)}, bf16[80,128]{1,0:T(8,128)(2,1)S(1)}, bf16[80,128]{1,0:T(8,128)(2,1)S(1)}) custom-call(bf16[24,32,128]{2,1,0:T(8,128)(2,1)S(1)} %get-tuple-element.33.refs_0_, bf16[2,8,2048]{2,1,0:T(8,128)(2,1)S(1)} %get-tuple-element.34.refs_1_.refs_3_, bf16[128,128]{1,0:T(8,128)(2,1)S(1)} %collective-permute-done.refs_2_.refs_4_), custom_call_target="tpu_custom_call" | custom-call | bytes 1048576 | tf_op jit(solution)/shard_map/pallas_call | solution.py:532
  3.5 3.0 %collective-permute-start.1 = (bf16[80,128]{1,0:T(8,128)(2,1)S(1)}, bf16[80,128]{1,0:T(8,128)(2,1)S(1)}, u32[]{:S(2)}, u32[]{:S(2)}) collective-permute-start(bf16[80,128]{1,0:T(8,128)(2,1)S(1)} %get-tuple-element.52), channel_id=1, source_target_pairs={{0,1},{1,0},{2,3},{3,2},{8,9},{9,8},{10,11},{11,10},{16,17},{17,16... | collective-permute-start | bytes 61448 | tf_op jit(solution)/shard_map/ppermute | solution.py:601
  6.5 1.5 %collective-permute-start.2 = (bf16[80,128]{1,0:T(8,128)(2,1)S(1)}, bf16[80,128]{1,0:T(8,128)(2,1)S(1)}, u32[]{:S(2)}, u32[]{:S(2)}) collective-permute-start(bf16[80,128]{1,0:T(8,128)(2,1)S(1)} %get-tuple-element.53), channel_id=1, source_target_pairs={{0,8},{1,2},{2,1},{3,11},{8,0},{9,10},{10,9},{11,3},{16,24},{17,18... | collective-permute-start | bytes 61448 | tf_op jit(solution)/shard_map/ppermute | solution.py:601
  8.0 2.5 %shard_map.78 = (bf16[5,8,64,128]{3,2,1,0:T(8,128)(2,1)S(1)}, bf16[5,128,256]{2,1,0:T(8,128)(2,1)S(1)}, bf16[3,4,112,128]{3,2,1,0:T(8,128)(2,1)S(1)}, f32[4,2,11...) custom-call(bf16[5,384,128]{2,1,0:T(8,128)(2,1)S(1)} %get-tuple-elem, ...), custom_call_target="tpu_custom_call" | custom-call | flops 2147483648 | bytes 1048576 | tf_op jit(solution)/shard_map/pallas_call | solution.py:532
  10.4 0.0 collective-permute-done.1.refs_13_
  10.4 0.0 collective-permute-done.2.refs_14_
  10.5 2.8 %shard_map.79 = (bf16[2,8,2048]{2,1,0:T(8,128)(2,1)}, bf16[4,16,2048]{2,1,0:T(8,128)(2,1)}, bf16[16,1024]{1,0:T(8,128)(2,1)S(1)}, bf16[16,1024]{1,0:T(8,128)(2,1...) custom-call(bf16[5,8,64,128]{3,2,1,0:T(8,128)(2,1)S(1)} %get-tuple-element.41.refs_0_, ...), custom_call_target="tpu_custom_call" | custom-call | bytes 1048576 | tf_op jit(solution)/shard_map/pallas_call | solution.py:532
  13.3 2.3 %collective-permute-start.3 = (bf16[16,1024]{1,0:T(8,128)(2,1)S(1)}, bf16[16,1024]{1,0:T(8,128)(2,1)S(1)}, u32[]{:S(2)}, u32[]{:S(2)}) collective-permute-start(bf16[16,1024]{1,0:T(8,128)(2,1)S(1)} %get-tuple-element.56), channel_id=1, source_target_pairs={{0,24},{8,16},{16,8},{24,0},{1,25},{9,17},{17,9},{25,1},{2,26},{10... | collective-permute-start | bytes 98312 | tf_op jit(solution)/shard_map/ppermute | solution.py:548
  15.6 0.7 %collective-permute-start.4 = (bf16[16,1024]{1,0:T(8,128)(2,1)S(1)}, bf16[16,1024]{1,0:T(8,128)(2,1)S(1)}, u32[]{:S(2)}, u32[]{:S(2)}) collective-permute-start(bf16[16,1024]{1,0:T(8,128)(2,1)S(1)} %get-tuple-element.57), channel_id=1, source_target_pairs={{0,8},{8,0},{16,24},{24,16},{1,9},{9,1},{17,25},{25,17},{2,10},{10... | collective-permute-start | bytes 98312 | tf_op jit(solution)/shard_map/ppermute | solution.py:548
  16.3 0.5 %collective-permute-start.5 = (bf16[16,1024]{1,0:T(8,128)(2,1)S(1)}, bf16[16,1024]{1,0:T(8,128)(2,1)S(1)}, u32[]{:S(2)}, u32[]{:S(2)}) collective-permute-start(bf16[16,1024]{1,0:T(8,128)(2,1)S(1)} %get-tuple-element.58), channel_id=1, source_target_pairs={{0,16},{8,24},{16,0},{24,8},{1,17},{9,25},{17,1},{25,9},{2,18},{10... | collective-permute-start | bytes 98312 | tf_op jit(solution)/shard_map/ppermute | solution.py:548
  16.8 1.3 %collective-permute-done.3.refs_0_ = bf16[16,1024]{1,0:T(8,128)(2,1)S(1)} collective-permute-done((bf16[16,1024]{1,0:T(8,128)(2,1)S(1)}, bf16[16,1024]{1,0:T(8,128)(2,1)S(1)}, u32[]{:S(2)}, u32[]{:S(2)}) %collective-permute-start.3) | collective-permute-done | bytes 32800 | tf_op jit(solution)/shard_map/ppermute | solution.py:548
  18.2 1.3 %collective-permute-done.4.refs_1_ = bf16[16,1024]{1,0:T(8,128)(2,1)S(1)} collective-permute-done((bf16[16,1024]{1,0:T(8,128)(2,1)S(1)}, bf16[16,1024]{1,0:T(8,128)(2,1)S(1)}, u32[]{:S(2)}, u32[]{:S(2)}) %collective-permute-start.4) | collective-permute-done | bytes 32800 | tf_op jit(solution)/shard_map/ppermute | solution.py:548
  19.5 0.7 %collective-permute-done.5.refs_2_ = bf16[16,1024]{1,0:T(8,128)(2,1)S(1)} collective-permute-done((bf16[16,1024]{1,0:T(8,128)(2,1)S(1)}, bf16[16,1024]{1,0:T(8,128)(2,1)S(1)}, u32[]{:S(2)}, u32[]{:S(2)}) %collective-permute-start.5) | collective-permute-done | bytes 32800 | tf_op jit(solution)/shard_map/ppermute | solution.py:548
  20.2 0.1 collective-permute-start.6
  20.3 1.2 %collective-permute-done.6.refs_1_ = bf16[16,1024]{1,0:T(8,128)(2,1)S(1)} collective-permute-done((bf16[16,1024]{1,0:T(8,128)(2,1)S(1)}, bf16[16,1024]{1,0:T(8,128)(2,1)S(1)}, u32[]{:S(2)}, u32[]{:S(2)}) %collective-permute-start.6) | collective-permute-done | bytes 32800 | tf_op jit(solution)/shard_map/ppermute | solution.py:548
  21.5 1.4 %collective-permute-start.8 = (bf16[16,1024]{1,0:T(8,128)(2,1)S(1)}, bf16[16,1024]{1,0:T(8,128)(2,1)S(1)}, u32[]{:S(2)}, u32[]{:S(2)}) collective-permute-start(bf16[16,1024]{1,0:T(8,128)(2,1)S(1)} %shard_map.81.mine_ref), channel_id=1, source_target_pairs={{0,8},{1,9},{2,10},{3,11},{4,7},{5,6},{6,5},{7,4},{8,0},{9,1},{10,... | collective-permute-start | bytes 98312 | tf_op jit(solution)/shard_map/ppermute | solution.py:561
  22.9 1.9 %collective-permute-start.7 = (bf16[16,1024]{1,0:T(8,128)(2,1)S(1)}, bf16[16,1024]{1,0:T(8,128)(2,1)S(1)}, u32[]{:S(2)}, u32[]{:S(2)}) collective-permute-start(bf16[16,1024]{1,0:T(8,128)(2,1)S(1)} %shard_map.81.mine_ref), channel_id=1, source_target_pairs={{0,1},{1,0},{2,3},{3,2},{4,6},{5,7},{6,4},{7,5},{8,9},{9,8},{10,11... | collective-permute-start | bytes 98312 | tf_op jit(solution)/shard_map/ppermute | solution.py:561
  24.8 0.8 %collective-permute-done.8.second_ref = bf16[16,1024]{1,0:T(8,128)(2,1)S(1)} collective-permute-done((bf16[16,1024]{1,0:T(8,128)(2,1)S(1)}, bf16[16,1024]{1,0:T(8,128)(2,1)S(1)}, u32[]{:S(2)}, u32[]{:S(2)}) %collective-permute-start.8) | collective-permute-done | bytes 32800 | tf_op jit(solution)/shard_map/ppermute | solution.py:561
  25.5 1.3 %collective-permute-done.7.first_ref = bf16[16,1024]{1,0:T(8,128)(2,1)S(1)} collective-permute-done((bf16[16,1024]{1,0:T(8,128)(2,1)S(1)}, bf16[16,1024]{1,0:T(8,128)(2,1)S(1)}, u32[]{:S(2)}, u32[]{:S(2)}) %collective-permute-start.7) | collective-permute-done | bytes 32800 | tf_op jit(solution)/shard_map/ppermute | solution.py:561
  26.9 1.1 %collective-permute-start.9 = (f32[16,1024]{1,0:T(8,128)S(1)}, f32[16,1024]{1,0:T(8,128)S(1)}, u32[]{:S(2)}, u32[]{:S(2)}) collective-permute-start(f32[16,1024]{1,0:T(8,128)S(1)} %shard_map.82.refs_0_), channel_id=1, source_target_pairs={{0,4},{4,0},{1,5},{5,1},{2,6},{6,2},{3,7},{7,3},{8,12},{12,8},{9,1... | collective-permute-start | bytes 196616 | tf_op jit(solution)/shard_map/ppermute | solution.py:548
  28.0 0.9 %collective-permute-done.9.refs_1_ = f32[16,1024]{1,0:T(8,128)S(1)} collective-permute-done((f32[16,1024]{1,0:T(8,128)S(1)}, f32[16,1024]{1,0:T(8,128)S(1)}, u32[]{:S(2)}, u32[]{:S(2)}) %collective-permute-start.9) | collective-permute-done | bytes 65568 | tf_op jit(solution)/shard_map/ppermute | solution.py:548
  28.9 0.8 %shard_map.83 = (f32[27,3,8]{2,1,0:T(4,128)}, f32[27,16,32]{2,1,0:T(8,128)}) custom-call(f32[16,1024]{1,0:T(8,128)S(1)} %shard_map.82.refs_0_, f32[16,1024]{1,0:T(8,128)S(1)} %collective-permute-done.9.refs_1_), custom_call_target="tpu_custom_call" | custom-call | bytes 1048576 | tf_op jit(solution)/shard_map/pallas_call | solution.py:532
  (3 shorter events, 0.0 us)
Async XLA Ops:
  1.8 1.4 %collective-permute-start = (bf16[128,128]{1,0:T(8,128)(2,1)S(1)}, bf16[128,128]{1,0:T(8,128)(2,1)S(1)}, u32[]{:S(2)}, u32[]{:S(2)}) collective-permute-start(bf16[128,128]{1,0:T(8,128)(2,1)S(1)} %get-tuple-element.35), channel_id=1, source_target_pairs={{0,4},{4,0},{8,12},{12,8},{16,20},{20,16},{24,28},{28,24},{1,5},{5... | collective-permute-start | bytes 98312 | tf_op jit(solution)/shard_map/ppermute | solution.py:587
  3.5 6.9 %collective-permute-start.1 = (bf16[80,128]{1,0:T(8,128)(2,1)S(1)}, bf16[80,128]{1,0:T(8,128)(2,1)S(1)}, u32[]{:S(2)}, u32[]{:S(2)}) collective-permute-start(bf16[80,128]{1,0:T(8,128)(2,1)S(1)} %get-tuple-element.52), channel_id=1, source_target_pairs={{0,1},{1,0},{2,3},{3,2},{8,9},{9,8},{10,11},{11,10},{16,17},{17,16... | collective-permute-start | bytes 61448 | tf_op jit(solution)/shard_map/ppermute | solution.py:601
  6.5 4.0 %collective-permute-start.2 = (bf16[80,128]{1,0:T(8,128)(2,1)S(1)}, bf16[80,128]{1,0:T(8,128)(2,1)S(1)}, u32[]{:S(2)}, u32[]{:S(2)}) collective-permute-start(bf16[80,128]{1,0:T(8,128)(2,1)S(1)} %get-tuple-element.53), channel_id=1, source_target_pairs={{0,8},{1,2},{2,1},{3,11},{8,0},{9,10},{10,9},{11,3},{16,24},{17,18... | collective-permute-start | bytes 61448 | tf_op jit(solution)/shard_map/ppermute | solution.py:601
  13.3 4.9 %collective-permute-start.3 = (bf16[16,1024]{1,0:T(8,128)(2,1)S(1)}, bf16[16,1024]{1,0:T(8,128)(2,1)S(1)}, u32[]{:S(2)}, u32[]{:S(2)}) collective-permute-start(bf16[16,1024]{1,0:T(8,128)(2,1)S(1)} %get-tuple-element.56), channel_id=1, source_target_pairs={{0,24},{8,16},{16,8},{24,0},{1,25},{9,17},{17,9},{25,1},{2,26},{10... | collective-permute-start | bytes 98312 | tf_op jit(solution)/shard_map/ppermute | solution.py:548
  15.6 3.9 %collective-permute-start.4 = (bf16[16,1024]{1,0:T(8,128)(2,1)S(1)}, bf16[16,1024]{1,0:T(8,128)(2,1)S(1)}, u32[]{:S(2)}, u32[]{:S(2)}) collective-permute-start(bf16[16,1024]{1,0:T(8,128)(2,1)S(1)} %get-tuple-element.57), channel_id=1, source_target_pairs={{0,8},{8,0},{16,24},{24,16},{1,9},{9,1},{17,25},{25,17},{2,10},{10... | collective-permute-start | bytes 98312 | tf_op jit(solution)/shard_map/ppermute | solution.py:548
  16.3 3.9 %collective-permute-start.5 = (bf16[16,1024]{1,0:T(8,128)(2,1)S(1)}, bf16[16,1024]{1,0:T(8,128)(2,1)S(1)}, u32[]{:S(2)}, u32[]{:S(2)}) collective-permute-start(bf16[16,1024]{1,0:T(8,128)(2,1)S(1)} %get-tuple-element.58), channel_id=1, source_target_pairs={{0,16},{8,24},{16,0},{24,8},{1,17},{9,25},{17,1},{25,9},{2,18},{10... | collective-permute-start | bytes 98312 | tf_op jit(solution)/shard_map/ppermute | solution.py:548
  20.2 1.3 %collective-permute-start.6 = (bf16[16,1024]{1,0:T(8,128)(2,1)S(1)}, bf16[16,1024]{1,0:T(8,128)(2,1)S(1)}, u32[]{:S(2)}, u32[]{:S(2)}) collective-permute-start(bf16[16,1024]{1,0:T(8,128)(2,1)S(1)} %shard_map.80.refs_0_), channel_id=1, source_target_pairs={{0,4},{4,0},{1,5},{5,1},{2,6},{6,2},{3,7},{7,3},{8,12},{12,8},{9,1... | collective-permute-start | bytes 98312 | tf_op jit(solution)/shard_map/ppermute | solution.py:548
  21.5 4.0 %collective-permute-start.8 = (bf16[16,1024]{1,0:T(8,128)(2,1)S(1)}, bf16[16,1024]{1,0:T(8,128)(2,1)S(1)}, u32[]{:S(2)}, u32[]{:S(2)}) collective-permute-start(bf16[16,1024]{1,0:T(8,128)(2,1)S(1)} %shard_map.81.mine_ref), channel_id=1, source_target_pairs={{0,8},{1,9},{2,10},{3,11},{4,7},{5,6},{6,5},{7,4},{8,0},{9,1},{10,... | collective-permute-start | bytes 98312 | tf_op jit(solution)/shard_map/ppermute | solution.py:561
  22.9 4.0 %collective-permute-start.7 = (bf16[16,1024]{1,0:T(8,128)(2,1)S(1)}, bf16[16,1024]{1,0:T(8,128)(2,1)S(1)}, u32[]{:S(2)}, u32[]{:S(2)}) collective-permute-start(bf16[16,1024]{1,0:T(8,128)(2,1)S(1)} %shard_map.81.mine_ref), channel_id=1, source_target_pairs={{0,1},{1,0},{2,3},{3,2},{4,6},{5,7},{6,4},{7,5},{8,9},{9,8},{10,11... | collective-permute-start | bytes 98312 | tf_op jit(solution)/shard_map/ppermute | solution.py:561
  26.9 2.0 %collective-permute-start.9 = (f32[16,1024]{1,0:T(8,128)S(1)}, f32[16,1024]{1,0:T(8,128)S(1)}, u32[]{:S(2)}, u32[]{:S(2)}) collective-permute-start(f32[16,1024]{1,0:T(8,128)S(1)} %shard_map.82.refs_0_), channel_id=1, source_target_pairs={{0,4},{4,0},{1,5},{5,1},{2,6},{6,2},{3,7},{7,3},{8,12},{12,8},{9,1... | collective-permute-start | bytes 196616 | tf_op jit(solution)/shard_map/ppermute | solution.py:548

commit v7 on v5

--- a/solution.py
+++ b/solution.py
@@ -381,17 +381,14 @@
             jnp.concatenate([outer_act[b, p] if p >= 0 else jnp.zeros((64, 128), BF) for b, p in planes], axis=1)
         )
     out = dot(jnp.concatenate(lhs, axis=0), w_two[...])
-    pairs, pairs_next, delta, patches = [], [], [], []
+    pairs, pairs_next, delta, patches, feats = [], [], [], [], []
     for k in range(2):
         own = out[64 * k : 64 * k + 64]
         pre = jnp.concatenate(
             [own[16:48, 0:128], ends_ref[k, 0], own[48:64, 0:128]], axis=0
         ) + jnp.concatenate([own[0:48, 128:256], ends_ref[k, 1]], axis=0)
         feat, value = second_level(pre, jnp.concatenate([cot_ref[k, 0:48, :], cot_y[k]], axis=0))
-        feat_ref[k, :, 0:384] = jnp.concatenate([feat[16 * m : 16 * m + 8] for m in range(3)], axis=1).astype(BF)
-        feat_ref[k, :, 384:2048] = feat_in[k]
-        copies.append(pltpu.make_async_copy(feat_ref.at[k], feat_hbm.at[k], sems.at[k]))
-        copies[-1].start()
+        feats.append(feat)
         value = value.reshape(4, 16, 128)
         outer = value[:, 0:8].reshape(32, 128)
         here = jnp.concatenate([outer[0:24], here_in[k], outer[24:32]], axis=0)
@@ -442,6 +439,11 @@
             )
         level_ref[p] = jnp.concatenate([rows_out[m] for m in range(16)], axis=1).astype(BF)
         copies.append(pltpu.make_async_copy(level_ref.at[p], level_hbm.at[p], sems.at[2 + p]))
+        copies[-1].start()
+    for k, feat in enumerate(feats):
+        feat_ref[k, :, 0:384] = jnp.concatenate([feat[16 * m : 16 * m + 8] for m in range(3)], axis=1).astype(BF)
+        feat_ref[k, :, 384:2048] = feat_in[k]
+        copies.append(pltpu.make_async_copy(feat_ref.at[k], feat_hbm.at[k], sems.at[k]))
         copies[-1].start()
     delta_one = jnp.concatenate(lhs_rows, axis=0).T
     windows = jnp.concatenate(rhs_rows, axis=0)

time: 29.7 us -> 29.7 us (level)
  no operation moved by 1% of the time
where the time goes in v7:
time: 29.7 us; the launch traced here: 29.5 us
  starting transfers between devices  12.9 us (43%)
  Pallas kernels  8.1 us (27%)
  waiting for transfers between devices  7.76 us (26%)
  between operations  0.71 us (2%)
    pallas_call x9, Pallas kernels, call(): pl.pallas_call(kernel, out_shape=outs, in_specs=[pl.BlockSpec(memory_spac...  8.1 us
    ppermute x5, waiting for transfers between devices, exchange(): lax.ppermute(value, axis, [(i, i ^ step) for i in range(lax.axis_size(axi...  5.5 us
    ppermute x5, starting transfers between devices, exchange(): lax.ppermute(value, axis, [(i, i ^ step) for i in range(lax.axis_size(axi...  4.72 us
    ppermute x2, starting transfers between devices, body(): lax.ppermute(edge, ('dp', 'gy'), pairs)  4.47 us
    ppermute x2, starting transfers between devices, trade_shared(): return lax.ppermute(value, ('dp', 'gx', 'gy'), pairs)  3.22 us
    ppermute x2, waiting for transfers between devices, trade_shared(): return lax.ppermute(value, ('dp', 'gx', 'gy'), pairs)  2.1 us
  transfers between devices with their start and end apart: 10, of which 8 were waited for; matrix products, arithmetic and copies ran while one was open for 0% of the time, Pallas kernels for 11%

profile of v7, /device:TPU:0, one launch (start us, length us, event | category | flops | bytes accessed | tf_op | source)
XLA Modules:
  0.0 29.5 jit_solution(17682778876780832489)
XLA Ops:
  0.6 1.1 %shard_map.75 = (bf16[24,32,128]{2,1,0:T(8,128)(2,1)S(1)}, bf16[2,8,2048]{2,1,0:T(8,128)(2,1)S(1)}, bf16[27,3,32]{2,1,0:T(4,128)(2,1)S(1)}, bf16[864,64]{1,0:T(8,128)(2,1)S(1)}, bf16[128,128]{1,0:T(8,128)(2,1)S(1)}) custom-call(bf16[24,32,128]{2,1,0:T(8,128)(2,1)} %bitcast.11, bf16[2,8,2048]{2,1,0:T(8,128)(2,1)} %bitcast.12, bf16[27,3,32]{2,1,0:T(4,128)(2,1)} %bitcast.13, ...), custom_call_target="tpu_custom_call" | custom-call | bytes 1048576 | tf_op jit(solution)/shard_map/pallas_call | solution.py:539
  1.8 0.5 %collective-permute-start = (bf16[128,128]{1,0:T(8,128)(2,1)S(1)}, bf16[128,128]{1,0:T(8,128)(2,1)S(1)}, u32[]{:S(2)}, u32[]{:S(2)}) collective-permute-start(bf16[128,128]{1,0:T(8,128)(2,1)S(1)} %get-tuple-element.35), channel_id=1, source_target_pairs={{0,4},{4,0},{8,12},{12,8},{16,20},{20,16},{24,28},{28,24},{1,5},{5... | collective-permute-start | bytes 98312 | tf_op jit(solution)/shard_map/ppermute | solution.py:594
  2.3 0.7 %shard_map.77 = (bf16[1152,256]{1,0:T(8,128)(2,1)S(1)}, bf16[1152,256]{1,0:T(8,128)(2,1)S(1)}, bf16[256,2048]{1,0:T(8,128)(2,1)S(1)}) custom-call(bf16[27,3,32]{2,1,0:T(4,128)(2,1)S(1)} %get-tuple-element.37.one_ref, bf16[864,64]{1,0:T(8,128)(2,1)S(1)} %get-tuple-element.38.two_ref), custom_call_target="tpu_custom_call" | custom-call | flops 1073741824 | bytes 1048576 | tf_op jit(solution)/shard_map/pallas_call | solution.py:539
  3.0 0.2 collective-permute-done.refs_2_.refs_4_
  3.1 0.4 %shard_map.76 = (bf16[5,384,128]{2,1,0:T(8,128)(2,1)S(1)}, bf16[80,128]{1,0:T(8,128)(2,1)S(1)}, bf16[80,128]{1,0:T(8,128)(2,1)S(1)}) custom-call(bf16[24,32,128]{2,1,0:T(8,128)(2,1)S(1)} %get-tuple-element.33.refs_0_, bf16[2,8,2048]{2,1,0:T(8,128)(2,1)S(1)} %get-tuple-element.34.refs_1_.refs_3_, bf16[128,128]{1,0:T(8,128)(2,1)S(1)} %collective-permute-done.refs_2_.refs_4_), custom_call_target="tpu_custom_call" | custom-call | bytes 1048576 | tf_op jit(solution)/shard_map/pallas_call | solution.py:539
  3.5 3.0 %collective-permute-start.1 = (bf16[80,128]{1,0:T(8,128)(2,1)S(1)}, bf16[80,128]{1,0:T(8,128)(2,1)S(1)}, u32[]{:S(2)}, u32[]{:S(2)}) collective-permute-start(bf16[80,128]{1,0:T(8,128)(2,1)S(1)} %get-tuple-element.52), channel_id=1, source_target_pairs={{0,1},{1,0},{2,3},{3,2},{8,9},{9,8},{10,11},{11,10},{16,17},{17,16... | collective-permute-start | bytes 61448 | tf_op jit(solution)/shard_map/ppermute | solution.py:608
  6.5 1.5 %collective-permute-start.2 = (bf16[80,128]{1,0:T(8,128)(2,1)S(1)}, bf16[80,128]{1,0:T(8,128)(2,1)S(1)}, u32[]{:S(2)}, u32[]{:S(2)}) collective-permute-start(bf16[80,128]{1,0:T(8,128)(2,1)S(1)} %get-tuple-element.53), channel_id=1, source_target_pairs={{0,8},{1,2},{2,1},{3,11},{8,0},{9,10},{10,9},{11,3},{16,24},{17,18... | collective-permute-start | bytes 61448 | tf_op jit(solution)/shard_map/ppermute | solution.py:608
  8.0 2.5 %shard_map.78 = (bf16[5,8,64,128]{3,2,1,0:T(8,128)(2,1)S(1)}, bf16[5,128,256]{2,1,0:T(8,128)(2,1)S(1)}, bf16[3,4,112,128]{3,2,1,0:T(8,128)(2,1)S(1)}, f32[4,2,11...) custom-call(bf16[5,384,128]{2,1,0:T(8,128)(2,1)S(1)} %get-tuple-elem, ...), custom_call_target="tpu_custom_call" | custom-call | flops 2147483648 | bytes 1048576 | tf_op jit(solution)/shard_map/pallas_call | solution.py:539
  10.4 0.0 collective-permute-done.1.refs_13_
  10.4 0.0 collective-permute-done.2.refs_14_
  10.5 2.6 %shard_map.79 = (bf16[2,8,2048]{2,1,0:T(8,128)(2,1)}, bf16[4,16,2048]{2,1,0:T(8,128)(2,1)}, bf16[16,1024]{1,0:T(8,128)(2,1)S(1)}, bf16[16,1024]{1,0:T(8,128)(2,1...) custom-call(bf16[5,8,64,128]{3,2,1,0:T(8,128)(2,1)S(1)} %get-tuple-element.41.refs_0_, ...), custom_call_target="tpu_custom_call" | custom-call | bytes 1048576 | tf_op jit(solution)/shard_map/pallas_call | solution.py:539
  13.1 2.3 %collective-permute-start.3 = (bf16[16,1024]{1,0:T(8,128)(2,1)S(1)}, bf16[16,1024]{1,0:T(8,128)(2,1)S(1)}, u32[]{:S(2)}, u32[]{:S(2)}) collective-permute-start(bf16[16,1024]{1,0:T(8,128)(2,1)S(1)} %get-tuple-element.56), channel_id=1, source_target_pairs={{0,24},{8,16},{16,8},{24,0},{1,25},{9,17},{17,9},{25,1},{2,26},{10... | collective-permute-start | bytes 98312 | tf_op jit(solution)/shard_map/ppermute | solution.py:555
  15.4 0.7 %collective-permute-start.4 = (bf16[16,1024]{1,0:T(8,128)(2,1)S(1)}, bf16[16,1024]{1,0:T(8,128)(2,1)S(1)}, u32[]{:S(2)}, u32[]{:S(2)}) collective-permute-start(bf16[16,1024]{1,0:T(8,128)(2,1)S(1)} %get-tuple-element.57), channel_id=1, source_target_pairs={{0,8},{8,0},{16,24},{24,16},{1,9},{9,1},{17,25},{25,17},{2,10},{10... | collective-permute-start | bytes 98312 | tf_op jit(solution)/shard_map/ppermute | solution.py:555
  16.1 0.5 %collective-permute-start.5 = (bf16[16,1024]{1,0:T(8,128)(2,1)S(1)}, bf16[16,1024]{1,0:T(8,128)(2,1)S(1)}, u32[]{:S(2)}, u32[]{:S(2)}) collective-permute-start(bf16[16,1024]{1,0:T(8,128)(2,1)S(1)} %get-tuple-element.58), channel_id=1, source_target_pairs={{0,16},{8,24},{16,0},{24,8},{1,17},{9,25},{17,1},{25,9},{2,18},{10... | collective-permute-start | bytes 98312 | tf_op jit(solution)/shard_map/ppermute | solution.py:555
  16.6 1.3 %collective-permute-done.3.refs_0_ = bf16[16,1024]{1,0:T(8,128)(2,1)S(1)} collective-permute-done((bf16[16,1024]{1,0:T(8,128)(2,1)S(1)}, bf16[16,1024]{1,0:T(8,128)(2,1)S(1)}, u32[]{:S(2)}, u32[]{:S(2)}) %collective-permute-start.3) | collective-permute-done | bytes 32800 | tf_op jit(solution)/shard_map/ppermute | solution.py:555
  18.0 1.3 %collective-permute-done.4.refs_1_ = bf16[16,1024]{1,0:T(8,128)(2,1)S(1)} collective-permute-done((bf16[16,1024]{1,0:T(8,128)(2,1)S(1)}, bf16[16,1024]{1,0:T(8,128)(2,1)S(1)}, u32[]{:S(2)}, u32[]{:S(2)}) %collective-permute-start.4) | collective-permute-done | bytes 32800 | tf_op jit(solution)/shard_map/ppermute | solution.py:555
  19.3 0.7 %collective-permute-done.5.refs_2_ = bf16[16,1024]{1,0:T(8,128)(2,1)S(1)} collective-permute-done((bf16[16,1024]{1,0:T(8,128)(2,1)S(1)}, bf16[16,1024]{1,0:T(8,128)(2,1)S(1)}, u32[]{:S(2)}, u32[]{:S(2)}) %collective-permute-start.5) | collective-permute-done | bytes 32800 | tf_op jit(solution)/shard_map/ppermute | solution.py:555
  20.1 0.1 collective-permute-start.6
  20.2 1.2 %collective-permute-done.6.refs_1_ = bf16[16,1024]{1,0:T(8,128)(2,1)S(1)} collective-permute-done((bf16[16,1024]{1,0:T(8,128)(2,1)S(1)}, bf16[16,1024]{1,0:T(8,128)(2,1)S(1)}, u32[]{:S(2)}, u32[]{:S(2)}) %collective-permute-start.6) | collective-permute-done | bytes 32800 | tf_op jit(solution)/shard_map/ppermute | solution.py:555
  21.4 1.4 %collective-permute-start.8 = (bf16[16,1024]{1,0:T(8,128)(2,1)S(1)}, bf16[16,1024]{1,0:T(8,128)(2,1)S(1)}, u32[]{:S(2)}, u32[]{:S(2)}) collective-permute-start(bf16[16,1024]{1,0:T(8,128)(2,1)S(1)} %shard_map.81.mine_ref), channel_id=1, source_target_pairs={{0,8},{1,9},{2,10},{3,11},{4,7},{5,6},{6,5},{7,4},{8,0},{9,1},{10,... | collective-permute-start | bytes 98312 | tf_op jit(solution)/shard_map/ppermute | solution.py:568
  22.7 1.9 %collective-permute-start.7 = (bf16[16,1024]{1,0:T(8,128)(2,1)S(1)}, bf16[16,1024]{1,0:T(8,128)(2,1)S(1)}, u32[]{:S(2)}, u32[]{:S(2)}) collective-permute-start(bf16[16,1024]{1,0:T(8,128)(2,1)S(1)} %shard_map.81.mine_ref), channel_id=1, source_target_pairs={{0,1},{1,0},{2,3},{3,2},{4,6},{5,7},{6,4},{7,5},{8,9},{9,8},{10,11... | collective-permute-start | bytes 98312 | tf_op jit(solution)/shard_map/ppermute | solution.py:568
  24.6 0.8 %collective-permute-done.8.second_ref = bf16[16,1024]{1,0:T(8,128)(2,1)S(1)} collective-permute-done((bf16[16,1024]{1,0:T(8,128)(2,1)S(1)}, bf16[16,1024]{1,0:T(8,128)(2,1)S(1)}, u32[]{:S(2)}, u32[]{:S(2)}) %collective-permute-start.8) | collective-permute-done | bytes 32800 | tf_op jit(solution)/shard_map/ppermute | solution.py:568
  25.3 1.3 %collective-permute-done.7.first_ref = bf16[16,1024]{1,0:T(8,128)(2,1)S(1)} collective-permute-done((bf16[16,1024]{1,0:T(8,128)(2,1)S(1)}, bf16[16,1024]{1,0:T(8,128)(2,1)S(1)}, u32[]{:S(2)}, u32[]{:S(2)}) %collective-permute-start.7) | collective-permute-done | bytes 32800 | tf_op jit(solution)/shard_map/ppermute | solution.py:568
  26.7 1.1 %collective-permute-start.9 = (f32[16,1024]{1,0:T(8,128)S(1)}, f32[16,1024]{1,0:T(8,128)S(1)}, u32[]{:S(2)}, u32[]{:S(2)}) collective-permute-start(f32[16,1024]{1,0:T(8,128)S(1)} %shard_map.82.refs_0_), channel_id=1, source_target_pairs={{0,4},{4,0},{1,5},{5,1},{2,6},{6,2},{3,7},{7,3},{8,12},{12,8},{9,1... | collective-permute-start | bytes 196616 | tf_op jit(solution)/shard_map/ppermute | solution.py:555
  27.8 0.9 %collective-permute-done.9.refs_1_ = f32[16,1024]{1,0:T(8,128)S(1)} collective-permute-done((f32[16,1024]{1,0:T(8,128)S(1)}, f32[16,1024]{1,0:T(8,128)S(1)}, u32[]{:S(2)}, u32[]{:S(2)}) %collective-permute-start.9) | collective-permute-done | bytes 65568 | tf_op jit(solution)/shard_map/ppermute | solution.py:555
  28.7 0.8 %shard_map.83 = (f32[27,3,8]{2,1,0:T(4,128)}, f32[27,16,32]{2,1,0:T(8,128)}) custom-call(f32[16,1024]{1,0:T(8,128)S(1)} %shard_map.82.refs_0_, f32[16,1024]{1,0:T(8,128)S(1)} %collective-permute-done.9.refs_1_), custom_call_target="tpu_custom_call" | custom-call | bytes 1048576 | tf_op jit(solution)/shard_map/pallas_call | solution.py:539
  (3 shorter events, 0.0 us)
Async XLA Ops:
  1.8 1.4 %collective-permute-start = (bf16[128,128]{1,0:T(8,128)(2,1)S(1)}, bf16[128,128]{1,0:T(8,128)(2,1)S(1)}, u32[]{:S(2)}, u32[]{:S(2)}) collective-permute-start(bf16[128,128]{1,0:T(8,128)(2,1)S(1)} %get-tuple-element.35), channel_id=1, source_target_pairs={{0,4},{4,0},{8,12},{12,8},{16,20},{20,16},{24,28},{28,24},{1,5},{5... | collective-permute-start | bytes 98312 | tf_op jit(solution)/shard_map/ppermute | solution.py:594
  3.5 6.9 %collective-permute-start.1 = (bf16[80,128]{1,0:T(8,128)(2,1)S(1)}, bf16[80,128]{1,0:T(8,128)(2,1)S(1)}, u32[]{:S(2)}, u32[]{:S(2)}) collective-permute-start(bf16[80,128]{1,0:T(8,128)(2,1)S(1)} %get-tuple-element.52), channel_id=1, source_target_pairs={{0,1},{1,0},{2,3},{3,2},{8,9},{9,8},{10,11},{11,10},{16,17},{17,16... | collective-permute-start | bytes 61448 | tf_op jit(solution)/shard_map/ppermute | solution.py:608
  6.5 4.0 %collective-permute-start.2 = (bf16[80,128]{1,0:T(8,128)(2,1)S(1)}, bf16[80,128]{1,0:T(8,128)(2,1)S(1)}, u32[]{:S(2)}, u32[]{:S(2)}) collective-permute-start(bf16[80,128]{1,0:T(8,128)(2,1)S(1)} %get-tuple-element.53), channel_id=1, source_target_pairs={{0,8},{1,2},{2,1},{3,11},{8,0},{9,10},{10,9},{11,3},{16,24},{17,18... | collective-permute-start | bytes 61448 | tf_op jit(solution)/shard_map/ppermute | solution.py:608
  13.1 4.9 %collective-permute-start.3 = (bf16[16,1024]{1,0:T(8,128)(2,1)S(1)}, bf16[16,1024]{1,0:T(8,128)(2,1)S(1)}, u32[]{:S(2)}, u32[]{:S(2)}) collective-permute-start(bf16[16,1024]{1,0:T(8,128)(2,1)S(1)} %get-tuple-element.56), channel_id=1, source_target_pairs={{0,24},{8,16},{16,8},{24,0},{1,25},{9,17},{17,9},{25,1},{2,26},{10... | collective-permute-start | bytes 98312 | tf_op jit(solution)/shard_map/ppermute | solution.py:555
  15.4 3.9 %collective-permute-start.4 = (bf16[16,1024]{1,0:T(8,128)(2,1)S(1)}, bf16[16,1024]{1,0:T(8,128)(2,1)S(1)}, u32[]{:S(2)}, u32[]{:S(2)}) collective-permute-start(bf16[16,1024]{1,0:T(8,128)(2,1)S(1)} %get-tuple-element.57), channel_id=1, source_target_pairs={{0,8},{8,0},{16,24},{24,16},{1,9},{9,1},{17,25},{25,17},{2,10},{10... | collective-permute-start | bytes 98312 | tf_op jit(solution)/shard_map/ppermute | solution.py:555
  16.1 3.9 %collective-permute-start.5 = (bf16[16,1024]{1,0:T(8,128)(2,1)S(1)}, bf16[16,1024]{1,0:T(8,128)(2,1)S(1)}, u32[]{:S(2)}, u32[]{:S(2)}) collective-permute-start(bf16[16,1024]{1,0:T(8,128)(2,1)S(1)} %get-tuple-element.58), channel_id=1, source_target_pairs={{0,16},{8,24},{16,0},{24,8},{1,17},{9,25},{17,1},{25,9},{2,18},{10... | collective-permute-start | bytes 98312 | tf_op jit(solution)/shard_map/ppermute | solution.py:555
  20.1 1.3 %collective-permute-start.6 = (bf16[16,1024]{1,0:T(8,128)(2,1)S(1)}, bf16[16,1024]{1,0:T(8,128)(2,1)S(1)}, u32[]{:S(2)}, u32[]{:S(2)}) collective-permute-start(bf16[16,1024]{1,0:T(8,128)(2,1)S(1)} %shard_map.80.refs_0_), channel_id=1, source_target_pairs={{0,4},{4,0},{1,5},{5,1},{2,6},{6,2},{3,7},{7,3},{8,12},{12,8},{9,1... | collective-permute-start | bytes 98312 | tf_op jit(solution)/shard_map/ppermute | solution.py:555
  21.4 4.0 %collective-permute-start.8 = (bf16[16,1024]{1,0:T(8,128)(2,1)S(1)}, bf16[16,1024]{1,0:T(8,128)(2,1)S(1)}, u32[]{:S(2)}, u32[]{:S(2)}) collective-permute-start(bf16[16,1024]{1,0:T(8,128)(2,1)S(1)} %shard_map.81.mine_ref), channel_id=1, source_target_pairs={{0,8},{1,9},{2,10},{3,11},{4,7},{5,6},{6,5},{7,4},{8,0},{9,1},{10,... | collective-permute-start | bytes 98312 | tf_op jit(solution)/shard_map/ppermute | solution.py:568
  22.7 4.0 %collective-permute-start.7 = (bf16[16,1024]{1,0:T(8,128)(2,1)S(1)}, bf16[16,1024]{1,0:T(8,128)(2,1)S(1)}, u32[]{:S(2)}, u32[]{:S(2)}) collective-permute-start(bf16[16,1024]{1,0:T(8,128)(2,1)S(1)} %shard_map.81.mine_ref), channel_id=1, source_target_pairs={{0,1},{1,0},{2,3},{3,2},{4,6},{5,7},{6,4},{7,5},{8,9},{9,8},{10,11... | collective-permute-start | bytes 98312 | tf_op jit(solution)/shard_map/ppermute | solution.py:568
  26.7 2.0 %collective-permute-start.9 = (f32[16,1024]{1,0:T(8,128)S(1)}, f32[16,1024]{1,0:T(8,128)S(1)}, u32[]{:S(2)}, u32[]{:S(2)}) collective-permute-start(f32[16,1024]{1,0:T(8,128)S(1)} %shard_map.82.refs_0_), channel_id=1, source_target_pairs={{0,4},{4,0},{1,5},{5,1},{2,6},{6,2},{3,7},{7,3},{8,12},{12,8},{9,1... | collective-permute-start | bytes 196616 | tf_op jit(solution)/shard_map/ppermute | solution.py:555
